TPU v7x, 32 devices: a whole 2x2x4 slice. The times are simulated.
32 devices in a mesh: seq: 8 (over z, x), layer: 4 (over y, core).
Axes of the slice: x: 2, y: 2, z: 4, core: 2. Of those that a mesh axis runs over, the one named last changes fastest.
Arguments:
- train_inputs: bfloat16 [4, 1024, 4096], P('layer', 'seq'), may hold values from -6 to 6
- out_grads: bfloat16 [4, 1024, 14336], P('layer', 'seq'), may hold values from -6 to 6
- query_blocks: bfloat16 [4, 14336, 4096], P('layer', 'seq'), may hold values from -0.00036621094 to 0.00036621094
- basis_in: bfloat16 [4, 32, 128, 128], P('layer'), may hold values from -0.5 to 0.5
- basis_out: bfloat16 [4, 112, 128, 128], P('layer', 'seq'), may hold values from -0.5 to 0.5
- block_of: int32 [4, 8], P('layer'), may hold values from 0 to 7, each once within a row
Outputs:
- scores: float32 [1024], P('seq')
Inputs may be any that keep to these rules, and one draw needn't show every extreme that they name: Each row of block_of names every eigenbasis block of its layer once.
All inputs are finite; a program needn't handle non-finite values.
Results may differ from a plain program's by a relative error of at most 0.0055.
Values may be sent and summed in bfloat16 or wider, within the bound.
No kernel may reach another device: no remote copies, remote signals or barrier semaphores. Data moves between devices by JAX's collectives and lax.ppermute only.
A program may use at most 128 MiB of HBM per device.

v0:
```python
import jax
import jax.numpy as jnp
from jax import lax
from jax.sharding import PartitionSpec as P


def turn_rows(rows, basis):
    count = rows.shape[0]
    groups = rows.reshape(count, basis.shape[0], basis.shape[1])
    turned = jnp.einsum("tnr,nrs->tns", groups, basis, preferred_element_type=jnp.float32)
    return turned.reshape(count, -1).astype(jnp.bfloat16)


def body(train_inputs, out_grads, query_blocks, basis_in, basis_out, block_of):
    acts = train_inputs[0]
    grads = out_grads[0]
    query = query_blocks[0]
    owners = block_of[0]
    count = acts.shape[0]
    rotated = turn_rows(acts, basis_in[0])
    outgoing = jnp.take(grads.reshape(count, owners.shape[0], -1), owners, axis=1)
    arrived = lax.all_to_all(outgoing, "seq", split_axis=1, concat_axis=0, tiled=True)
    turned = turn_rows(arrived.reshape(arrived.shape[0], -1), basis_out[0])
    partial_scores = jnp.sum(
        lax.dot_general(
            lax.all_gather(rotated, "seq", axis=0, tiled=True),
            query,
            (((1,), (1,)), ((), ())),
            preferred_element_type=jnp.float32,
        )
        * turned.astype(jnp.float32),
        axis=1,
    )
    share = lax.psum_scatter(partial_scores, "seq", scatter_dimension=0, tiled=True)
    return lax.psum(share, "layer")


def solution(mesh):
    placed = (
        P("layer", "seq", None),
        P("layer", "seq", None),
        P("layer", "seq", None),
        P("layer", None, None, None),
        P("layer", "seq", None, None),
        P("layer", None),
    )
    return jax.shard_map(body, mesh=mesh, in_specs=placed, out_specs=P("seq"), check_vma=False)
```

profile of v0, /device:TPU:0, one launch (start us, length us, event | category | flops | bytes accessed | tf_op | source)
XLA Modules:
  0.0 271.7 jit_solution(14903285362589704911)
XLA Ops:
  6.5 0.0 copy-start
  6.5 0.0 all-gather.2.cloned.1.call-start
  6.5 1.5 copy.39
  8.1 0.0 copy-done
  8.1 1.9 convolution_convert_fusion
  10.0 0.0 all-gather.2.cloned.1.call-update
  10.0 6.1 %copy.27 = bf16[1,128,14336]{1,2,0:T(8,128)(2,1)} copy(bf16[1,128,14336]{2,1,0:T(8,128)(2,1)} %param.7) | data formatting | bytes 7340032 | tf_op args[1]
  16.1 0.0 copy-start.3
  16.1 6.1 %copy.28 = bf16[128,8,1792]{2,0,1:T(8,128)(2,1)} copy(bf16[128,8,1792]{0,2,1:T(8,128)(2,1)} %bitcast.39) | data formatting | bytes 7340032 | tf_op jit(solution)/shard_map/reshape;squeeze | solution.py:21
  22.1 0.0 copy-done.3
  22.1 4.8 %gather_fusion = bf16[8,128,1792]{2,1,0:T(8,128)(2,1)} fusion(bf16[128,8,1792]{2,0,1:T(8,128)(2,1)} %copy.28, s32[1024]{0:T(1024)S(1)} %pad_clamp_fusion), kind=kCustom, calls=%fused_computation | custom fusion | bytes 7340064 | tf_op jit(solution)/shard_map/jit(_take)/gather | solution.py:21
  26.9 4.3 %select_bitcast_fusion = bf16[128,8,1792]{2,0,1:T(8,128)(2,1)} fusion(bf16[8,128,1792]{2,1,0:T(8,128)(2,1)} %gather_fusion, pred[8]{0:T(512)(128)(4,1)S(1)} %compare_and_fusion), kind=kLoop, calls=%fused_computation.6 | loop fusion | flops 1835008 | bytes 7340040 | tf_op jit(solution)/shard_map/jit(_take)/select_n | solution.py:21
  31.2 0.0 copy-start.4
  31.2 7.2 %all-to-all-start = ((bf16[128,8,1792]{2,0,1:T(8,128)(2,1)}), bf16[128,8,1792]{2,0,1:T(8,128)(2,1)}, u32[]{:S(2)}, u32[]{:S(2)}) async-start(bf16[128,8,1792]{2,0,1:T(8,128)(2,1)} %select_bitcast_fusion), calls=%async_computation | async-start | bytes 7340032 | tf_op jit(solution)/shard_map/all_to_all | solution.py:22
  38.4 0.0 copy-start.2
  38.4 0.0 copy-done.4
  38.5 0.6 dynamic-slice
  39.7 153.7 %all-to-all-done = bf16[128,8,1792]{2,0,1:T(8,128)(2,1)} async-done(((bf16[128,8,1792]{2,0,1:T(8,128)(2,1)}), bf16[128,8,1792]{2,0,1:T(8,128)(2,1)}, u32[]{:S(2)}, u32[]{:S(2)}) %all-to-all-start) | async-done | bytes 3670048 | tf_op jit(solution)/shard_map/all_to_all | solution.py:22
  193.4 7.4 %reshape.50 = bf16[1024,14,128]{2,1,0:T(8,128)(2,1)} reshape(bf16[8,128,1,1792]{3,1,0,2:T(8,128)(2,1)} %bitcast.10) | data formatting | bytes 7340032 | tf_op jit(solution)/shard_map/reshape;reshape | solution.py:9
  200.8 0.0 copy-done.2
  200.8 7.6 %convert_convert_fusion = f32[14,1024,128]{1,2,0:T(8,128)} fusion(bf16[1024,14,128]{2,1,0:T(8,128)(2,1)} %reshape.50, bf16[1,14,128,128]{3,2,1,0:T(8,128)(2,1)S(1)} %copy-done.2), kind=kOutput, calls=%fused_computation.7 | convolution fusion | flops 473432064 | bytes 11468800 | tf_op jit(solution)/shard_map/tnr,nrs->tns/dot_general | solution.py:10
  208.4 8.4 %copy.32 = f32[1024,1792]{1,0:T(8,128)} copy(f32[1024,1792]{0,1:T(8,128)} %bitcast.38) | data formatting | bytes 14680064 | tf_op jit(solution)/shard_map/convert_element_type | solution.py:31
  216.8 0.0 all-gather.2.cloned.1.call-done
  216.8 0.0 copy-start.1
  216.8 22.9 %multiply_reduce_fusion = f32[1024]{0:T(1024)S(1)} fusion(f32[1024,1792]{1,0:T(8,128)} %copy.32, bf16[1024,4096]{0,1:T(8,128)(2,1)} %all-gather.2.cloned.1.call-done, bf16[1,1792,4096]{2,1,0:T(8,128)(2,1)} %param.8), kind=kOutput, calls=%fused_computation.3 | convolution fusion | flops 15036054528 | bytes 30412800 | tf_op jit(solution)/shard_map/dot_general | solution.py:25
  239.7 19.0 %all-reduce = f32[1024]{0:T(1024)S(1)} all-reduce(f32[1024]{0:T(1024)S(1)} %multiply_reduce_fusion), channel_id=2, replica_groups=mesh['seq'=8,'layer'=4] {'seq'}, use_global_device_ids=true, to_apply=%region_1.2.clone | all-reduce | flops 1024 | bytes 8192
  258.7 0.1 dynamic-slice.1
  258.7 6.1 %psum.7 = f32[128]{0:T(128)} all-reduce(f32[128]{0:T(128)S(1)} %dynamic-slice.1), channel_id=1, replica_groups=mesh['seq'=8,'layer'=4] {'layer'}, use_global_device_ids=true, to_apply=%region_2.3 | all-reduce | flops 128 | bytes 1024 | tf_op jit(solution)/shard_map/psum | solution.py:35
  264.9 0.0 copy-done.1
  (3 shorter events, 0.0 us)
Async XLA Ops:
  6.5 1.6 copy-start
  6.5 210.3 %all-gather.2.cloned.1.call-start = ((), (), s32[]{:S(2)}) async-start(), calls=%async_computation.1 | async-start | bytes 9437184 | tf_op jit(solution)/shard_map/all_gather | solution.py:26
  16.1 6.1 %copy-start.3 = (s32[1,8]{1,0:T(1,128)S(1)}, s32[1,8]{1,0:T(1,128)}, u32[]{:S(2)}) copy-start(s32[1,8]{1,0:T(1,128)} %param.11) | copy-start | bytes 100
  31.2 7.3 %copy-start.4 = (u32[32]{0:T(128)S(1)}, u32[32]{0:T(128)}, u32[]{:S(2)}) copy-start(u32[32]{0:T(128)} %constant.26) | copy-start | bytes 388
  31.2 162.2 %all-to-all-start = ((bf16[128,8,1792]{2,0,1:T(8,128)(2,1)}), bf16[128,8,1792]{2,0,1:T(8,128)(2,1)}, u32[]{:S(2)}, u32[]{:S(2)}) async-start(bf16[128,8,1792]{2,0,1:T(8,128)(2,1)} %select_bitcast_fusion), calls=%async_computation | async-start | bytes 7340032 | tf_op jit(solution)/shard_map/all_to_all | solution.py:22
  38.4 162.4 %copy-start.2 = (bf16[1,14,128,128]{3,2,1,0:T(8,128)(2,1)S(1)}, bf16[1,14,128,128]{3,2,1,0:T(8,128)(2,1)}, u32[]{:S(2)}) copy-start(bf16[1,14,128,128]{3,2,1,0:T(8,128)(2,1)} %param.10) | copy-start | bytes 1376260
  216.8 48.1 %copy-start.1 = (bf16[1,32,128,128]{3,2,1,0:T(8,128)(2,1)S(1)}, bf16[1,32,128,128]{3,2,1,0:T(8,128)(2,1)}, u32[]{:S(2)}) copy-start(bf16[1,32,128,128]{3,2,1,0:T(8,128)(2,1)} %param.9) | copy-start | bytes 3145732
Sparse Core Ops, SparseCore 0:
  10.1 198.6 all-gather.1
where the time goes:
time: 273 us; the launch traced here: 272 us
  waiting for transfers between devices  154 us (56%)
  local copies, waits for them, and re-layouts  34.9 us (13%)
  matrix products  32.3 us (12%)
  blocking collectives  25.1 us (9%)
  between operations  14.1 us (5%)
  starting transfers between devices  7.24 us (3%)
  other arithmetic  4.28 us (2%)
    all_to_all x1, waiting for transfers between devices, body(): lax.all_to_all(outgoing, 'seq', split_axis=1, concat_axis=0, tiled=True)  154 us
    dot_general x1, matrix products, body(): lax.dot_general(lax.all_gather(rotated, 'seq', axis=0, tiled=True), query...  22.9 us
    unnamed x1, blocking collectives  19 us
    dot_general x2, matrix products, turn_rows(): jnp.einsum('tnr,nrs->tns', groups, basis, preferred_element_type=jnp.floa...  9.44 us
    convert_element_type x1, local copies, waits for them, and re-layouts, body(): turned.astype(jnp.float32)  8.43 us
    unnamed x14, local copies, waits for them, and re-layouts  8.28 us
    another operation x1, local copies, waits for them, and re-layouts, turn_rows(): groups = rows.reshape(count, basis.shape[0], basis.shape[1])  7.38 us
    all_to_all x1, starting transfers between devices, body(): lax.all_to_all(outgoing, 'seq', split_axis=1, concat_axis=0, tiled=True)  7.24 us
  transfers between devices with their start and end apart: 2, of which 1 were waited for; matrix products, arithmetic and copies ran while one was open for 17% of the time, Pallas kernels for 0%

commit v1 on v0

v1 whole, which is shorter than its diff:
```python
import functools

import jax
import jax.numpy as jnp
from jax import lax
from jax.experimental import pallas as pl
from jax.experimental.pallas import tpu as pltpu
from jax.sharding import PartitionSpec as P

LINE = 4
TILE = 128
NT = (((1,), (1,)), ((), ()))
hold = lax.optimization_barrier


def project_kernel(count, *refs):
    chunks, (basis, query, out, turned) = refs[:count], refs[count:]
    rows, order = chunks[0].shape[0], basis.shape[1]

    @pl.when(pl.program_id(0) == 0)
    def _():
        for c, chunk in enumerate(chunks):
            for n in range(basis.shape[0]):
                part = pl.ds(n * order, order)
                turned[pl.ds(c * rows, rows), part] = jnp.dot(
                    chunk[:, part], basis[n], preferred_element_type=jnp.float32
                ).astype(jnp.bfloat16)

    found = lax.dot_general(turned[...], query[...], NT, preferred_element_type=jnp.float32)
    out[...] = found.reshape(out.shape)


def project(chunks, basis, query):
    count, (rows, wide) = len(chunks), chunks[0].shape
    units = query.shape[0]
    step = 2 * TILE if units % (2 * TILE) == 0 else TILE
    whole = lambda *shape: pl.BlockSpec(shape, lambda i: (0,) * len(shape))
    return pl.pallas_call(
        functools.partial(project_kernel, count),
        grid=(units // step,),
        in_specs=[whole(rows, wide)] * count + [whole(*basis.shape), pl.BlockSpec((step, wide), lambda i: (i, 0))],
        out_specs=pl.BlockSpec((count, rows, step), lambda i: (0, 0, i)),
        out_shape=jax.ShapeDtypeStruct((count, rows, units), jnp.float32),
        scratch_shapes=[pltpu.VMEM((count * rows, wide), jnp.bfloat16)],
        compiler_params=pltpu.CompilerParams(vmem_limit_bytes=24 * 2**20),
        cost_estimate=pl.CostEstimate(
            flops=2 * count * rows * wide * (units + TILE), bytes_accessed=2 * wide * units, transcendentals=0
        ),
    )(*chunks, basis, query)


def score_kernel(pick, first, second, piece, basis, out):
    order = basis.shape[1]
    total = jnp.zeros((piece.shape[0], order), jnp.float32)
    for n in range(basis.shape[0]):
        part = pl.ds(n * order, order)
        turned = jnp.dot(piece[:, part], basis[n], preferred_element_type=jnp.float32).astype(jnp.bfloat16)
        held = jnp.where(pick[0] == 1, first[:, part], second[:, part])
        total += turned.astype(jnp.float32) * held
    out[...] = jnp.sum(total.T, axis=0, keepdims=True)


def score(pick, first, second, piece, basis):
    vmem = pl.BlockSpec(memory_space=pltpu.VMEM)
    return pl.pallas_call(
        score_kernel,
        in_specs=[pl.BlockSpec(memory_space=pltpu.SMEM)] + [vmem] * 4,
        out_specs=vmem,
        out_shape=jax.ShapeDtypeStruct((1, piece.shape[0]), jnp.float32),
        compiler_params=pltpu.CompilerParams(vmem_limit_bytes=16 * 2**20),
    )(pick, first, second, piece, basis)


def body(across, train_inputs, out_grads, query_blocks, basis_in, basis_out, block_of):
    own, grads, query = train_inputs[0], out_grads[0], query_blocks[0]
    turn_in, turn_out, owners = basis_in[0], basis_out[0], block_of[0]
    size, units = LINE * across, query.shape[0]
    me = lax.axis_index("seq")
    inner = (me // across == 1) | (me // across == 2)
    pick = inner.astype(jnp.int32).reshape(1)

    def move(value, place):
        pairs = []
        for s in range(size):
            to = place(s // across, s % across)
            if to is not None:
                pairs.append((s, to[0] * across + to[1]))
        return lax.ppermute(value, "seq", pairs)

    def swap(value, j):
        return lax.ppermute(value, "seq", [(s, s ^ j) for s in range(size)])

    def sideways(value):
        return [swap(value, j) for j in range(1, across)]

    middle = lambda value: move(value, lambda z, x: (3 - z, x) if z in (1, 2) else None)
    inward = lambda value: move(value, lambda z, x: (z ^ 1, x) if z in (1, 2) else None)
    line = lambda value, d: swap(value, d * across)
    piece_for = lambda j: lax.dynamic_slice_in_dim(grads, owners[me ^ j] * units, units, axis=1)
    send = lambda pieces, js: {j: swap(pieces[j], j) for j in js}
    aside = lambda d: [d * across + j for j in range(1, across)]

    a1, a2, a3 = line(own, 1), middle(own), sideways(own)
    pieces = {j: piece_for(j) for j in range(size)}
    p_own = project([own], turn_in, query)
    a1, a2, a3, pieces, p_own = hold((a1, a2, a3, pieces, p_own))
    b1, b2, b3 = middle(a1), inward(a2), sideways(a1)
    p_a = project([a1] + a3, turn_in, query)
    r0 = score(pick, p_own[0], p_own[0], pieces[0], turn_out)
    b1, b2, b3, pieces, p_a, r0 = hold((b1, b2, b3, pieces, p_a, r0))
    c1 = inward(b1)
    near = jnp.where(inner, a2, b2)
    near_side = sideways(near)
    got = send(pieces, aside(2) + [3 * across] + aside(0))
    p_b = project([near] + b3, turn_in, query)
    c1, near_side, got, pieces, p_b = hold((c1, near_side, got, pieces, p_b))
    far = jnp.where(inner, b1, c1)
    far_side = sideways(far)
    got.update(send(pieces, [2 * across] + aside(3) + aside(1) + [across]))
    p_c = project([far] + near_side, turn_in, query)
    scores = {0: r0}
    for j in range(1, across):
        scores[j] = score(pick, p_a[j], p_a[j], got[j], turn_out)
    scores, far_side, got, p_c = hold((scores, far_side, got, p_c))
    p_d = project(far_side, turn_in, query)
    scores[across] = score(pick, p_a[0], p_a[0], got[across], turn_out)
    scores[2 * across] = score(pick, p_c[0], p_b[0], got[2 * across], turn_out)
    scores[3 * across] = score(pick, p_b[0], p_c[0], got[3 * across], turn_out)
    for j in range(1, across):
        scores[across + j] = score(pick, p_b[j], p_b[j], got[across + j], turn_out)
        scores[2 * across + j] = score(pick, p_d[j - 1], p_c[j], got[2 * across + j], turn_out)
        scores[3 * across + j] = score(pick, p_c[j], p_d[j - 1], got[3 * across + j], turn_out)
    partial = jnp.concatenate([scores[j] for j in range(size)], axis=0)
    partial = jnp.take(partial, jnp.arange(size) ^ me, axis=0)
    share = jnp.sum(lax.all_to_all(partial, "seq", split_axis=0, concat_axis=0, tiled=True), axis=0)
    return lax.psum(share, "layer")


def solution(mesh):
    placed = (
        P("layer", "seq", None),
        P("layer", "seq", None),
        P("layer", "seq", None),
        P("layer", None, None, None),
        P("layer", "seq", None, None),
        P("layer", None),
    )
    across = mesh.shape["seq"] // LINE
    return jax.shard_map(
        functools.partial(body, across), mesh=mesh, in_specs=placed, out_specs=P("seq"), check_vma=False
    )
```

time: 273 us -> 179 us (0.66)
  waiting for transfers between devices: 154 us -> 74.5 us
  Pallas kernels: 0 us -> 36.5 us
  matrix products: 32.3 us -> 0 us
  starting transfers between devices: 7.24 us -> 26.2 us
  local copies, waits for them, and re-layouts: 34.9 us -> 17.3 us
  between operations: 14.1 us -> 5.41 us
  blocking collectives: 25.1 us -> 16.8 us
    all_to_all x1 -> x0, waiting for transfers between devices: 154 us -> none  [body(): lax.all_to_all(outgoing, 'seq', split_axis=1, concat_axis=0, tiled=True)]
    ppermute x0 -> x16, waiting for transfers between devices: none -> 74.5 us  [the longest x12 61.7 us: swap(): return lax.ppermute(value, 'seq', [(s, s ^ j) for s in range(size)])]
    pallas_call x0 -> x13, Pallas kernels: none -> 36.5 us  [the longest x5 33.4 us: project(): pl.pallas_call(functools.partial(project_kernel, count), grid=(units // s...]
    dot_general x3 -> x0, matrix products: 32.3 us -> none  [the longest x1 22.9 us: body(): lax.dot_general(lax.all_gather(rotated, 'seq', axis=0, tiled=True), query...]
    ppermute x0 -> x16, starting transfers between devices: none -> 26.2 us  [the longest x12 20.4 us: swap(): return lax.ppermute(value, 'seq', [(s, s ^ j) for s in range(size)])]
    unnamed x1 -> x0, blocking collectives: 19 us -> none
    another operation x2 -> x0, local copies, waits for them, and re-layouts: 13.4 us -> none  [the longest x1 7.38 us: turn_rows(): groups = rows.reshape(count, basis.shape[0], basis.shape[1])]
    all_to_all x0 -> x1, blocking collectives: none -> 10.6 us  [body(): lax.all_to_all(partial, 'seq', split_axis=0, concat_axis=0, tiled=True)]
  transfers between devices with their start and end apart: 2 -> 16, of which waited for: 1 -> 10; matrix products, arithmetic and copies ran while one was open for 17% -> 2% of each run, Pallas kernels for 0% -> 16%
where the time goes in v1:
time: 179 us; the launch traced here: 178 us
  waiting for transfers between devices  74.5 us (42%)
  Pallas kernels  36.5 us (20%)
  starting transfers between devices  26.2 us (15%)
  local copies, waits for them, and re-layouts  17.3 us (10%)
  blocking collectives  16.8 us (9%)
  between operations  5.41 us (3%)
    ppermute x12, waiting for transfers between devices, swap(): return lax.ppermute(value, 'seq', [(s, s ^ j) for s in range(size)])  61.7 us
    pallas_call x5, Pallas kernels, project(): pl.pallas_call(functools.partial(project_kernel, count), grid=(units // s...  33.4 us
    ppermute x12, starting transfers between devices, swap(): return lax.ppermute(value, 'seq', [(s, s ^ j) for s in range(size)])  20.4 us
    unnamed x26, local copies, waits for them, and re-layouts  13.1 us
    ppermute x4, waiting for transfers between devices, move(): return lax.ppermute(value, 'seq', pairs)  12.8 us
    all_to_all x1, blocking collectives, body(): lax.all_to_all(partial, 'seq', split_axis=0, concat_axis=0, tiled=True)  10.6 us
    psum x1, blocking collectives, body(): return lax.psum(share, 'layer')  6.16 us
    ppermute x4, starting transfers between devices, move(): return lax.ppermute(value, 'seq', pairs)  5.8 us
  transfers between devices with their start and end apart: 16, of which 10 were waited for; matrix products, arithmetic and copies ran while one was open for 2% of the time, Pallas kernels for 16%

profile of v1, /device:TPU:0, one launch (start us, length us, event | category | flops | bytes accessed | tf_op | source)
XLA Modules:
  0.0 178.2 jit_solution(12819918663956765811)
XLA Ops:
  0.0 3.0 %collective-permute-start = (bf16[128,4096]{1,0:T(8,128)(2,1)}, bf16[128,4096]{1,0:T(8,128)(2,1)}, u32[]{:S(2)}, u32[]{:S(2)}) collective-permute-start(bf16[128,4096]{1,0:T(8,128)(2,1)} %bitcast.70), channel_id=1, source_target_pairs={{0,8},{4,12},{8,0},{12,4},{16,24},{20,28},{24,16},{28,20},{1,9},{5... | collective-permute-start | bytes 3145736 | tf_op jit(solution)/shard_map/ppermute | solution.py:91
  3.0 1.6 collective-permute-start.1
  4.6 1.5 collective-permute-start.2
  6.1 1.6 constant_dynamic-slice_fusion
  12.9 0.0 copy-start
  12.9 5.2 %copy-done = bf16[1,1792,4096]{2,1,0:T(8,128)(2,1)S(1)} copy-done((bf16[1,1792,4096]{2,1,0:T(8,128)(2,1)S(1)}, bf16[1,1792,4096]{2,1,0:T(8,128)(2,1)}, u32[]{:S(2)}) %copy-start) | copy-done | bytes 14680088
  18.1 1.2 copy-done.3
  19.3 1.2 copy-done.5
  20.5 6.3 %shard_map.64 = f32[1,128,1792]{2,1,0:T(8,128)S(1)} custom-call(bf16[128,4096]{1,0:T(8,128)(2,1)S(1)} %bitcast.73, bf16[32,128,128]{2,1,0:T(8,128)(2,1)S(1)} %bitcast.61, bf16[1792,4096]{1,0:T(8,128)(2,1)S(1)} %bitcast.48), custom_call_target="tpu_custom_call" | custom-call | flops 2013265920 | bytes 14680064 | tf_op jit(solution)/shard_map/pallas_call | solution.py:38
  26.8 0.0 copy-start.2
  26.9 1.7 dynamic-slice_bitcast_fusion
  28.5 0.0 collective-permute-done.refs_0_
  28.5 0.0 collective-permute-done.1
  28.5 1.0 collective-permute-done.2.refs_1_
  29.6 1.6 collective-permute-start.3
  31.2 1.3 collective-permute-start.4
  32.5 1.6 collective-permute-start.5
  34.0 0.4 shard_map.66
  34.4 0.0 copy-start.1
  34.4 5.2 %copy-done.1 = bf16[1,1792,4096]{2,1,0:T(8,128)(2,1)S(1)} copy-done((bf16[1,1792,4096]{2,1,0:T(8,128)(2,1)S(1)}, bf16[1,1792,4096]{2,1,0:T(8,128)(2,1)}, u32[]{:S(2)}) %copy-start.1) | copy-done | bytes 14680088
  39.6 7.5 %shard_map.65 = f32[2,128,1792]{2,1,0:T(8,128)S(1)} custom-call(bf16[128,4096]{1,0:T(8,128)(2,1)} %collective-permute-done.refs_0_, bf16[128,4096]{1,0:T(8,128)(2,1)} %collective-permute-done.2.refs_1_, bf16[32,128,128]{2,1,0:T(8,128)(2,1)S(1)} %bitcast.62, bf16[1792,4096]{1,0:T(8,128)(2,1)S(1)} %bitcast.49), custom_call_target="tpu_custom_call" | custom-call | flops 4026531840 | bytes 14680064 | tf_op jit(solution)/shard_map/pallas_call | solution.py:38
  47.2 0.0 collective-permute-done.3
  47.2 11.1 %collective-permute-done.4 = bf16[128,4096]{1,0:T(8,128)(2,1)} collective-permute-done((bf16[128,4096]{1,0:T(8,128)(2,1)}, bf16[128,4096]{1,0:T(8,128)(2,1)}, u32[]{:S(2)}, u32[]{:S(2)}) %collective-permute-start.4) | collective-permute-done | bytes 1048608 | tf_op jit(solution)/shard_map/ppermute | solution.py:88
  58.3 0.0 collective-permute-done.5.refs_1_
  58.3 1.3 broadcast_select_fusion.1.refs_0_
  59.6 1.6 collective-permute-start.7
  61.2 1.3 collective-permute-start.6
  62.5 2.4 %collective-permute-start.10 = (bf16[128,1792]{1,0:T(8,128)(2,1)S(1)}, bf16[128,1792]{1,0:T(8,128)(2,1)S(1)}, u32[]{:S(2)}, u32[]{:S(2)}) collective-permute-start(bf16[128,1792]{1,0:T(8,128)(2,1)S(1)} %copy-done.12), channel_id=1, source_target_pairs={{0,24},{4,28},{8,16},{12,20},{16,8},{20,12},{24,0},{28,4},{1,25},{... | collective-permute-start | bytes 1376264 | tf_op jit(solution)/shard_map/ppermute | solution.py:91
  64.9 0.7 collective-permute-start.8
  65.6 2.7 %collective-permute-start.9 = (bf16[128,1792]{1,0:T(8,128)(2,1)S(1)}, bf16[128,1792]{1,0:T(8,128)(2,1)S(1)}, u32[]{:S(2)}, u32[]{:S(2)}) collective-permute-start(bf16[128,1792]{1,0:T(8,128)(2,1)S(1)} %copy-done.10), channel_id=1, source_target_pairs={{0,20},{4,16},{8,28},{12,24},{16,4},{20,0},{24,12},{28,8},{1,21},{... | collective-permute-start | bytes 1376264 | tf_op jit(solution)/shard_map/ppermute | solution.py:91
  68.3 7.2 %shard_map.67 = f32[2,128,1792]{2,1,0:T(8,128)S(1)} custom-call(bf16[128,4096]{1,0:T(8,128)(2,1)S(1)} %broadcast_select_fusion.1.refs_0_, bf16[128,4096]{1,0:T(8,128)(2,1)} %collective-permute-done.5.refs_1_, bf16[32,128,128]{2,1,0:T(8,128)(2,1)S(1)} %bitcast.63, bf16[1792,4096]{1,0:T(8,128)(2,1)S(1)} %bitcast.50), custom_call_target="tpu_custom_call" | custom-call | flops 4026531840 | bytes 14680064 | tf_op jit(solution)/shard_map/pallas_call | solution.py:38
  75.6 2.3 %collective-permute-done.10.piece = bf16[128,1792]{1,0:T(8,128)(2,1)S(1)} collective-permute-done((bf16[128,1792]{1,0:T(8,128)(2,1)S(1)}, bf16[128,1792]{1,0:T(8,128)(2,1)S(1)}, u32[]{:S(2)}, u32[]{:S(2)}) %collective-permute-start.10) | collective-permute-done | bytes 458784 | tf_op jit(solution)/shard_map/ppermute | solution.py:91
  77.9 14.4 %collective-permute-done.8.piece = bf16[128,1792]{1,0:T(8,128)(2,1)S(1)} collective-permute-done((bf16[128,1792]{1,0:T(8,128)(2,1)S(1)}, bf16[128,1792]{1,0:T(8,128)(2,1)S(1)}, u32[]{:S(2)}, u32[]{:S(2)}) %collective-permute-start.8) | collective-permute-done | bytes 458784 | tf_op jit(solution)/shard_map/ppermute | solution.py:91
  92.3 11.5 %collective-permute-done.9.piece = bf16[128,1792]{1,0:T(8,128)(2,1)S(1)} collective-permute-done((bf16[128,1792]{1,0:T(8,128)(2,1)S(1)}, bf16[128,1792]{1,0:T(8,128)(2,1)S(1)}, u32[]{:S(2)}, u32[]{:S(2)}) %collective-permute-start.9) | collective-permute-done | bytes 458784 | tf_op jit(solution)/shard_map/ppermute | solution.py:91
  103.8 0.0 collective-permute-done.7.refs_1_
  103.8 1.7 collective-permute-done.6
  105.5 0.1 broadcast_select_fusion.refs_0_
  105.7 0.6 collective-permute-start.11
  106.3 0.1 slice_bitcast_fusion.4
  106.4 0.3 copy-done.9
  106.7 1.1 collective-permute-start.12
  107.7 1.7 collective-permute-start.13
  109.4 1.4 collective-permute-start.14
  110.9 2.1 %collective-permute-start.15 = (bf16[128,1792]{1,0:T(8,128)(2,1)S(1)}, bf16[128,1792]{1,0:T(8,128)(2,1)S(1)}, u32[]{:S(2)}, u32[]{:S(2)}) collective-permute-start(bf16[128,1792]{1,0:T(8,128)(2,1)S(1)} %get-tuple-element.80), channel_id=1, source_target_pairs={{0,28},{4,24},{8,20},{12,16},{16,12},{20,8},{24,4},{28,0},{1,29},{... | collective-permute-start | bytes 1376264 | tf_op jit(solution)/shard_map/ppermute | solution.py:91
  113.0 0.4 shard_map.68
  113.4 6.0 %shard_map.69 = f32[2,128,1792]{2,1,0:T(8,128)S(1)} custom-call(bf16[128,4096]{1,0:T(8,128)(2,1)S(1)} %broadcast_select_fusion.refs_0_, bf16[128,4096]{1,0:T(8,128)(2,1)S(1)} %collective-permute-done.7.refs_1_, bf16[32,128,128]{2,1,0:T(8,128)(2,1)S(1)} %bitcast.64, bf16[1792,4096]{1,0:T(8,128)(2,1)S(1)} %bitcast.51), custom_call_target="tpu_custom_call" | custom-call | flops 4026531840 | bytes 14680064 | tf_op jit(solution)/shard_map/pallas_call | solution.py:38
  119.5 0.1 slice_bitcast_fusion.1
  119.6 10.4 %collective-permute-done.12.piece = bf16[128,1792]{1,0:T(8,128)(2,1)S(1)} collective-permute-done((bf16[128,1792]{1,0:T(8,128)(2,1)S(1)}, bf16[128,1792]{1,0:T(8,128)(2,1)S(1)}, u32[]{:S(2)}, u32[]{:S(2)}) %collective-permute-start.12) | collective-permute-done | bytes 458784 | tf_op jit(solution)/shard_map/ppermute | solution.py:91
  130.0 8.3 %collective-permute-done.13.piece = bf16[128,1792]{1,0:T(8,128)(2,1)S(1)} collective-permute-done((bf16[128,1792]{1,0:T(8,128)(2,1)S(1)}, bf16[128,1792]{1,0:T(8,128)(2,1)S(1)}, u32[]{:S(2)}, u32[]{:S(2)}) %collective-permute-start.13) | collective-permute-done | bytes 458784 | tf_op jit(solution)/shard_map/ppermute | solution.py:91
  138.2 3.5 %collective-permute-done.14.piece = bf16[128,1792]{1,0:T(8,128)(2,1)S(1)} collective-permute-done((bf16[128,1792]{1,0:T(8,128)(2,1)S(1)}, bf16[128,1792]{1,0:T(8,128)(2,1)S(1)}, u32[]{:S(2)}, u32[]{:S(2)}) %collective-permute-start.14) | collective-permute-done | bytes 458784 | tf_op jit(solution)/shard_map/ppermute | solution.py:91
  141.8 10.2 %collective-permute-done.15.piece = bf16[128,1792]{1,0:T(8,128)(2,1)S(1)} collective-permute-done((bf16[128,1792]{1,0:T(8,128)(2,1)S(1)}, bf16[128,1792]{1,0:T(8,128)(2,1)S(1)}, u32[]{:S(2)}, u32[]{:S(2)}) %collective-permute-start.15) | collective-permute-done | bytes 458784 | tf_op jit(solution)/shard_map/ppermute | solution.py:91
  151.9 0.0 collective-permute-done.11.refs_0_
  151.9 0.1 slice_bitcast_fusion
  152.1 6.3 %shard_map.73 = f32[1,128,1792]{2,1,0:T(8,128)S(1)} custom-call(bf16[128,4096]{1,0:T(8,128)(2,1)S(1)} %collective-permute-done.11.refs_0_, bf16[32,128,128]{2,1,0:T(8,128)(2,1)S(1)} %bitcast.65, bf16[1792,4096]{1,0:T(8,128)(2,1)S(1)} %bitcast.52), custom_call_target="tpu_custom_call" | custom-call | flops 2013265920 | bytes 14680064 | tf_op jit(solution)/shard_map/pallas_call | solution.py:38
  158.4 0.4 shard_map.76
  158.8 0.4 shard_map.74
  159.2 0.4 shard_map.75
  159.6 0.4 shard_map.72
  160.0 0.4 shard_map.71
  160.3 0.4 shard_map.70
  160.8 0.6 gather_fusion
  161.3 0.1 bitcast_select_fusion
  161.4 10.6 %all_to_all.6 = f32[8,1,128]{2,1,0:T(1,128)S(1)} all-to-all(f32[8,1,128]{2,1,0:T(1,128)S(1)} %bitcast.74), channel_id=1, replica_groups=mesh['seq'=8,'layer'=4] {'seq'}, dimensions={0} | all-to-all | bytes 8192 | tf_op jit(solution)/shard_map/all_to_all | solution.py:135
  172.0 6.2 %psum.7 = f32[128]{0:T(128)} all-reduce(f32[128]{0:T(128)S(1)} %reduce_sum.9), channel_id=1, replica_groups=mesh['seq'=8,'layer'=4] {'layer'}, use_global_device_ids=true, to_apply=%region_1.2 | all-reduce | flops 128 | bytes 1024 | tf_op jit(solution)/shard_map/psum | solution.py:136
  (23 shorter events, 0.1 us)
Async XLA Ops:
  0.0 28.5 %collective-permute-start = (bf16[128,4096]{1,0:T(8,128)(2,1)}, bf16[128,4096]{1,0:T(8,128)(2,1)}, u32[]{:S(2)}, u32[]{:S(2)}) collective-permute-start(bf16[128,4096]{1,0:T(8,128)(2,1)} %bitcast.70), channel_id=1, source_target_pairs={{0,8},{4,12},{8,0},{12,4},{16,24},{20,28},{24,16},{28,20},{1,9},{5... | collective-permute-start | bytes 3145736 | tf_op jit(solution)/shard_map/ppermute | solution.py:91
  3.0 25.5 %collective-permute-start.1 = (bf16[128,4096]{1,0:T(8,128)(2,1)}, bf16[128,4096]{1,0:T(8,128)(2,1)}, u32[]{:S(2)}, u32[]{:S(2)}) collective-permute-start(bf16[128,4096]{1,0:T(8,128)(2,1)} %bitcast.71), channel_id=1, source_target_pairs={{8,16},{12,20},{16,8},{20,12},{9,17},{13,21},{17,9},{21,13},{10,18... | collective-permute-start | bytes 3145736 | tf_op jit(solution)/shard_map/ppermute | solution.py:88
  4.6 24.9 %collective-permute-start.2 = (bf16[128,4096]{1,0:T(8,128)(2,1)}, bf16[128,4096]{1,0:T(8,128)(2,1)}, u32[]{:S(2)}, u32[]{:S(2)}) collective-permute-start(bf16[128,4096]{1,0:T(8,128)(2,1)} %bitcast.72), channel_id=1, source_target_pairs={{0,4},{4,0},{8,12},{12,8},{16,20},{20,16},{24,28},{28,24},{1,5},{5... | collective-permute-start | bytes 3145736 | tf_op jit(solution)/shard_map/ppermute | solution.py:91
  12.9 5.2 %copy-start = (bf16[1,1792,4096]{2,1,0:T(8,128)(2,1)S(1)}, bf16[1,1792,4096]{2,1,0:T(8,128)(2,1)}, u32[]{:S(2)}) copy-start(bf16[1,1792,4096]{2,1,0:T(8,128)(2,1)} %param.8) | copy-start | bytes 44040196
  18.1 1.2 copy-start.3
  19.3 1.2 copy-start.5
  20.5 6.3 %copy-start.6 = (bf16[1,128,14336]{2,1,0:T(8,128)(2,1)S(1)}, bf16[1,128,14336]{2,1,0:T(8,128)(2,1)}, u32[]{:S(2)}) copy-start(bf16[1,128,14336]{2,1,0:T(8,128)(2,1)} %param.7) | copy-start | bytes 11010052
  26.8 7.2 %copy-start.2 = (bf16[1,14,128,128]{3,2,1,0:T(8,128)(2,1)S(1)}, bf16[1,14,128,128]{3,2,1,0:T(8,128)(2,1)}, u32[]{:S(2)}) copy-start(bf16[1,14,128,128]{3,2,1,0:T(8,128)(2,1)} %param.10) | copy-start | bytes 1376260
  28.5 5.9 %copy-start.4 = (bf16[1,32,128,128]{3,2,1,0:T(8,128)(2,1)S(1)}, bf16[1,32,128,128]{3,2,1,0:T(8,128)(2,1)}, u32[]{:S(2)}) copy-start(bf16[1,32,128,128]{3,2,1,0:T(8,128)(2,1)} %param.9) | copy-start | bytes 3145732
  29.6 17.6 %collective-permute-start.3 = (bf16[128,4096]{1,0:T(8,128)(2,1)}, bf16[128,4096]{1,0:T(8,128)(2,1)}, u32[]{:S(2)}, u32[]{:S(2)}) collective-permute-start(bf16[128,4096]{1,0:T(8,128)(2,1)} %collective-permute-done.refs_0_), channel_id=1, source_target_pairs={{8,16},{12,20},{16,8},{20,12},{9,17},{13,21},{17,9},{21,13},{10,18... | collective-permute-start | bytes 3145736 | tf_op jit(solution)/shard_map/ppermute | solution.py:88
  31.2 27.1 %collective-permute-start.4 = (bf16[128,4096]{1,0:T(8,128)(2,1)}, bf16[128,4096]{1,0:T(8,128)(2,1)}, u32[]{:S(2)}, u32[]{:S(2)}) collective-permute-start(bf16[128,4096]{1,0:T(8,128)(2,1)} %collective-permute-done.1), channel_id=1, source_target_pairs={{8,0},{12,4},{16,24},{20,28},{9,1},{13,5},{17,25},{21,29},{10,2},{... | collective-permute-start | bytes 3145736 | tf_op jit(solution)/shard_map/ppermute | solution.py:88
  32.5 25.8 %collective-permute-start.5 = (bf16[128,4096]{1,0:T(8,128)(2,1)}, bf16[128,4096]{1,0:T(8,128)(2,1)}, u32[]{:S(2)}, u32[]{:S(2)}) collective-permute-start(bf16[128,4096]{1,0:T(8,128)(2,1)} %collective-permute-done.refs_0_), channel_id=1, source_target_pairs={{0,4},{4,0},{8,12},{12,8},{16,20},{20,16},{24,28},{28,24},{1,5},{5... | collective-permute-start | bytes 3145736 | tf_op jit(solution)/shard_map/ppermute | solution.py:91
  34.4 5.2 %copy-start.1 = (bf16[1,1792,4096]{2,1,0:T(8,128)(2,1)S(1)}, bf16[1,1792,4096]{2,1,0:T(8,128)(2,1)}, u32[]{:S(2)}) copy-start(bf16[1,1792,4096]{2,1,0:T(8,128)(2,1)} %param.8) | copy-start | bytes 44040196
  47.2 15.3 %copy-start.12 = (bf16[128,1792]{1,0:T(8,128)(2,1)S(1)}, bf16[128,1792]{1,0:T(8,128)(2,1)}, u32[]{:S(2)}) copy-start(bf16[128,1792]{1,0:T(8,128)(2,1)} %get-tuple-element.67) | copy-start | bytes 1376260
  47.2 17.7 %copy-start.11 = (bf16[128,1792]{1,0:T(8,128)(2,1)S(1)}, bf16[128,1792]{1,0:T(8,128)(2,1)}, u32[]{:S(2)}) copy-start(bf16[128,1792]{1,0:T(8,128)(2,1)} %get-tuple-element.65) | copy-start | bytes 1376260
  47.2 18.4 %copy-start.10 = (bf16[128,1792]{1,0:T(8,128)(2,1)S(1)}, bf16[128,1792]{1,0:T(8,128)(2,1)}, u32[]{:S(2)}) copy-start(bf16[128,1792]{1,0:T(8,128)(2,1)} %get-tuple-element.66) | copy-start | bytes 1376260
  59.6 44.2 %collective-permute-start.7 = (bf16[128,4096]{1,0:T(8,128)(2,1)S(1)}, bf16[128,4096]{1,0:T(8,128)(2,1)S(1)}, u32[]{:S(2)}, u32[]{:S(2)}) collective-permute-start(bf16[128,4096]{1,0:T(8,128)(2,1)S(1)} %broadcast_select_fusion.1.refs_0_), channel_id=1, source_target_pairs={{0,4},{4,0},{8,12},{12,8},{16,20},{20,16},{24,28},{28,24},{1,5},{5... | collective-permute-start | bytes 3145736 | tf_op jit(solution)/shard_map/ppermute | solution.py:91
  61.2 44.4 %collective-permute-start.6 = (bf16[128,4096]{1,0:T(8,128)(2,1)}, bf16[128,4096]{1,0:T(8,128)(2,1)S(1)}, u32[]{:S(2)}, u32[]{:S(2)}) collective-permute-start(bf16[128,4096]{1,0:T(8,128)(2,1)} %collective-permute-done.3), channel_id=1, source_target_pairs={{8,0},{12,4},{16,24},{20,28},{9,1},{13,5},{17,25},{21,29},{10,2},{... | collective-permute-start | bytes 3145736 | tf_op jit(solution)/shard_map/ppermute | solution.py:88
  62.5 15.4 %collective-permute-start.10 = (bf16[128,1792]{1,0:T(8,128)(2,1)S(1)}, bf16[128,1792]{1,0:T(8,128)(2,1)S(1)}, u32[]{:S(2)}, u32[]{:S(2)}) collective-permute-start(bf16[128,1792]{1,0:T(8,128)(2,1)S(1)} %copy-done.12), channel_id=1, source_target_pairs={{0,24},{4,28},{8,16},{12,20},{16,8},{20,12},{24,0},{28,4},{1,25},{... | collective-permute-start | bytes 1376264 | tf_op jit(solution)/shard_map/ppermute | solution.py:91
  64.9 27.4 %collective-permute-start.8 = (bf16[128,1792]{1,0:T(8,128)(2,1)S(1)}, bf16[128,1792]{1,0:T(8,128)(2,1)S(1)}, u32[]{:S(2)}, u32[]{:S(2)}) collective-permute-start(bf16[128,1792]{1,0:T(8,128)(2,1)S(1)} %copy-done.11), channel_id=1, source_target_pairs={{0,4},{4,0},{8,12},{12,8},{16,20},{20,16},{24,28},{28,24},{1,5},{5... | collective-permute-start | bytes 1376264 | tf_op jit(solution)/shard_map/ppermute | solution.py:91
  65.6 38.2 %collective-permute-start.9 = (bf16[128,1792]{1,0:T(8,128)(2,1)S(1)}, bf16[128,1792]{1,0:T(8,128)(2,1)S(1)}, u32[]{:S(2)}, u32[]{:S(2)}) collective-permute-start(bf16[128,1792]{1,0:T(8,128)(2,1)S(1)} %copy-done.10), channel_id=1, source_target_pairs={{0,20},{4,16},{8,28},{12,24},{16,4},{20,0},{24,12},{28,8},{1,21},{... | collective-permute-start | bytes 1376264 | tf_op jit(solution)/shard_map/ppermute | solution.py:91
  105.7 1.0 copy-start.9
  105.7 2.1 %copy-start.8 = (bf16[128,1792]{1,0:T(8,128)(2,1)S(1)}, bf16[128,1792]{1,0:T(8,128)(2,1)}, u32[]{:S(2)}) copy-start(bf16[128,1792]{1,0:T(8,128)(2,1)} %get-tuple-element.76) | copy-start | bytes 1376260
  105.7 3.8 %copy-start.7 = (bf16[128,1792]{1,0:T(8,128)(2,1)S(1)}, bf16[128,1792]{1,0:T(8,128)(2,1)}, u32[]{:S(2)}) copy-start(bf16[128,1792]{1,0:T(8,128)(2,1)} %get-tuple-element.77) | copy-start | bytes 1376260
  105.7 46.3 %collective-permute-start.11 = (bf16[128,4096]{1,0:T(8,128)(2,1)S(1)}, bf16[128,4096]{1,0:T(8,128)(2,1)S(1)}, u32[]{:S(2)}, u32[]{:S(2)}) collective-permute-start(bf16[128,4096]{1,0:T(8,128)(2,1)S(1)} %broadcast_select_fusion.refs_0_), channel_id=1, source_target_pairs={{0,4},{4,0},{8,12},{12,8},{16,20},{20,16},{24,28},{28,24},{1,5},{5... | collective-permute-start | bytes 3145736 | tf_op jit(solution)/shard_map/ppermute | solution.py:91
  106.7 23.3 %collective-permute-start.12 = (bf16[128,1792]{1,0:T(8,128)(2,1)S(1)}, bf16[128,1792]{1,0:T(8,128)(2,1)S(1)}, u32[]{:S(2)}, u32[]{:S(2)}) collective-permute-start(bf16[128,1792]{1,0:T(8,128)(2,1)S(1)} %copy-done.9), channel_id=1, source_target_pairs={{0,8},{4,12},{8,0},{12,4},{16,24},{20,28},{24,16},{28,20},{1,9},{5... | collective-permute-start | bytes 1376264 | tf_op jit(solution)/shard_map/ppermute | solution.py:91
  107.7 30.5 %collective-permute-start.13 = (bf16[128,1792]{1,0:T(8,128)(2,1)S(1)}, bf16[128,1792]{1,0:T(8,128)(2,1)S(1)}, u32[]{:S(2)}, u32[]{:S(2)}) collective-permute-start(bf16[128,1792]{1,0:T(8,128)(2,1)S(1)} %copy-done.8), channel_id=1, source_target_pairs={{0,12},{4,8},{8,4},{12,0},{16,28},{20,24},{24,20},{28,16},{1,13},{... | collective-permute-start | bytes 1376264 | tf_op jit(solution)/shard_map/ppermute | solution.py:91
  109.4 32.3 %collective-permute-start.14 = (bf16[128,1792]{1,0:T(8,128)(2,1)S(1)}, bf16[128,1792]{1,0:T(8,128)(2,1)S(1)}, u32[]{:S(2)}, u32[]{:S(2)}) collective-permute-start(bf16[128,1792]{1,0:T(8,128)(2,1)S(1)} %copy-done.7), channel_id=1, source_target_pairs={{0,16},{4,20},{8,24},{12,28},{16,0},{20,4},{24,8},{28,12},{1,17},{... | collective-permute-start | bytes 1376264 | tf_op jit(solution)/shard_map/ppermute | solution.py:91
  110.9 41.0 %collective-permute-start.15 = (bf16[128,1792]{1,0:T(8,128)(2,1)S(1)}, bf16[128,1792]{1,0:T(8,128)(2,1)S(1)}, u32[]{:S(2)}, u32[]{:S(2)}) collective-permute-start(bf16[128,1792]{1,0:T(8,128)(2,1)S(1)} %get-tuple-element.80), channel_id=1, source_target_pairs={{0,28},{4,24},{8,20},{12,16},{16,12},{20,8},{24,4},{28,0},{1,29},{... | collective-permute-start | bytes 1376264 | tf_op jit(solution)/shard_map/ppermute | solution.py:91

commit v2 on v1

--- a/solution.py
+++ b/solution.py
@@ -71,6 +71,50 @@
     )(pick, first, second, piece, basis)
 
 
+def back_kernel(found, basis, out):
+    order = basis.shape[1]
+    for n in range(basis.shape[0]):
+        part = pl.ds(n * order, order)
+        held = found[:, part]
+        high = held.astype(jnp.bfloat16)
+        low = (held - high.astype(jnp.float32)).astype(jnp.bfloat16)
+        turned = lax.dot_general(high, basis[n], NT, preferred_element_type=jnp.float32)
+        turned += lax.dot_general(low, basis[n], NT, preferred_element_type=jnp.float32)
+        out[:, part] = turned.astype(jnp.bfloat16)
+
+
+def back(found, basis):
+    vmem = pl.BlockSpec(memory_space=pltpu.VMEM)
+    return pl.pallas_call(
+        back_kernel,
+        in_specs=[vmem] * 2,
+        out_specs=vmem,
+        out_shape=jax.ShapeDtypeStruct(found.shape, jnp.bfloat16),
+        compiler_params=pltpu.CompilerParams(vmem_limit_bytes=16 * 2**20),
+    )(found, basis)
+
+
+def meet_kernel(count, *refs):
+    out = refs[-1]
+    total = jnp.zeros((refs[0].shape[0], TILE), jnp.float32)
+    for c in range(count):
+        for n in range(refs[c].shape[1] // TILE):
+            part = pl.ds(n * TILE, TILE)
+            total += refs[c][:, part].astype(jnp.float32) * refs[count + c][:, part].astype(jnp.float32)
+    out[...] = jnp.sum(total.T, axis=0, keepdims=True)
+
+
+def meet(lefts, rights):
+    vmem = pl.BlockSpec(memory_space=pltpu.VMEM)
+    return pl.pallas_call(
+        functools.partial(meet_kernel, len(lefts)),
+        in_specs=[vmem] * (2 * len(lefts)),
+        out_specs=vmem,
+        out_shape=jax.ShapeDtypeStruct((1, lefts[0].shape[0]), jnp.float32),
+        compiler_params=pltpu.CompilerParams(vmem_limit_bytes=16 * 2**20),
+    )(*lefts, *rights)
+
+
 def body(across, train_inputs, out_grads, query_blocks, basis_in, basis_out, block_of):
     own, grads, query = train_inputs[0], out_grads[0], query_blocks[0]
     turn_in, turn_out, owners = basis_in[0], basis_out[0], block_of[0]
@@ -97,8 +141,9 @@
     inward = lambda value: move(value, lambda z, x: (z ^ 1, x) if z in (1, 2) else None)
     line = lambda value, d: swap(value, d * across)
     piece_for = lambda j: lax.dynamic_slice_in_dim(grads, owners[me ^ j] * units, units, axis=1)
-    send = lambda pieces, js: {j: swap(pieces[j], j) for j in js}
+    send = lambda values: {j: swap(value, j) for j, value in values.items()}
     aside = lambda d: [d * across + j for j in range(1, across)]
+    forward = aside(2) + aside(3)
 
     a1, a2, a3 = line(own, 1), middle(own), sideways(own)
     pieces = {j: piece_for(j) for j in range(size)}
@@ -106,34 +151,38 @@
     a1, a2, a3, pieces, p_own = hold((a1, a2, a3, pieces, p_own))
     b1, b2, b3 = middle(a1), inward(a2), sideways(a1)
     p_a = project([a1] + a3, turn_in, query)
-    r0 = score(pick, p_own[0], p_own[0], pieces[0], turn_out)
-    b1, b2, b3, pieces, p_a, r0 = hold((b1, b2, b3, pieces, p_a, r0))
+    total = score(pick, p_own[0], p_own[0], pieces[0], turn_out)
+    b1, b2, b3, pieces, p_a, total = hold((b1, b2, b3, pieces, p_a, total))
     c1 = inward(b1)
     near = jnp.where(inner, a2, b2)
     near_side = sideways(near)
-    got = send(pieces, aside(2) + [3 * across] + aside(0))
+    got = send({j: pieces[j] for j in forward})
     p_b = project([near] + b3, turn_in, query)
-    c1, near_side, got, pieces, p_b = hold((c1, near_side, got, pieces, p_b))
+    ready = {across: back(p_a[0], turn_out)}
+    for j in range(1, across):
+        ready[j] = back(p_a[j], turn_out)
+        ready[across + j] = back(p_b[j], turn_out)
+    c1, near_side, got, pieces, p_b, ready = hold((c1, near_side, got, pieces, p_b, ready))
     far = jnp.where(inner, b1, c1)
     far_side = sideways(far)
-    got.update(send(pieces, [2 * across] + aside(3) + aside(1) + [across]))
+    got[3 * across] = swap(pieces[3 * across], 3 * across)
+    come = {across: swap(ready[across], across)}
     p_c = project([far] + near_side, turn_in, query)
-    scores = {0: r0}
+    come[2 * across] = swap(back(jnp.where(inner, p_c[0], p_b[0]), turn_out), 2 * across)
+    far_side, late, p_c = hold((far_side, {j: ready[j] for j in aside(0) + aside(1)}, p_c))
+    come.update(send(late))
+    p_d = project(far_side, turn_in, query)
+    sums = {3 * across: score(pick, p_b[0], p_c[0], got[3 * across], turn_out)}
     for j in range(1, across):
-        scores[j] = score(pick, p_a[j], p_a[j], got[j], turn_out)
-    scores, far_side, got, p_c = hold((scores, far_side, got, p_c))
-    p_d = project(far_side, turn_in, query)
-    scores[across] = score(pick, p_a[0], p_a[0], got[across], turn_out)
-    scores[2 * across] = score(pick, p_c[0], p_b[0], got[2 * across], turn_out)
-    scores[3 * across] = score(pick, p_b[0], p_c[0], got[3 * across], turn_out)
-    for j in range(1, across):
-        scores[across + j] = score(pick, p_b[j], p_b[j], got[across + j], turn_out)
-        scores[2 * across + j] = score(pick, p_d[j - 1], p_c[j], got[2 * across + j], turn_out)
-        scores[3 * across + j] = score(pick, p_c[j], p_d[j - 1], got[3 * across + j], turn_out)
-    partial = jnp.concatenate([scores[j] for j in range(size)], axis=0)
-    partial = jnp.take(partial, jnp.arange(size) ^ me, axis=0)
-    share = jnp.sum(lax.all_to_all(partial, "seq", split_axis=0, concat_axis=0, tiled=True), axis=0)
-    return lax.psum(share, "layer")
+        sums[2 * across + j] = score(pick, p_d[j - 1], p_c[j], got[2 * across + j], turn_out)
+        sums[3 * across + j] = score(pick, p_c[j], p_d[j - 1], got[3 * across + j], turn_out)
+    for value in send(sums).values():
+        total += value
+    first = [across, 2 * across]
+    total += meet([come[j] for j in first], [pieces[j] for j in first])
+    total, late = hold((total, {j: come[j] for j in late}))
+    total += meet(list(late.values()), [pieces[j] for j in late])
+    return lax.psum(total[0], "layer")
 
 
 def solution(mesh):

time: 179 us -> 167 us (0.933)
  waiting for transfers between devices: 74.5 us -> 50.2 us
  starting transfers between devices: 26.2 us -> 47.7 us
  blocking collectives: 16.8 us -> 6.17 us
  Pallas kernels: 36.5 us -> 38.7 us
    ppermute x12 -> x15, waiting for transfers between devices: 61.7 us -> 38.2 us  [swap(): return lax.ppermute(value, 'seq', [(s, s ^ j) for s in range(size)])]
    ppermute x12 -> x15, starting transfers between devices: 20.4 us -> 41.7 us  [swap(): return lax.ppermute(value, 'seq', [(s, s ^ j) for s in range(size)])]
    all_to_all x1 -> x0, blocking collectives: 10.6 us -> none  [body(): lax.all_to_all(partial, 'seq', split_axis=0, concat_axis=0, tiled=True)]
    pallas_call x0 -> x6, Pallas kernels: none -> 3.67 us  [the longest x4 3 us: back(): pl.pallas_call(back_kernel, in_specs=[vmem] * 2, out_specs=vmem, out_shap...]
    unnamed x26 -> x28, local copies, waits for them, and re-layouts: 13.1 us -> 13 us
  transfers between devices with their start and end apart: 16 -> 19, of which waited for: 10 -> 8; matrix products, arithmetic and copies ran while one was open for 2% -> 2% of each run, Pallas kernels for 16% -> 23%
where the time goes in v2:
time: 167 us; the launch traced here: 166 us
  waiting for transfers between devices  50.2 us (30%)
  starting transfers between devices  47.7 us (29%)
  Pallas kernels  38.7 us (23%)
  local copies, waits for them, and re-layouts  16.6 us (10%)
  blocking collectives  6.17 us (4%)
  between operations  5.37 us (3%)
    ppermute x15, starting transfers between devices, swap(): return lax.ppermute(value, 'seq', [(s, s ^ j) for s in range(size)])  41.7 us
    ppermute x15, waiting for transfers between devices, swap(): return lax.ppermute(value, 'seq', [(s, s ^ j) for s in range(size)])  38.2 us
    pallas_call x5, Pallas kernels, project(): pl.pallas_call(functools.partial(project_kernel, count), grid=(units // s...  33.5 us
    unnamed x28, local copies, waits for them, and re-layouts  13 us
    ppermute x4, waiting for transfers between devices, move(): return lax.ppermute(value, 'seq', pairs)  12 us
    psum x1, blocking collectives, body(): return lax.psum(total[0], 'layer')  6.17 us
    ppermute x4, starting transfers between devices, move(): return lax.ppermute(value, 'seq', pairs)  6 us
  transfers between devices with their start and end apart: 19, of which 8 were waited for; matrix products, arithmetic and copies ran while one was open for 2% of the time, Pallas kernels for 23%

profile of v2, /device:TPU:0, one launch (start us, length us, event | category | flops | bytes accessed | tf_op | source)
XLA Modules:
  0.0 166.4 jit_solution(12323096055850191706)
XLA Ops:
  0.0 3.0 %collective-permute-start = (bf16[128,4096]{1,0:T(8,128)(2,1)}, bf16[128,4096]{1,0:T(8,128)(2,1)}, u32[]{:S(2)}, u32[]{:S(2)}) collective-permute-start(bf16[128,4096]{1,0:T(8,128)(2,1)} %bitcast.73), channel_id=1, source_target_pairs={{0,8},{4,12},{8,0},{12,4},{16,24},{20,28},{24,16},{28,20},{1,9},{5... | collective-permute-start | bytes 3145736 | tf_op jit(solution)/shard_map/ppermute | solution.py:135
  3.0 1.6 collective-permute-start.1
  4.6 1.5 collective-permute-start.2
  6.1 1.6 constant_dynamic-slice_fusion
  12.8 0.0 copy-start
  12.8 5.2 %copy-done = bf16[1,1792,4096]{2,1,0:T(8,128)(2,1)S(1)} copy-done((bf16[1,1792,4096]{2,1,0:T(8,128)(2,1)S(1)}, bf16[1,1792,4096]{2,1,0:T(8,128)(2,1)}, u32[]{:S(2)}) %copy-start) | copy-done | bytes 14680088
  18.0 1.2 copy-done.4
  19.2 1.2 copy-done.9
  20.4 6.3 %shard_map.64 = f32[1,128,1792]{2,1,0:T(8,128)S(1)} custom-call(bf16[128,4096]{1,0:T(8,128)(2,1)S(1)} %bitcast.76, bf16[32,128,128]{2,1,0:T(8,128)(2,1)S(1)} %bitcast.64, bf16[1792,4096]{1,0:T(8,128)(2,1)S(1)} %bitcast.51), custom_call_target="tpu_custom_call" | custom-call | flops 2013265920 | bytes 14680064 | tf_op jit(solution)/shard_map/pallas_call | solution.py:38
  26.8 0.0 copy-start.3
  26.8 1.6 dynamic-slice_bitcast_fusion
  28.4 0.0 collective-permute-done.1
  28.4 1.2 collective-permute-done.2.refs_1_
  29.6 1.6 collective-permute-start.3
  31.2 1.3 collective-permute-start.4
  32.5 1.6 collective-permute-start.5
  34.1 0.4 shard_map.66
  34.5 0.0 copy-start.1
  34.5 5.2 %copy-done.1 = bf16[1,1792,4096]{2,1,0:T(8,128)(2,1)S(1)} copy-done((bf16[1,1792,4096]{2,1,0:T(8,128)(2,1)S(1)}, bf16[1,1792,4096]{2,1,0:T(8,128)(2,1)}, u32[]{:S(2)}) %copy-start.1) | copy-done | bytes 14680088
  39.6 7.7 %shard_map.65 = f32[2,128,1792]{2,1,0:T(8,128)S(1)} custom-call(bf16[128,4096]{1,0:T(8,128)(2,1)} %collective-permute-done.refs_0_, bf16[128,4096]{1,0:T(8,128)(2,1)} %collective-permute-done.2.refs_1_, bf16[32,128,128]{2,1,0:T(8,128)(2,1)S(1)} %bitcast.65, bf16[1792,4096]{1,0:T(8,128)(2,1)S(1)} %bitcast.52), custom_call_target="tpu_custom_call" | custom-call | flops 4026531840 | bytes 14680064 | tf_op jit(solution)/shard_map/pallas_call | solution.py:38
  47.4 0.0 collective-permute-done.3
  47.4 10.9 %collective-permute-done.4 = bf16[128,4096]{1,0:T(8,128)(2,1)} collective-permute-done((bf16[128,4096]{1,0:T(8,128)(2,1)}, bf16[128,4096]{1,0:T(8,128)(2,1)}, u32[]{:S(2)}, u32[]{:S(2)}) %collective-permute-start.4) | collective-permute-done | bytes 1048608 | tf_op jit(solution)/shard_map/ppermute | solution.py:132
  58.3 0.0 collective-permute-done.5.refs_1_
  58.3 1.3 broadcast_select_fusion.1.refs_0_
  59.6 1.6 collective-permute-start.7
  61.2 1.5 collective-permute-start.6
  62.7 7.3 %shard_map.67 = f32[2,128,1792]{2,1,0:T(8,128)S(1)} custom-call(bf16[128,4096]{1,0:T(8,128)(2,1)S(1)} %broadcast_select_fusion.1.refs_0_, bf16[128,4096]{1,0:T(8,128)(2,1)} %collective-permute-done.5.refs_1_, bf16[32,128,128]{2,1,0:T(8,128)(2,1)S(1)} %bitcast.66, bf16[1792,4096]{1,0:T(8,128)(2,1)S(1)} %bitcast.53), custom_call_target="tpu_custom_call" | custom-call | flops 4026531840 | bytes 14680064 | tf_op jit(solution)/shard_map/pallas_call | solution.py:38
  69.9 0.1 slice_bitcast_fusion.1.found
  70.0 0.7 shard_map.70
  70.8 0.2 copy-done.13
  70.9 3.8 %collective-permute-start.8 = (bf16[128,1792]{1,0:T(8,128)(2,1)S(1)}, bf16[128,1792]{1,0:T(8,128)(2,1)S(1)}, u32[]{:S(2)}, u32[]{:S(2)}) collective-permute-start(bf16[128,1792]{1,0:T(8,128)(2,1)S(1)} %copy-done.13), channel_id=1, source_target_pairs={{0,20},{4,16},{8,28},{12,24},{16,4},{20,0},{24,12},{28,8},{1,21},{... | collective-permute-start | bytes 1376264 | tf_op jit(solution)/shard_map/ppermute | solution.py:135
  74.8 2.3 %collective-permute-start.9 = (bf16[128,1792]{1,0:T(8,128)(2,1)S(1)}, bf16[128,1792]{1,0:T(8,128)(2,1)S(1)}, u32[]{:S(2)}, u32[]{:S(2)}) collective-permute-start(bf16[128,1792]{1,0:T(8,128)(2,1)S(1)} %copy-done.12), channel_id=1, source_target_pairs={{0,28},{4,24},{8,20},{12,16},{16,12},{20,8},{24,4},{28,0},{1,29},{... | collective-permute-start | bytes 1376264 | tf_op jit(solution)/shard_map/ppermute | solution.py:135
  77.1 0.1 slice_bitcast_fusion.5
  77.2 0.7 shard_map.68
  78.0 0.8 shard_map.69
  78.7 25.8 %collective-permute-done.8.piece = bf16[128,1792]{1,0:T(8,128)(2,1)S(1)} collective-permute-done((bf16[128,1792]{1,0:T(8,128)(2,1)S(1)}, bf16[128,1792]{1,0:T(8,128)(2,1)S(1)}, u32[]{:S(2)}, u32[]{:S(2)}) %collective-permute-start.8) | collective-permute-done | bytes 458784 | tf_op jit(solution)/shard_map/ppermute | solution.py:135
  104.5 1.1 collective-permute-done.6
  105.6 0.1 broadcast_select_fusion.refs_0_
  105.7 0.6 collective-permute-start.10
  106.3 6.0 %shard_map.71 = f32[2,128,1792]{2,1,0:T(8,128)S(1)} custom-call(bf16[128,4096]{1,0:T(8,128)(2,1)S(1)} %broadcast_select_fusion.refs_0_, bf16[128,4096]{1,0:T(8,128)(2,1)S(1)} %collective-permute-done.7.refs_1_, bf16[32,128,128]{2,1,0:T(8,128)(2,1)S(1)} %bitcast.67, bf16[1792,4096]{1,0:T(8,128)(2,1)S(1)} %bitcast.54), custom_call_target="tpu_custom_call" | custom-call | flops 4026531840 | bytes 14680064 | tf_op jit(solution)/shard_map/pallas_call | solution.py:38
  112.3 2.4 %collective-permute-start.11 = (bf16[128,1792]{1,0:T(8,128)(2,1)S(1)}, bf16[128,1792]{1,0:T(8,128)(2,1)S(1)}, u32[]{:S(2)}, u32[]{:S(2)}) collective-permute-start(bf16[128,1792]{1,0:T(8,128)(2,1)S(1)} %copy-done.11), channel_id=1, source_target_pairs={{0,24},{4,28},{8,16},{12,20},{16,8},{20,12},{24,0},{28,4},{1,25},{... | collective-permute-start | bytes 1376264 | tf_op jit(solution)/shard_map/ppermute | solution.py:135
  114.7 0.1 fusion.found
  114.8 0.7 shard_map.76
  115.6 8.2 %collective-permute-start.16 = (bf16[128,1792]{1,0:T(8,128)(2,1)S(1)}, bf16[128,1792]{1,0:T(8,128)(2,1)S(1)}, u32[]{:S(2)}, u32[]{:S(2)}) collective-permute-start(bf16[128,1792]{1,0:T(8,128)(2,1)S(1)} %shard_map.76), channel_id=1, source_target_pairs={{0,16},{4,20},{8,24},{12,28},{16,0},{20,4},{24,8},{28,12},{1,17},{... | collective-permute-start | bytes 1376264 | tf_op jit(solution)/shard_map/ppermute | solution.py:135
  123.7 0.0 collective-permute-start.15
  123.7 0.1 slice_bitcast_fusion.4.first
  123.8 4.6 %collective-permute-done.10.refs_0_ = bf16[128,4096]{1,0:T(8,128)(2,1)S(1)} collective-permute-done((bf16[128,4096]{1,0:T(8,128)(2,1)S(1)}, bf16[128,4096]{1,0:T(8,128)(2,1)S(1)}, u32[]{:S(2)}, u32[]{:S(2)}) %collective-permute-start.10) | collective-permute-done | bytes 1048608 | tf_op jit(solution)/shard_map/ppermute | solution.py:135
  128.4 1.3 collective-permute-start.17
  129.7 9.0 %collective-permute-start.18 = (bf16[128,1792]{1,0:T(8,128)(2,1)S(1)}, bf16[128,1792]{1,0:T(8,128)(2,1)S(1)}, u32[]{:S(2)}, u32[]{:S(2)}) collective-permute-start(bf16[128,1792]{1,0:T(8,128)(2,1)S(1)} %shard_map.70), channel_id=1, source_target_pairs={{0,12},{4,8},{8,4},{12,0},{16,28},{20,24},{24,20},{28,16},{1,13},{... | collective-permute-start | bytes 1376264 | tf_op jit(solution)/shard_map/ppermute | solution.py:135
  138.7 0.1 slice_bitcast_fusion.3
  138.8 0.0 collective-permute-done.11.piece
  138.8 0.4 shard_map.72
  139.2 2.4 %collective-permute-start.12 = (f32[1,128]{1,0:T(1,128)S(1)}, f32[1,128]{1,0:T(1,128)S(1)}, u32[]{:S(2)}, u32[]{:S(2)}) collective-permute-start(f32[1,128]{1,0:T(1,128)S(1)} %shard_map.72), channel_id=1, source_target_pairs={{0,24},{4,28},{8,16},{12,20},{16,8},{20,12},{24,0},{28,4},{1,25},{... | collective-permute-start | bytes 1544 | tf_op jit(solution)/shard_map/ppermute | solution.py:135
  141.6 6.3 %shard_map.73 = f32[1,128,1792]{2,1,0:T(8,128)S(1)} custom-call(bf16[128,4096]{1,0:T(8,128)(2,1)S(1)} %collective-permute-done.10.refs_0_, bf16[32,128,128]{2,1,0:T(8,128)(2,1)S(1)} %bitcast.68, bf16[1792,4096]{1,0:T(8,128)(2,1)S(1)} %bitcast.55), custom_call_target="tpu_custom_call" | custom-call | flops 2013265920 | bytes 14680064 | tf_op jit(solution)/shard_map/pallas_call | solution.py:38
  147.9 0.4 shard_map.74
  148.3 0.4 shard_map.75
  148.7 3.5 %collective-permute-done.16.refs_1_ = bf16[128,1792]{1,0:T(8,128)(2,1)S(1)} collective-permute-done((bf16[128,1792]{1,0:T(8,128)(2,1)S(1)}, bf16[128,1792]{1,0:T(8,128)(2,1)S(1)}, u32[]{:S(2)}, u32[]{:S(2)}) %collective-permute-start.16) | collective-permute-done | bytes 458784 | tf_op jit(solution)/shard_map/ppermute | solution.py:135
  152.3 1.3 collective-permute-start.13
  153.6 2.8 %collective-permute-start.14 = (f32[1,128]{1,0:T(1,128)S(1)}, f32[1,128]{1,0:T(1,128)S(1)}, u32[]{:S(2)}, u32[]{:S(2)}) collective-permute-start(f32[1,128]{1,0:T(1,128)S(1)} %shard_map.75), channel_id=1, source_target_pairs={{0,28},{4,24},{8,20},{12,16},{16,12},{20,8},{24,4},{28,0},{1,29},{... | collective-permute-start | bytes 1544 | tf_op jit(solution)/shard_map/ppermute | solution.py:135
  156.4 0.3 shard_map.77
  156.8 0.8 collective-permute-done.13
  157.6 2.2 %collective-permute-done.14 = f32[1,128]{1,0:T(1,128)S(1)} collective-permute-done((f32[1,128]{1,0:T(1,128)S(1)}, f32[1,128]{1,0:T(1,128)S(1)}, u32[]{:S(2)}, u32[]{:S(2)}) %collective-permute-start.14) | collective-permute-done | bytes 544 | tf_op jit(solution)/shard_map/ppermute | solution.py:135
  159.8 0.3 shard_map.78
  160.2 6.2 %psum.7 = f32[128]{0:T(128)} all-reduce(f32[128]{0:T(128)S(1)} %add_bitcast_fusion), channel_id=1, replica_groups=mesh['seq'=8,'layer'=4] {'layer'}, use_global_device_ids=true, to_apply=%region_0.1 | all-reduce | flops 128 | bytes 1024 | tf_op jit(solution)/shard_map/psum | solution.py:185
  (29 shorter events, 0.1 us)
Async XLA Ops:
  0.0 28.4 %collective-permute-start = (bf16[128,4096]{1,0:T(8,128)(2,1)}, bf16[128,4096]{1,0:T(8,128)(2,1)}, u32[]{:S(2)}, u32[]{:S(2)}) collective-permute-start(bf16[128,4096]{1,0:T(8,128)(2,1)} %bitcast.73), channel_id=1, source_target_pairs={{0,8},{4,12},{8,0},{12,4},{16,24},{20,28},{24,16},{28,20},{1,9},{5... | collective-permute-start | bytes 3145736 | tf_op jit(solution)/shard_map/ppermute | solution.py:135
  3.0 25.4 %collective-permute-start.1 = (bf16[128,4096]{1,0:T(8,128)(2,1)}, bf16[128,4096]{1,0:T(8,128)(2,1)}, u32[]{:S(2)}, u32[]{:S(2)}) collective-permute-start(bf16[128,4096]{1,0:T(8,128)(2,1)} %bitcast.74), channel_id=1, source_target_pairs={{8,16},{12,20},{16,8},{20,12},{9,17},{13,21},{17,9},{21,13},{10,18... | collective-permute-start | bytes 3145736 | tf_op jit(solution)/shard_map/ppermute | solution.py:132
  4.6 24.9 %collective-permute-start.2 = (bf16[128,4096]{1,0:T(8,128)(2,1)}, bf16[128,4096]{1,0:T(8,128)(2,1)}, u32[]{:S(2)}, u32[]{:S(2)}) collective-permute-start(bf16[128,4096]{1,0:T(8,128)(2,1)} %bitcast.75), channel_id=1, source_target_pairs={{0,4},{4,0},{8,12},{12,8},{16,20},{20,16},{24,28},{28,24},{1,5},{5... | collective-permute-start | bytes 3145736 | tf_op jit(solution)/shard_map/ppermute | solution.py:135
  12.8 5.2 %copy-start = (bf16[1,1792,4096]{2,1,0:T(8,128)(2,1)S(1)}, bf16[1,1792,4096]{2,1,0:T(8,128)(2,1)}, u32[]{:S(2)}) copy-start(bf16[1,1792,4096]{2,1,0:T(8,128)(2,1)} %param.8) | copy-start | bytes 44040196
  18.0 1.2 copy-start.4
  19.2 1.2 copy-start.9
  20.4 6.3 %copy-start.10 = (bf16[1,128,14336]{2,1,0:T(8,128)(2,1)S(1)}, bf16[1,128,14336]{2,1,0:T(8,128)(2,1)}, u32[]{:S(2)}) copy-start(bf16[1,128,14336]{2,1,0:T(8,128)(2,1)} %param.7) | copy-start | bytes 11010052
  26.8 7.3 %copy-start.3 = (bf16[1,14,128,128]{3,2,1,0:T(8,128)(2,1)S(1)}, bf16[1,14,128,128]{3,2,1,0:T(8,128)(2,1)}, u32[]{:S(2)}) copy-start(bf16[1,14,128,128]{3,2,1,0:T(8,128)(2,1)} %param.10) | copy-start | bytes 1376260
  28.4 6.1 %copy-start.5 = (bf16[1,32,128,128]{3,2,1,0:T(8,128)(2,1)S(1)}, bf16[1,32,128,128]{3,2,1,0:T(8,128)(2,1)}, u32[]{:S(2)}) copy-start(bf16[1,32,128,128]{3,2,1,0:T(8,128)(2,1)} %param.9) | copy-start | bytes 3145732
  29.6 17.8 %collective-permute-start.3 = (bf16[128,4096]{1,0:T(8,128)(2,1)}, bf16[128,4096]{1,0:T(8,128)(2,1)}, u32[]{:S(2)}, u32[]{:S(2)}) collective-permute-start(bf16[128,4096]{1,0:T(8,128)(2,1)} %collective-permute-done.refs_0_), channel_id=1, source_target_pairs={{8,16},{12,20},{16,8},{20,12},{9,17},{13,21},{17,9},{21,13},{10,18... | collective-permute-start | bytes 3145736 | tf_op jit(solution)/shard_map/ppermute | solution.py:132
  31.2 27.1 %collective-permute-start.4 = (bf16[128,4096]{1,0:T(8,128)(2,1)}, bf16[128,4096]{1,0:T(8,128)(2,1)}, u32[]{:S(2)}, u32[]{:S(2)}) collective-permute-start(bf16[128,4096]{1,0:T(8,128)(2,1)} %collective-permute-done.1), channel_id=1, source_target_pairs={{8,0},{12,4},{16,24},{20,28},{9,1},{13,5},{17,25},{21,29},{10,2},{... | collective-permute-start | bytes 3145736 | tf_op jit(solution)/shard_map/ppermute | solution.py:132
  32.5 25.8 %collective-permute-start.5 = (bf16[128,4096]{1,0:T(8,128)(2,1)}, bf16[128,4096]{1,0:T(8,128)(2,1)}, u32[]{:S(2)}, u32[]{:S(2)}) collective-permute-start(bf16[128,4096]{1,0:T(8,128)(2,1)} %collective-permute-done.refs_0_), channel_id=1, source_target_pairs={{0,4},{4,0},{8,12},{12,8},{16,20},{20,16},{24,28},{28,24},{1,5},{5... | collective-permute-start | bytes 3145736 | tf_op jit(solution)/shard_map/ppermute | solution.py:135
  34.5 5.2 %copy-start.1 = (bf16[1,1792,4096]{2,1,0:T(8,128)(2,1)S(1)}, bf16[1,1792,4096]{2,1,0:T(8,128)(2,1)}, u32[]{:S(2)}) copy-start(bf16[1,1792,4096]{2,1,0:T(8,128)(2,1)} %param.8) | copy-start | bytes 44040196
  39.6 23.0 %copy-start.2 = (bf16[1,1792,4096]{2,1,0:T(8,128)(2,1)S(1)}, bf16[1,1792,4096]{2,1,0:T(8,128)(2,1)}, u32[]{:S(2)}) copy-start(bf16[1,1792,4096]{2,1,0:T(8,128)(2,1)} %param.8) | copy-start | bytes 44040196
  59.6 44.9 %collective-permute-start.7 = (bf16[128,4096]{1,0:T(8,128)(2,1)S(1)}, bf16[128,4096]{1,0:T(8,128)(2,1)S(1)}, u32[]{:S(2)}, u32[]{:S(2)}) collective-permute-start(bf16[128,4096]{1,0:T(8,128)(2,1)S(1)} %broadcast_select_fusion.1.refs_0_), channel_id=1, source_target_pairs={{0,4},{4,0},{8,12},{12,8},{16,20},{20,16},{24,28},{28,24},{1,5},{5... | collective-permute-start | bytes 3145736 | tf_op jit(solution)/shard_map/ppermute | solution.py:135
  61.2 44.4 %collective-permute-start.6 = (bf16[128,4096]{1,0:T(8,128)(2,1)}, bf16[128,4096]{1,0:T(8,128)(2,1)S(1)}, u32[]{:S(2)}, u32[]{:S(2)}) collective-permute-start(bf16[128,4096]{1,0:T(8,128)(2,1)} %collective-permute-done.3), channel_id=1, source_target_pairs={{8,0},{12,4},{16,24},{20,28},{9,1},{13,5},{17,25},{21,29},{10,2},{... | collective-permute-start | bytes 3145736 | tf_op jit(solution)/shard_map/ppermute | solution.py:132
  69.9 1.0 copy-start.13
  69.9 4.9 %copy-start.12 = (bf16[128,1792]{1,0:T(8,128)(2,1)S(1)}, bf16[128,1792]{1,0:T(8,128)(2,1)}, u32[]{:S(2)}) copy-start(bf16[128,1792]{1,0:T(8,128)(2,1)} %get-tuple-element.65) | copy-start | bytes 1376260
  70.9 33.6 %collective-permute-start.8 = (bf16[128,1792]{1,0:T(8,128)(2,1)S(1)}, bf16[128,1792]{1,0:T(8,128)(2,1)S(1)}, u32[]{:S(2)}, u32[]{:S(2)}) collective-permute-start(bf16[128,1792]{1,0:T(8,128)(2,1)S(1)} %copy-done.13), channel_id=1, source_target_pairs={{0,20},{4,16},{8,28},{12,24},{16,4},{20,0},{24,12},{28,8},{1,21},{... | collective-permute-start | bytes 1376264 | tf_op jit(solution)/shard_map/ppermute | solution.py:135
  74.8 29.7 %collective-permute-start.9 = (bf16[128,1792]{1,0:T(8,128)(2,1)S(1)}, bf16[128,1792]{1,0:T(8,128)(2,1)S(1)}, u32[]{:S(2)}, u32[]{:S(2)}) collective-permute-start(bf16[128,1792]{1,0:T(8,128)(2,1)S(1)} %copy-done.12), channel_id=1, source_target_pairs={{0,28},{4,24},{8,20},{12,16},{16,12},{20,8},{24,4},{28,0},{1,29},{... | collective-permute-start | bytes 1376264 | tf_op jit(solution)/shard_map/ppermute | solution.py:135
  105.7 6.6 %copy-start.11 = (bf16[128,1792]{1,0:T(8,128)(2,1)S(1)}, bf16[128,1792]{1,0:T(8,128)(2,1)}, u32[]{:S(2)}) copy-start(bf16[128,1792]{1,0:T(8,128)(2,1)} %get-tuple-element.79) | copy-start | bytes 1376260
  105.7 22.7 %collective-permute-start.10 = (bf16[128,4096]{1,0:T(8,128)(2,1)S(1)}, bf16[128,4096]{1,0:T(8,128)(2,1)S(1)}, u32[]{:S(2)}, u32[]{:S(2)}) collective-permute-start(bf16[128,4096]{1,0:T(8,128)(2,1)S(1)} %broadcast_select_fusion.refs_0_), channel_id=1, source_target_pairs={{0,4},{4,0},{8,12},{12,8},{16,20},{20,16},{24,28},{28,24},{1,5},{5... | collective-permute-start | bytes 3145736 | tf_op jit(solution)/shard_map/ppermute | solution.py:135
  112.3 26.5 %collective-permute-start.11 = (bf16[128,1792]{1,0:T(8,128)(2,1)S(1)}, bf16[128,1792]{1,0:T(8,128)(2,1)S(1)}, u32[]{:S(2)}, u32[]{:S(2)}) collective-permute-start(bf16[128,1792]{1,0:T(8,128)(2,1)S(1)} %copy-done.11), channel_id=1, source_target_pairs={{0,24},{4,28},{8,16},{12,20},{16,8},{20,12},{24,0},{28,4},{1,25},{... | collective-permute-start | bytes 1376264 | tf_op jit(solution)/shard_map/ppermute | solution.py:135
  115.6 36.7 %collective-permute-start.16 = (bf16[128,1792]{1,0:T(8,128)(2,1)S(1)}, bf16[128,1792]{1,0:T(8,128)(2,1)S(1)}, u32[]{:S(2)}, u32[]{:S(2)}) collective-permute-start(bf16[128,1792]{1,0:T(8,128)(2,1)S(1)} %shard_map.76), channel_id=1, source_target_pairs={{0,16},{4,20},{8,24},{12,28},{16,0},{20,4},{24,8},{28,12},{1,17},{... | collective-permute-start | bytes 1376264 | tf_op jit(solution)/shard_map/ppermute | solution.py:135
  123.7 29.9 %collective-permute-start.15 = (bf16[128,1792]{1,0:T(8,128)(2,1)S(1)}, bf16[128,1792]{1,0:T(8,128)(2,1)S(1)}, u32[]{:S(2)}, u32[]{:S(2)}) collective-permute-start(bf16[128,1792]{1,0:T(8,128)(2,1)S(1)} %shard_map.69), channel_id=1, source_target_pairs={{0,8},{4,12},{8,0},{12,4},{16,24},{20,28},{24,16},{28,20},{1,9},{5... | collective-permute-start | bytes 1376264 | tf_op jit(solution)/shard_map/ppermute | solution.py:135
  128.4 31.4 %collective-permute-start.17 = (bf16[128,1792]{1,0:T(8,128)(2,1)S(1)}, bf16[128,1792]{1,0:T(8,128)(2,1)S(1)}, u32[]{:S(2)}, u32[]{:S(2)}) collective-permute-start(bf16[128,1792]{1,0:T(8,128)(2,1)S(1)} %shard_map.68), channel_id=1, source_target_pairs={{0,4},{4,0},{8,12},{12,8},{16,20},{20,16},{24,28},{28,24},{1,5},{5... | collective-permute-start | bytes 1376264 | tf_op jit(solution)/shard_map/ppermute | solution.py:135
  129.7 30.2 %collective-permute-start.18 = (bf16[128,1792]{1,0:T(8,128)(2,1)S(1)}, bf16[128,1792]{1,0:T(8,128)(2,1)S(1)}, u32[]{:S(2)}, u32[]{:S(2)}) collective-permute-start(bf16[128,1792]{1,0:T(8,128)(2,1)S(1)} %shard_map.70), channel_id=1, source_target_pairs={{0,12},{4,8},{8,4},{12,0},{16,28},{20,24},{24,20},{28,16},{1,13},{... | collective-permute-start | bytes 1376264 | tf_op jit(solution)/shard_map/ppermute | solution.py:135
  139.2 17.5 %collective-permute-start.12 = (f32[1,128]{1,0:T(1,128)S(1)}, f32[1,128]{1,0:T(1,128)S(1)}, u32[]{:S(2)}, u32[]{:S(2)}) collective-permute-start(f32[1,128]{1,0:T(1,128)S(1)} %shard_map.72), channel_id=1, source_target_pairs={{0,24},{4,28},{8,16},{12,20},{16,8},{20,12},{24,0},{28,4},{1,25},{... | collective-permute-start | bytes 1544 | tf_op jit(solution)/shard_map/ppermute | solution.py:135
  148.3 8.1 %copy-start.7 = (bf16[128,1792]{1,0:T(8,128)(2,1)S(1)}, bf16[128,1792]{1,0:T(8,128)(2,1)}, u32[]{:S(2)}) copy-start(bf16[128,1792]{1,0:T(8,128)(2,1)} %get-tuple-element.85.refs_3_) | copy-start | bytes 1376260
  148.3 8.1 %copy-start.8 = (bf16[128,1792]{1,0:T(8,128)(2,1)S(1)}, bf16[128,1792]{1,0:T(8,128)(2,1)}, u32[]{:S(2)}) copy-start(bf16[128,1792]{1,0:T(8,128)(2,1)} %get-tuple-element.84.refs_2_) | copy-start | bytes 1376260
  148.3 11.5 %copy-start.6 = (bf16[128,1792]{1,0:T(8,128)(2,1)S(1)}, bf16[128,1792]{1,0:T(8,128)(2,1)}, u32[]{:S(2)}) copy-start(bf16[128,1792]{1,0:T(8,128)(2,1)} %get-tuple-element.91.refs_2_) | copy-start | bytes 1376260
  152.3 5.3 %collective-permute-start.13 = (f32[1,128]{1,0:T(1,128)S(1)}, f32[1,128]{1,0:T(1,128)S(1)}, u32[]{:S(2)}, u32[]{:S(2)}) collective-permute-start(f32[1,128]{1,0:T(1,128)S(1)} %shard_map.74), channel_id=1, source_target_pairs={{0,20},{4,16},{8,28},{12,24},{16,4},{20,0},{24,12},{28,8},{1,21},{... | collective-permute-start | bytes 1544 | tf_op jit(solution)/shard_map/ppermute | solution.py:135
  153.6 6.2 %collective-permute-start.14 = (f32[1,128]{1,0:T(1,128)S(1)}, f32[1,128]{1,0:T(1,128)S(1)}, u32[]{:S(2)}, u32[]{:S(2)}) collective-permute-start(f32[1,128]{1,0:T(1,128)S(1)} %shard_map.75), channel_id=1, source_target_pairs={{0,28},{4,24},{8,20},{12,16},{16,12},{20,8},{24,4},{28,0},{1,29},{... | collective-permute-start | bytes 1544 | tf_op jit(solution)/shard_map/ppermute | solution.py:135

commit v3 on v1

v3 whole, which is shorter than its diff:
```python
import functools

import jax
import jax.numpy as jnp
from jax import lax
from jax.experimental import pallas as pl
from jax.experimental.pallas import tpu as pltpu
from jax.sharding import PartitionSpec as P

LINE = 4
TILE = 128
MIB = 2**20
NT = (((1,), (1,)), ((), ()))
hold = lax.optimization_barrier
free = pl.CostEstimate(flops=0, bytes_accessed=0, transcendentals=0)


def blocks_of(wide):
    return [pl.ds(n * TILE, TILE) for n in range(wide // TILE)]


def project_kernel(count, *refs):
    chunks, (basis, query, out, turned) = refs[:count], refs[count:]
    rows = chunks[0].shape[0]

    @pl.when(pl.program_id(0) == 0)
    def _():
        for c, chunk in enumerate(chunks):
            for n, part in enumerate(blocks_of(chunk.shape[1])):
                turned[pl.ds(c * rows, rows), part] = jnp.dot(
                    chunk[:, part], basis[n], preferred_element_type=jnp.float32
                ).astype(jnp.bfloat16)

    found = lax.dot_general(turned[...], query[...], NT, preferred_element_type=jnp.float32)
    out[...] = found.reshape(out.shape)


def project(chunks, basis, query):
    count, (rows, wide) = len(chunks), chunks[0].shape
    units = query.shape[0]
    step = 2 * TILE if units % (2 * TILE) == 0 else TILE
    whole = lambda *shape: pl.BlockSpec(shape, lambda i: (0,) * len(shape))
    return pl.pallas_call(
        functools.partial(project_kernel, count),
        grid=(units // step,),
        in_specs=[whole(rows, wide)] * count + [whole(*basis.shape), pl.BlockSpec((step, wide), lambda i: (i, 0))],
        out_specs=pl.BlockSpec((count, rows, step), lambda i: (0, 0, i)),
        out_shape=jax.ShapeDtypeStruct((count, rows, units), jnp.float32),
        scratch_shapes=[pltpu.VMEM((count * rows, wide), jnp.bfloat16)],
        compiler_params=pltpu.CompilerParams(vmem_limit_bytes=50 * MIB),
        cost_estimate=free,
    )(*chunks, basis, query)


def pack_kernel(count, order, *refs):
    for piece, out in zip(refs[:count], refs[count:]):
        out[...] = piece[...]


def pack(offsets, order, grads, units):
    rows, count = grads.shape[0], len(offsets)
    found = pl.pallas_call(
        functools.partial(pack_kernel, count),
        grid_spec=pltpu.PrefetchScalarGridSpec(
            num_scalar_prefetch=1,
            grid=(1,),
            in_specs=[pl.BlockSpec((rows, units), lambda i, order, j=j: (0, order[j])) for j in offsets],
            out_specs=[pl.BlockSpec((rows, units), lambda i, order: (0, 0))] * count,
        ),
        out_shape=[jax.ShapeDtypeStruct((rows, units), grads.dtype)] * count,
        compiler_params=pltpu.CompilerParams(vmem_limit_bytes=16 * MIB),
        cost_estimate=free,
    )(order, *[grads] * count)
    return dict(zip(offsets, found))


def lay(total):
    return jnp.sum(total.T, axis=0, keepdims=True)


def score_kernel(order, found, piece, basis, out):
    total = jnp.zeros((piece.shape[0], TILE), jnp.float32)
    for n, part in enumerate(blocks_of(piece.shape[1])):
        turned = jnp.dot(piece[:, part], basis[n], preferred_element_type=jnp.float32).astype(jnp.bfloat16)
        total += turned.astype(jnp.float32) * found[:, part]
    out[...] = lay(total)


def meet_kernel(count, order, *refs):
    total = jnp.zeros((refs[0].shape[0], TILE), jnp.float32)
    for came, piece in zip(refs[:count], refs[count:-1]):
        for part in blocks_of(piece.shape[1]):
            total += came[:, part].astype(jnp.float32) * piece[:, part].astype(jnp.float32)
    refs[-1][...] = lay(total)


def small(kernel, order, in_specs, rows, *args):
    return pl.pallas_call(
        kernel,
        grid_spec=pltpu.PrefetchScalarGridSpec(
            num_scalar_prefetch=1,
            grid=(1,),
            in_specs=in_specs,
            out_specs=pl.BlockSpec((1, rows), lambda i, order: (0, 0)),
        ),
        out_shape=jax.ShapeDtypeStruct((1, rows), jnp.float32),
        compiler_params=pltpu.CompilerParams(vmem_limit_bytes=16 * MIB),
        cost_estimate=free,
    )(order, *args)


def score(found, c, order, j, values, basis):
    _, rows, units = found.shape
    at = (lambda i, order: (0, 0)) if j is None else (lambda i, order: (0, order[j]))
    specs = [
        pl.BlockSpec((None, rows, units), lambda i, order: (c, 0, 0)),
        pl.BlockSpec((rows, units), at),
        pl.BlockSpec(basis.shape, lambda i, order: (0, 0, 0)),
    ]
    return small(score_kernel, order, specs, rows, found, values, basis)


def meet(come, order, grads):
    offsets = list(come)
    rows, units = come[offsets[0]].shape
    specs = [pl.BlockSpec((rows, units), lambda i, order: (0, 0))] * len(offsets)
    specs += [pl.BlockSpec((rows, units), lambda i, order, j=j: (0, order[j])) for j in offsets]
    args = [come[j] for j in offsets] + [grads] * len(offsets)
    return small(functools.partial(meet_kernel, len(offsets)), order, specs, rows, *args)


def back_kernel(found, basis, out):
    for n, part in enumerate(blocks_of(found.shape[1])):
        held = found[:, part]
        high = held.astype(jnp.bfloat16)
        low = (held - high.astype(jnp.float32)).astype(jnp.bfloat16)
        turned = lax.dot_general(high, basis[n], NT, preferred_element_type=jnp.float32)
        turned += lax.dot_general(low, basis[n], NT, preferred_element_type=jnp.float32)
        out[:, part] = turned.astype(jnp.bfloat16)


def back(found, c, basis):
    _, rows, units = found.shape
    return pl.pallas_call(
        back_kernel,
        grid=(1,),
        in_specs=[
            pl.BlockSpec((None, rows, units), lambda i: (c, 0, 0)),
            pl.BlockSpec(basis.shape, lambda i: (0, 0, 0)),
        ],
        out_specs=pl.BlockSpec((rows, units), lambda i: (0, 0)),
        out_shape=jax.ShapeDtypeStruct((rows, units), jnp.bfloat16),
        compiler_params=pltpu.CompilerParams(vmem_limit_bytes=16 * MIB),
        cost_estimate=free,
    )(found, basis)


def body(across, train_inputs, out_grads, query_blocks, basis_in, basis_out, block_of):
    own, grads, query = train_inputs[0], out_grads[0], query_blocks[0]
    turn_in, turn_out, owners = basis_in[0], basis_out[0], block_of[0]
    size, units = LINE * across, query.shape[0]
    me = lax.axis_index("seq")
    inner = (me // across == 1) | (me // across == 2)
    order = jnp.take(owners, jnp.arange(size) ^ me)

    def move(value, place):
        pairs = []
        for s in range(size):
            to = place(s // across, s % across)
            if to is not None:
                pairs.append((s, to[0] * across + to[1]))
        return lax.ppermute(value, "seq", pairs)

    def swap(value, j):
        return lax.ppermute(value, "seq", [(s, s ^ j) for s in range(size)])

    def sideways(value):
        return [swap(value, j) for j in range(1, across)]

    middle = lambda value: move(value, lambda z, x: (3 - z, x) if z in (1, 2) else None)
    inward = lambda value: move(value, lambda z, x: (z ^ 1, x) if z in (1, 2) else None)
    line = lambda value, d: swap(value, d * across)
    send = lambda values, js: {j: swap(values[j], j) for j in js}
    aside = lambda d: [d * across + j for j in range(1, across)]
    one, two, three = across, 2 * across, 3 * across

    a1, a2, a3 = line(own, 1), middle(own), sideways(own)
    pieces = pack([three] + aside(3), order, grads, units)
    p_own = project([own], turn_in, query)
    a1, pieces, p_own = hold((a1, pieces, p_own))
    b1, b3, b2 = middle(a1), sideways(a1), inward(a2)
    p_a = project([a1] + a3, turn_in, query)
    total = score(p_own, 0, order, 0, grads, turn_out)
    ready = {one: back(p_a, 0, turn_out)}
    for j in range(1, across):
        ready[j] = back(p_a, j, turn_out)
    a2, b1, b2, b3, pieces, total, ready = hold((a2, b1, b2, b3, pieces, total, ready))
    c1 = inward(b1)
    far2 = jnp.where(inner, b1, b2)
    side2 = sideways(far2)
    got = send(pieces, [three] + aside(3))
    come = send(ready, aside(0))
    p_b = project([far2] + b3, turn_in, query)
    ready[two] = back(p_b, 0, turn_out)
    for j in range(1, across):
        ready[one + j] = back(p_b, j, turn_out)
    c1, side2, got, come, ready = hold((c1, side2, got, come, ready))
    far3 = jnp.where(inner, a2, c1)
    side3 = sideways(far3)
    come.update(send(ready, [two, one]))
    p_c = project([far3] + side2, turn_in, query)
    sums = {three: score(p_c, 0, order, None, got[three], turn_out)}
    for j in range(1, across):
        ready[two + j] = back(p_c, j, turn_out)
    total += meet({j: come[j] for j in aside(0)}, order, grads)
    side3, ready, total = hold((side3, ready, total))
    late = aside(2) + aside(1)
    come.update(send(ready, late))
    p_d = project(side3, turn_in, query)
    for j in range(1, across):
        sums[three + j] = score(p_d, j - 1, order, None, got[three + j], turn_out)
    for value in send(sums, list(sums)).values():
        total += value
    total += meet({j: come[j] for j in (two, one)}, order, grads)
    total, come = hold((total, come))
    total += meet({j: come[j] for j in late}, order, grads)
    return lax.psum(total[0], "layer")


def solution(mesh):
    placed = (
        P("layer", "seq", None),
        P("layer", "seq", None),
        P("layer", "seq", None),
        P("layer", None, None, None),
        P("layer", "seq", None, None),
        P("layer", None),
    )
    across = mesh.shape["seq"] // LINE
    return jax.shard_map(
        functools.partial(body, across), mesh=mesh, in_specs=placed, out_specs=P("seq"), check_vma=False
    )
```

time: 179 us -> 161 us (0.90)
  Pallas kernels: 36.5 us -> 64.5 us
  waiting for transfers between devices: 74.5 us -> 47.9 us
  blocking collectives: 16.8 us -> 6.17 us
  local copies, waits for them, and re-layouts: 17.3 us -> 7.88 us
  starting transfers between devices: 26.2 us -> 32.3 us
  between operations: 5.41 us -> 0.25 us
    pallas_call x5, Pallas kernels: 33.4 us -> 54.8 us  [project(): pl.pallas_call(functools.partial(project_kernel, count), grid=(units // s...]
    ppermute x12 -> x14, waiting for transfers between devices: 61.7 us -> 41.7 us  [swap(): return lax.ppermute(value, 'seq', [(s, s ^ j) for s in range(size)])]
    all_to_all x1 -> x0, blocking collectives: 10.6 us -> none  [body(): lax.all_to_all(partial, 'seq', split_axis=0, concat_axis=0, tiled=True)]
    pallas_call x8 -> x12, Pallas kernels: 3.04 us -> 9.71 us  [the longest x6 5.36 us: small(): pl.pallas_call(kernel, grid_spec=pltpu.PrefetchScalarGridSpec(num_scalar_...]
    ppermute x4, waiting for transfers between devices: 12.8 us -> 6.21 us  [move(): return lax.ppermute(value, 'seq', pairs)]
    ppermute x12 -> x14, starting transfers between devices: 20.4 us -> 26.4 us  [swap(): return lax.ppermute(value, 'seq', [(s, s ^ j) for s in range(size)])]
    unnamed x26 -> x22, local copies, waits for them, and re-layouts: 13.1 us -> 7.24 us
    dynamic_slice x2 -> x0, local copies, waits for them, and re-layouts: 3.3 us -> none  [the longest x1 1.66 us: body(): lax.dynamic_slice_in_dim(grads, owners[me ^ j] * units, units, axis=1)]
  transfers between devices with their start and end apart: 16 -> 18, of which waited for: 10 -> 9; matrix products, arithmetic and copies ran while one was open for 2% -> 0% of each run, Pallas kernels for 16% -> 40%
where the time goes in v3:
time: 161 us; the launch traced here: 160 us
  Pallas kernels  64.5 us (40%)
  waiting for transfers between devices  47.9 us (30%)
  starting transfers between devices  32.3 us (20%)
  local copies, waits for them, and re-layouts  7.88 us (5%)
  blocking collectives  6.17 us (4%)
    pallas_call x5, Pallas kernels, project(): pl.pallas_call(functools.partial(project_kernel, count), grid=(units // s...  54.8 us
    ppermute x14, waiting for transfers between devices, swap(): return lax.ppermute(value, 'seq', [(s, s ^ j) for s in range(size)])  41.7 us
    ppermute x14, starting transfers between devices, swap(): return lax.ppermute(value, 'seq', [(s, s ^ j) for s in range(size)])  26.4 us
    unnamed x22, local copies, waits for them, and re-layouts  7.24 us
    ppermute x4, waiting for transfers between devices, move(): return lax.ppermute(value, 'seq', pairs)  6.21 us
    psum x1, blocking collectives, body(): return lax.psum(total[0], 'layer')  6.17 us
    ppermute x4, starting transfers between devices, move(): return lax.ppermute(value, 'seq', pairs)  5.87 us
    pallas_call x6, Pallas kernels, small(): pl.pallas_call(kernel, grid_spec=pltpu.PrefetchScalarGridSpec(num_scalar_...  5.36 us
  transfers between devices with their start and end apart: 18, of which 9 were waited for; matrix products, arithmetic and copies ran while one was open for 0% of the time, Pallas kernels for 40%

profile of v3, /device:TPU:0, one launch (start us, length us, event | category | flops | bytes accessed | tf_op | source)
XLA Modules:
  0.0 160.4 jit_solution(1253136744100387437)
XLA Ops:
  0.0 3.0 %collective-permute-start.1 = (bf16[128,4096]{1,0:T(8,128)(2,1)}, bf16[128,4096]{1,0:T(8,128)(2,1)}, u32[]{:S(2)}, u32[]{:S(2)}) collective-permute-start(bf16[128,4096]{1,0:T(8,128)(2,1)} %bitcast.32), channel_id=1, source_target_pairs={{0,8},{4,12},{8,0},{12,4},{16,24},{20,28},{24,16},{28,20},{1,9},{5... | collective-permute-start | bytes 3145736 | tf_op jit(solution)/shard_map/ppermute | solution.py:175
  3.0 1.6 %collective-permute-start = (bf16[128,4096]{1,0:T(8,128)(2,1)}, bf16[128,4096]{1,0:T(8,128)(2,1)}, u32[]{:S(2)}, u32[]{:S(2)}) collective-permute-start(bf16[128,4096]{1,0:T(8,128)(2,1)} %bitcast.33), channel_id=1, source_target_pairs={{8,16},{12,20},{16,8},{20,12},{9,17},{13,21},{17,9},{21,13},{10,18... | collective-permute-start | bytes 3145736 | tf_op jit(solution)/shard_map/ppermute | solution.py:172
  4.7 1.5 collective-permute-start.5
  6.2 0.6 gather_fusion
  6.8 0.0 copy-start.1
  6.9 2.0 %copy-done.1 = bf16[1,128,14336]{2,1,0:T(8,128)(2,1)S(1)} copy-done((bf16[1,128,14336]{2,1,0:T(8,128)(2,1)S(1)}, bf16[1,128,14336]{2,1,0:T(8,128)(2,1)}, u32[]{:S(2)}) %copy-start.1) | copy-done | bytes 3670040
  8.9 0.6 shard_map.64
  9.5 0.7 copy-done.9
  10.3 0.2 copy-done.8
  10.4 10.3 %shard_map.65.found = f32[1,128,1792]{2,1,0:T(8,128)S(1)} custom-call(bf16[128,4096]{1,0:T(8,128)(2,1)S(1)} %bitcast.35, bf16[32,128,128]{2,1,0:T(8,128)(2,1)S(1)} %bitcast.27, bf16[1792,4096]{1,0:T(8,128)(2,1)} %bitcast.36), custom_call_target="tpu_custom_call" | custom-call | tf_op jit(solution)/shard_map/pallas_call | solution.py:43
  20.7 5.8 %collective-permute-done.1.refs_0_ = bf16[128,4096]{1,0:T(8,128)(2,1)} collective-permute-done((bf16[128,4096]{1,0:T(8,128)(2,1)}, bf16[128,4096]{1,0:T(8,128)(2,1)}, u32[]{:S(2)}, u32[]{:S(2)}) %collective-permute-start.1) | collective-permute-done | bytes 1048608 | tf_op jit(solution)/shard_map/ppermute | solution.py:175
  26.5 1.7 %collective-permute-start.2 = (bf16[128,4096]{1,0:T(8,128)(2,1)}, bf16[128,4096]{1,0:T(8,128)(2,1)}, u32[]{:S(2)}, u32[]{:S(2)}) collective-permute-start(bf16[128,4096]{1,0:T(8,128)(2,1)} %collective-permute-done.1.refs_0_), channel_id=1, source_target_pairs={{8,16},{12,20},{16,8},{20,12},{9,17},{13,21},{17,9},{21,13},{10,18... | collective-permute-start | bytes 3145736 | tf_op jit(solution)/shard_map/ppermute | solution.py:172
  28.2 1.7 %collective-permute-start.4 = (bf16[128,4096]{1,0:T(8,128)(2,1)}, bf16[128,4096]{1,0:T(8,128)(2,1)S(1)}, u32[]{:S(2)}, u32[]{:S(2)}) collective-permute-start(bf16[128,4096]{1,0:T(8,128)(2,1)} %collective-permute-done.1.refs_0_), channel_id=1, source_target_pairs={{0,4},{4,0},{8,12},{12,8},{16,20},{20,16},{24,28},{28,24},{1,5},{5... | collective-permute-start | bytes 3145736 | tf_op jit(solution)/shard_map/ppermute | solution.py:175
  29.8 0.0 collective-permute-done
  29.8 1.3 collective-permute-start.3
  31.1 0.0 copy-start.3
  31.1 0.0 collective-permute-done.5.refs_1_
  31.2 11.9 %shard_map.67.found = f32[2,128,1792]{2,1,0:T(8,128)} custom-call(bf16[128,4096]{1,0:T(8,128)(2,1)} %collective-permute-done.1.refs_0_, bf16[128,4096]{1,0:T(8,128)(2,1)} %collective-permute-done.5.refs_1_, bf16[32,128,128]{2,1,0:T(8,128)(2,1)S(1)} %bitcast.28, bf16[1792,4096]{1,0:T(8,128)(2,1)} %bitcast.37), custom_call_target="tpu_custom_call" | custom-call | tf_op jit(solution)/shard_map/pallas_call | solution.py:43
  43.0 1.5 copy-done.6
  44.5 0.7 shard_map.68
  45.3 0.8 shard_map.69
  46.0 0.5 copy-done.2
  46.5 0.9 shard_map.66
  47.5 0.0 collective-permute-done.2
  47.5 5.2 %collective-permute-done.4.refs_1_ = bf16[128,4096]{1,0:T(8,128)(2,1)S(1)} collective-permute-done((bf16[128,4096]{1,0:T(8,128)(2,1)}, bf16[128,4096]{1,0:T(8,128)(2,1)S(1)}, u32[]{:S(2)}, u32[]{:S(2)}) %collective-permute-start.4) | collective-permute-done | bytes 1048608 | tf_op jit(solution)/shard_map/ppermute | solution.py:175
  52.7 3.9 %collective-permute-done.3 = bf16[128,4096]{1,0:T(8,128)(2,1)} collective-permute-done((bf16[128,4096]{1,0:T(8,128)(2,1)}, bf16[128,4096]{1,0:T(8,128)(2,1)}, u32[]{:S(2)}, u32[]{:S(2)}) %collective-permute-start.3) | collective-permute-done | bytes 1048608 | tf_op jit(solution)/shard_map/ppermute | solution.py:172
  56.6 1.3 broadcast_select_fusion.1.refs_0_
  57.9 0.6 collective-permute-start.7
  58.5 1.3 collective-permute-start.6
  59.8 1.6 collective-permute-start.10
  61.4 2.8 %collective-permute-start.8 = (bf16[128,1792]{1,0:T(8,128)(2,1)S(1)}, bf16[128,1792]{1,0:T(8,128)(2,1)S(1)}, u32[]{:S(2)}, u32[]{:S(2)}) collective-permute-start(bf16[128,1792]{1,0:T(8,128)(2,1)S(1)} %copy-done.10), channel_id=1, source_target_pairs={{0,24},{4,28},{8,16},{12,20},{16,8},{20,12},{24,0},{28,4},{1,25},{... | collective-permute-start | bytes 1376264 | tf_op jit(solution)/shard_map/ppermute | solution.py:175
  64.2 1.0 collective-permute-start.9
  65.2 11.2 %shard_map.70.found = f32[2,128,1792]{2,1,0:T(8,128)} custom-call(bf16[128,4096]{1,0:T(8,128)(2,1)S(1)} %broadcast_select_fusion.1.refs_0_, bf16[128,4096]{1,0:T(8,128)(2,1)S(1)} %collective-permute-done.4.refs_1_, bf16[32,128,128]{2,1,0:T(8,128)(2,1)S(1)} %bitcast.29, bf16[1792,4096]{1,0:T(8,128)(2,1)} %bitcast.38), custom_call_target="tpu_custom_call" | custom-call | tf_op jit(solution)/shard_map/pallas_call | solution.py:43
  76.4 1.5 copy-done.7
  77.9 0.7 shard_map.71
  78.6 0.8 shard_map.72
  79.4 21.1 %collective-permute-done.10.refs_0_ = bf16[128,1792]{1,0:T(8,128)(2,1)S(1)} collective-permute-done((bf16[128,1792]{1,0:T(8,128)(2,1)S(1)}, bf16[128,1792]{1,0:T(8,128)(2,1)S(1)}, u32[]{:S(2)}, u32[]{:S(2)}) %collective-permute-start.10) | collective-permute-done | bytes 458784 | tf_op jit(solution)/shard_map/ppermute | solution.py:175
  100.5 0.0 collective-permute-done.8.piece
  100.5 0.0 collective-permute-done.9.piece
  100.5 0.0 collective-permute-done.7.refs_1_
  100.5 2.3 %collective-permute-done.6 = bf16[128,4096]{1,0:T(8,128)(2,1)S(1)} collective-permute-done((bf16[128,4096]{1,0:T(8,128)(2,1)}, bf16[128,4096]{1,0:T(8,128)(2,1)S(1)}, u32[]{:S(2)}, u32[]{:S(2)}) %collective-permute-start.6) | collective-permute-done | bytes 1048608 | tf_op jit(solution)/shard_map/ppermute | solution.py:172
  102.8 0.1 broadcast_select_fusion.refs_0_
  103.0 1.6 collective-permute-start.11
  104.5 2.5 %collective-permute-start.14 = (bf16[128,1792]{1,0:T(8,128)(2,1)S(1)}, bf16[128,1792]{1,0:T(8,128)(2,1)S(1)}, u32[]{:S(2)}, u32[]{:S(2)}) collective-permute-start(bf16[128,1792]{1,0:T(8,128)(2,1)S(1)} %shard_map.72), channel_id=1, source_target_pairs={{0,16},{4,20},{8,24},{12,28},{16,0},{20,4},{24,8},{28,12},{1,17},{... | collective-permute-start | bytes 1376264 | tf_op jit(solution)/shard_map/ppermute | solution.py:175
  107.1 0.8 collective-permute-start.15
  107.9 11.2 %shard_map.73.found = f32[2,128,1792]{2,1,0:T(8,128)} custom-call(bf16[128,4096]{1,0:T(8,128)(2,1)S(1)} %broadcast_select_fusion.refs_0_, bf16[128,4096]{1,0:T(8,128)(2,1)S(1)} %collective-permute-done.7.refs_1_, bf16[32,128,128]{2,1,0:T(8,128)(2,1)S(1)} %bitcast.30, bf16[1792,4096]{1,0:T(8,128)(2,1)} %bitcast.39), custom_call_target="tpu_custom_call" | custom-call | tf_op jit(solution)/shard_map/pallas_call | solution.py:43
  119.1 0.8 shard_map.75
  119.8 0.7 copy-done.5
  120.5 0.7 shard_map.74
  121.3 5.1 %collective-permute-done.11.refs_0_ = bf16[128,4096]{1,0:T(8,128)(2,1)S(1)} collective-permute-done((bf16[128,4096]{1,0:T(8,128)(2,1)S(1)}, bf16[128,4096]{1,0:T(8,128)(2,1)S(1)}, u32[]{:S(2)}, u32[]{:S(2)}) %collective-permute-start.11) | collective-permute-done | bytes 1048608 | tf_op jit(solution)/shard_map/ppermute | solution.py:175
  126.4 3.8 %collective-permute-start.16 = (bf16[128,1792]{1,0:T(8,128)(2,1)S(1)}, bf16[128,1792]{1,0:T(8,128)(2,1)S(1)}, u32[]{:S(2)}, u32[]{:S(2)}) collective-permute-start(bf16[128,1792]{1,0:T(8,128)(2,1)S(1)} %shard_map.71), channel_id=1, source_target_pairs={{0,12},{4,8},{8,4},{12,0},{16,28},{20,24},{24,20},{28,16},{1,13},{... | collective-permute-start | bytes 1376264 | tf_op jit(solution)/shard_map/ppermute | solution.py:175
  130.3 1.3 collective-permute-start.17
  131.6 0.9 shard_map.76
  132.5 1.5 collective-permute-start.12
  134.0 10.3 %shard_map.77.found = f32[1,128,1792]{2,1,0:T(8,128)S(1)} custom-call(bf16[128,4096]{1,0:T(8,128)(2,1)S(1)} %collective-permute-done.11.refs_0_, bf16[32,128,128]{2,1,0:T(8,128)(2,1)S(1)} %bitcast.31, bf16[1792,4096]{1,0:T(8,128)(2,1)} %bitcast.40), custom_call_target="tpu_custom_call" | custom-call | tf_op jit(solution)/shard_map/pallas_call | solution.py:43
  144.3 0.9 shard_map.78
  145.2 2.7 %collective-permute-start.13 = (f32[1,128]{1,0:T(1,128)S(1)}, f32[1,128]{1,0:T(1,128)S(1)}, u32[]{:S(2)}, u32[]{:S(2)}) collective-permute-start(f32[1,128]{1,0:T(1,128)S(1)} %shard_map.78), channel_id=1, source_target_pairs={{0,28},{4,24},{8,20},{12,16},{16,12},{20,8},{24,4},{28,0},{1,29},{... | collective-permute-start | bytes 1544 | tf_op jit(solution)/shard_map/ppermute | solution.py:175
  147.9 0.9 shard_map.79
  148.8 3.6 %collective-permute-done.12 = f32[1,128]{1,0:T(1,128)S(1)} collective-permute-done((f32[1,128]{1,0:T(1,128)S(1)}, f32[1,128]{1,0:T(1,128)S(1)}, u32[]{:S(2)}, u32[]{:S(2)}) %collective-permute-start.12) | collective-permute-done | bytes 544 | tf_op jit(solution)/shard_map/ppermute | solution.py:175
  152.4 0.1 collective-permute-done.13
  152.5 0.0 collective-permute-done.16.refs_1_
  152.5 0.8 collective-permute-done.17.refs_0_
  153.3 0.9 shard_map.80
  154.2 6.2 %psum.7 = f32[128]{0:T(128)} all-reduce(f32[128]{0:T(128)S(1)} %add_bitcast_fusion), channel_id=1, replica_groups=mesh['seq'=8,'layer'=4] {'layer'}, use_global_device_ids=true, to_apply=%region_0.1 | all-reduce | flops 128 | bytes 1024 | tf_op jit(solution)/shard_map/psum | solution.py:227
  (21 shorter events, 0.1 us)
Async XLA Ops:
  0.0 6.2 %copy-start = (s32[1,8]{1,0:T(1,128)S(1)}, s32[1,8]{1,0:T(1,128)}, u32[]{:S(2)}) copy-start(s32[1,8]{1,0:T(1,128)} %param.11) | copy-start | bytes 100
  0.0 26.5 %collective-permute-start.1 = (bf16[128,4096]{1,0:T(8,128)(2,1)}, bf16[128,4096]{1,0:T(8,128)(2,1)}, u32[]{:S(2)}, u32[]{:S(2)}) collective-permute-start(bf16[128,4096]{1,0:T(8,128)(2,1)} %bitcast.32), channel_id=1, source_target_pairs={{0,8},{4,12},{8,0},{12,4},{16,24},{20,28},{24,16},{28,20},{1,9},{5... | collective-permute-start | bytes 3145736 | tf_op jit(solution)/shard_map/ppermute | solution.py:175
  3.0 26.8 %collective-permute-start = (bf16[128,4096]{1,0:T(8,128)(2,1)}, bf16[128,4096]{1,0:T(8,128)(2,1)}, u32[]{:S(2)}, u32[]{:S(2)}) collective-permute-start(bf16[128,4096]{1,0:T(8,128)(2,1)} %bitcast.33), channel_id=1, source_target_pairs={{8,16},{12,20},{16,8},{20,12},{9,17},{13,21},{17,9},{21,13},{10,18... | collective-permute-start | bytes 3145736 | tf_op jit(solution)/shard_map/ppermute | solution.py:172
  4.7 26.5 %collective-permute-start.5 = (bf16[128,4096]{1,0:T(8,128)(2,1)}, bf16[128,4096]{1,0:T(8,128)(2,1)}, u32[]{:S(2)}, u32[]{:S(2)}) collective-permute-start(bf16[128,4096]{1,0:T(8,128)(2,1)} %bitcast.34), channel_id=1, source_target_pairs={{0,4},{4,0},{8,12},{12,8},{16,20},{20,16},{24,28},{28,24},{1,5},{5... | collective-permute-start | bytes 3145736 | tf_op jit(solution)/shard_map/ppermute | solution.py:175
  6.8 2.0 %copy-start.1 = (bf16[1,128,14336]{2,1,0:T(8,128)(2,1)S(1)}, bf16[1,128,14336]{2,1,0:T(8,128)(2,1)}, u32[]{:S(2)}) copy-start(bf16[1,128,14336]{2,1,0:T(8,128)(2,1)} %param.7) | copy-start | bytes 11010052
  8.9 1.4 copy-start.4
  8.9 1.5 copy-start.8
  9.5 0.8 copy-start.9
  26.5 21.0 %collective-permute-start.2 = (bf16[128,4096]{1,0:T(8,128)(2,1)}, bf16[128,4096]{1,0:T(8,128)(2,1)}, u32[]{:S(2)}, u32[]{:S(2)}) collective-permute-start(bf16[128,4096]{1,0:T(8,128)(2,1)} %collective-permute-done.1.refs_0_), channel_id=1, source_target_pairs={{8,16},{12,20},{16,8},{20,12},{9,17},{13,21},{17,9},{21,13},{10,18... | collective-permute-start | bytes 3145736 | tf_op jit(solution)/shard_map/ppermute | solution.py:172
  28.2 24.6 %collective-permute-start.4 = (bf16[128,4096]{1,0:T(8,128)(2,1)}, bf16[128,4096]{1,0:T(8,128)(2,1)S(1)}, u32[]{:S(2)}, u32[]{:S(2)}) collective-permute-start(bf16[128,4096]{1,0:T(8,128)(2,1)} %collective-permute-done.1.refs_0_), channel_id=1, source_target_pairs={{0,4},{4,0},{8,12},{12,8},{16,20},{20,16},{24,28},{28,24},{1,5},{5... | collective-permute-start | bytes 3145736 | tf_op jit(solution)/shard_map/ppermute | solution.py:175
  29.8 26.8 %collective-permute-start.3 = (bf16[128,4096]{1,0:T(8,128)(2,1)}, bf16[128,4096]{1,0:T(8,128)(2,1)}, u32[]{:S(2)}, u32[]{:S(2)}) collective-permute-start(bf16[128,4096]{1,0:T(8,128)(2,1)} %collective-permute-done), channel_id=1, source_target_pairs={{8,0},{12,4},{16,24},{20,28},{9,1},{13,5},{17,25},{21,29},{10,2},{... | collective-permute-start | bytes 3145736 | tf_op jit(solution)/shard_map/ppermute | solution.py:172
  31.1 11.9 %copy-start.3 = (bf16[1,14,128,128]{3,2,1,0:T(8,128)(2,1)S(1)}, bf16[1,14,128,128]{3,2,1,0:T(8,128)(2,1)}, u32[]{:S(2)}) copy-start(bf16[1,14,128,128]{3,2,1,0:T(8,128)(2,1)} %param.10) | copy-start | bytes 1376260
  43.0 1.5 copy-start.6
  44.5 2.0 %copy-start.2 = (bf16[1,128,14336]{2,1,0:T(8,128)(2,1)S(1)}, bf16[1,128,14336]{2,1,0:T(8,128)(2,1)}, u32[]{:S(2)}) copy-start(bf16[1,128,14336]{2,1,0:T(8,128)(2,1)} %param.7) | copy-start | bytes 11010052
  47.5 13.9 %copy-start.10 = (bf16[128,1792]{1,0:T(8,128)(2,1)S(1)}, bf16[128,1792]{1,0:T(8,128)(2,1)}, u32[]{:S(2)}) copy-start(bf16[128,1792]{1,0:T(8,128)(2,1)} %copy-done.9) | copy-start | bytes 1376260
  57.9 42.6 %collective-permute-start.7 = (bf16[128,4096]{1,0:T(8,128)(2,1)S(1)}, bf16[128,4096]{1,0:T(8,128)(2,1)S(1)}, u32[]{:S(2)}, u32[]{:S(2)}) collective-permute-start(bf16[128,4096]{1,0:T(8,128)(2,1)S(1)} %broadcast_select_fusion.1.refs_0_), channel_id=1, source_target_pairs={{0,4},{4,0},{8,12},{12,8},{16,20},{20,16},{24,28},{28,24},{1,5},{5... | collective-permute-start | bytes 3145736 | tf_op jit(solution)/shard_map/ppermute | solution.py:175
  58.5 44.3 %collective-permute-start.6 = (bf16[128,4096]{1,0:T(8,128)(2,1)}, bf16[128,4096]{1,0:T(8,128)(2,1)S(1)}, u32[]{:S(2)}, u32[]{:S(2)}) collective-permute-start(bf16[128,4096]{1,0:T(8,128)(2,1)} %collective-permute-done.2), channel_id=1, source_target_pairs={{8,0},{12,4},{16,24},{20,28},{9,1},{13,5},{17,25},{21,29},{10,2},{... | collective-permute-start | bytes 3145736 | tf_op jit(solution)/shard_map/ppermute | solution.py:172
  59.8 40.7 %collective-permute-start.10 = (bf16[128,1792]{1,0:T(8,128)(2,1)S(1)}, bf16[128,1792]{1,0:T(8,128)(2,1)S(1)}, u32[]{:S(2)}, u32[]{:S(2)}) collective-permute-start(bf16[128,1792]{1,0:T(8,128)(2,1)S(1)} %shard_map.68), channel_id=1, source_target_pairs={{0,4},{4,0},{8,12},{12,8},{16,20},{20,16},{24,28},{28,24},{1,5},{5... | collective-permute-start | bytes 1376264 | tf_op jit(solution)/shard_map/ppermute | solution.py:175
  61.4 39.1 %collective-permute-start.8 = (bf16[128,1792]{1,0:T(8,128)(2,1)S(1)}, bf16[128,1792]{1,0:T(8,128)(2,1)S(1)}, u32[]{:S(2)}, u32[]{:S(2)}) collective-permute-start(bf16[128,1792]{1,0:T(8,128)(2,1)S(1)} %copy-done.10), channel_id=1, source_target_pairs={{0,24},{4,28},{8,16},{12,20},{16,8},{20,12},{24,0},{28,4},{1,25},{... | collective-permute-start | bytes 1376264 | tf_op jit(solution)/shard_map/ppermute | solution.py:175
  64.2 36.3 %collective-permute-start.9 = (bf16[128,1792]{1,0:T(8,128)(2,1)S(1)}, bf16[128,1792]{1,0:T(8,128)(2,1)S(1)}, u32[]{:S(2)}, u32[]{:S(2)}) collective-permute-start(bf16[128,1792]{1,0:T(8,128)(2,1)S(1)} %get-tuple-element.45), channel_id=1, source_target_pairs={{0,28},{4,24},{8,20},{12,16},{16,12},{20,8},{24,4},{28,0},{1,29},{... | collective-permute-start | bytes 1376264 | tf_op jit(solution)/shard_map/ppermute | solution.py:175
  76.4 1.5 copy-start.7
  103.0 23.5 %collective-permute-start.11 = (bf16[128,4096]{1,0:T(8,128)(2,1)S(1)}, bf16[128,4096]{1,0:T(8,128)(2,1)S(1)}, u32[]{:S(2)}, u32[]{:S(2)}) collective-permute-start(bf16[128,4096]{1,0:T(8,128)(2,1)S(1)} %broadcast_select_fusion.refs_0_), channel_id=1, source_target_pairs={{0,4},{4,0},{8,12},{12,8},{16,20},{20,16},{24,28},{28,24},{1,5},{5... | collective-permute-start | bytes 3145736 | tf_op jit(solution)/shard_map/ppermute | solution.py:175
  104.5 40.7 %collective-permute-start.14 = (bf16[128,1792]{1,0:T(8,128)(2,1)S(1)}, bf16[128,1792]{1,0:T(8,128)(2,1)S(1)}, u32[]{:S(2)}, u32[]{:S(2)}) collective-permute-start(bf16[128,1792]{1,0:T(8,128)(2,1)S(1)} %shard_map.72), channel_id=1, source_target_pairs={{0,16},{4,20},{8,24},{12,28},{16,0},{20,4},{24,8},{28,12},{1,17},{... | collective-permute-start | bytes 1376264 | tf_op jit(solution)/shard_map/ppermute | solution.py:175
  107.1 40.9 %collective-permute-start.15 = (bf16[128,1792]{1,0:T(8,128)(2,1)S(1)}, bf16[128,1792]{1,0:T(8,128)(2,1)S(1)}, u32[]{:S(2)}, u32[]{:S(2)}) collective-permute-start(bf16[128,1792]{1,0:T(8,128)(2,1)S(1)} %shard_map.69), channel_id=1, source_target_pairs={{0,8},{4,12},{8,0},{12,4},{16,24},{20,28},{24,16},{28,20},{1,9},{5... | collective-permute-start | bytes 1376264 | tf_op jit(solution)/shard_map/ppermute | solution.py:175
  119.0 1.5 copy-start.5
  126.4 26.1 %collective-permute-start.16 = (bf16[128,1792]{1,0:T(8,128)(2,1)S(1)}, bf16[128,1792]{1,0:T(8,128)(2,1)S(1)}, u32[]{:S(2)}, u32[]{:S(2)}) collective-permute-start(bf16[128,1792]{1,0:T(8,128)(2,1)S(1)} %shard_map.71), channel_id=1, source_target_pairs={{0,12},{4,8},{8,4},{12,0},{16,28},{20,24},{24,20},{28,16},{1,13},{... | collective-permute-start | bytes 1376264 | tf_op jit(solution)/shard_map/ppermute | solution.py:175
  130.3 23.0 %collective-permute-start.17 = (bf16[128,1792]{1,0:T(8,128)(2,1)S(1)}, bf16[128,1792]{1,0:T(8,128)(2,1)S(1)}, u32[]{:S(2)}, u32[]{:S(2)}) collective-permute-start(bf16[128,1792]{1,0:T(8,128)(2,1)S(1)} %shard_map.74), channel_id=1, source_target_pairs={{0,20},{4,16},{8,28},{12,24},{16,4},{20,0},{24,12},{28,8},{1,21},{... | collective-permute-start | bytes 1376264 | tf_op jit(solution)/shard_map/ppermute | solution.py:175
  132.5 19.9 %collective-permute-start.12 = (f32[1,128]{1,0:T(1,128)S(1)}, f32[1,128]{1,0:T(1,128)S(1)}, u32[]{:S(2)}, u32[]{:S(2)}) collective-permute-start(f32[1,128]{1,0:T(1,128)S(1)} %shard_map.76), channel_id=1, source_target_pairs={{0,24},{4,28},{8,16},{12,20},{16,8},{20,12},{24,0},{28,4},{1,25},{... | collective-permute-start | bytes 1544 | tf_op jit(solution)/shard_map/ppermute | solution.py:175
  145.2 7.3 %collective-permute-start.13 = (f32[1,128]{1,0:T(1,128)S(1)}, f32[1,128]{1,0:T(1,128)S(1)}, u32[]{:S(2)}, u32[]{:S(2)}) collective-permute-start(f32[1,128]{1,0:T(1,128)S(1)} %shard_map.78), channel_id=1, source_target_pairs={{0,28},{4,24},{8,20},{12,16},{16,12},{20,8},{24,4},{28,0},{1,29},{... | collective-permute-start | bytes 1544 | tf_op jit(solution)/shard_map/ppermute | solution.py:175

commit v4 on v3

--- a/solution.py
+++ b/solution.py
@@ -47,7 +47,7 @@
         out_specs=pl.BlockSpec((count, rows, step), lambda i: (0, 0, i)),
         out_shape=jax.ShapeDtypeStruct((count, rows, units), jnp.float32),
         scratch_shapes=[pltpu.VMEM((count * rows, wide), jnp.bfloat16)],
-        compiler_params=pltpu.CompilerParams(vmem_limit_bytes=50 * MIB),
+        compiler_params=pltpu.CompilerParams(vmem_limit_bytes=20 * MIB),
         cost_estimate=free,
     )(*chunks, basis, query)
 
@@ -155,6 +155,47 @@
     )(found, basis)
 
 
+def project_score_kernel(chunk, basis, query, piece, turn, out, turned, total):
+    @pl.when(pl.program_id(0) == 0)
+    def _():
+        for n, part in enumerate(blocks_of(chunk.shape[1])):
+            turned[:, part] = jnp.dot(chunk[:, part], basis[n], preferred_element_type=jnp.float32).astype(jnp.bfloat16)
+        total[...] = jnp.zeros_like(total)
+
+    found = lax.dot_general(turned[...], query[...], NT, preferred_element_type=jnp.float32)
+    for n in range(turn.shape[0]):
+        part = slice(n * TILE, (n + 1) * TILE)
+        held = jnp.dot(piece[:, part], turn[n], preferred_element_type=jnp.float32).astype(jnp.bfloat16)
+        total[...] += held.astype(jnp.float32) * found[:, part]
+
+    @pl.when(pl.program_id(0) == pl.num_programs(0) - 1)
+    def _():
+        out[...] = lay(total[...])
+
+
+def project_score(chunk, basis, query, piece, turn):
+    rows, wide = chunk.shape
+    units = query.shape[0]
+    step = 2 * TILE if units % (2 * TILE) == 0 else TILE
+    whole = lambda *shape: pl.BlockSpec(shape, lambda i: (0,) * len(shape))
+    return pl.pallas_call(
+        project_score_kernel,
+        grid=(units // step,),
+        in_specs=[
+            whole(rows, wide),
+            whole(*basis.shape),
+            pl.BlockSpec((step, wide), lambda i: (i, 0)),
+            pl.BlockSpec((rows, step), lambda i: (0, i)),
+            pl.BlockSpec((step // TILE, *turn.shape[1:]), lambda i: (i, 0, 0)),
+        ],
+        out_specs=whole(1, rows),
+        out_shape=jax.ShapeDtypeStruct((1, rows), jnp.float32),
+        scratch_shapes=[pltpu.VMEM((rows, wide), jnp.bfloat16), pltpu.VMEM((rows, TILE), jnp.float32)],
+        compiler_params=pltpu.CompilerParams(vmem_limit_bytes=20 * MIB),
+        cost_estimate=free,
+    )(chunk, basis, query, piece, turn)
+
+
 def body(across, train_inputs, out_grads, query_blocks, basis_in, basis_out, block_of):
     own, grads, query = train_inputs[0], out_grads[0], query_blocks[0]
     turn_in, turn_out, owners = basis_in[0], basis_out[0], block_of[0]
@@ -178,7 +219,6 @@
         return [swap(value, j) for j in range(1, across)]
 
     middle = lambda value: move(value, lambda z, x: (3 - z, x) if z in (1, 2) else None)
-    inward = lambda value: move(value, lambda z, x: (z ^ 1, x) if z in (1, 2) else None)
     line = lambda value, d: swap(value, d * across)
     send = lambda values, js: {j: swap(values[j], j) for j in js}
     aside = lambda d: [d * across + j for j in range(1, across)]
@@ -188,17 +228,18 @@
     pieces = pack([three] + aside(3), order, grads, units)
     p_own = project([own], turn_in, query)
     a1, pieces, p_own = hold((a1, pieces, p_own))
-    b1, b3, b2 = middle(a1), sideways(a1), inward(a2)
+    got = send(pieces, aside(3))
+    b1, b3, b2 = middle(a1), sideways(a1), line(a2, 1)
     p_a = project([a1] + a3, turn_in, query)
     total = score(p_own, 0, order, 0, grads, turn_out)
     ready = {one: back(p_a, 0, turn_out)}
     for j in range(1, across):
         ready[j] = back(p_a, j, turn_out)
     a2, b1, b2, b3, pieces, total, ready = hold((a2, b1, b2, b3, pieces, total, ready))
-    c1 = inward(b1)
+    c1 = line(b1, 1)
     far2 = jnp.where(inner, b1, b2)
     side2 = sideways(far2)
-    got = send(pieces, [three] + aside(3))
+    got.update(send(pieces, [three]))
     come = send(ready, aside(0))
     p_b = project([far2] + b3, turn_in, query)
     ready[two] = back(p_b, 0, turn_out)
@@ -213,18 +254,25 @@
     for j in range(1, across):
         ready[two + j] = back(p_c, j, turn_out)
     total += meet({j: come[j] for j in aside(0)}, order, grads)
-    side3, ready, total = hold((side3, ready, total))
+    sums = send(sums, list(sums))
+    side3, ready, total, sums = hold((side3, ready, total, sums))
+    total += sums[three]
+    sums = {}
     late = aside(2) + aside(1)
     come.update(send(ready, late))
-    p_d = project(side3, turn_in, query)
-    for j in range(1, across):
-        sums[three + j] = score(p_d, j - 1, order, None, got[three + j], turn_out)
+    for j in range(1, across):
+        sums[three + j] = project_score(side3[j - 1], turn_in, query, got[three + j], turn_out)
     for value in send(sums, list(sums)).values():
         total += value
     total += meet({j: come[j] for j in (two, one)}, order, grads)
     total, come = hold((total, come))
     total += meet({j: come[j] for j in late}, order, grads)
-    return lax.psum(total[0], "layer")
+    mine, layers = total[0], lax.axis_size("layer")
+    if layers & (layers - 1) or layers > 4:
+        return lax.psum(mine, "layer")
+    for j in range(1, layers):
+        total += lax.ppermute(mine, "layer", [(s, s ^ j) for s in range(layers)])
+    return total[0]
 
 
 def solution(mesh):

time: 161 us -> 153 us (0.950)
  Pallas kernels: 64.5 us -> 41.6 us
  waiting for transfers between devices: 47.9 us -> 60.1 us
  local copies, waits for them, and re-layouts: 7.88 us -> 14.5 us
  blocking collectives: 6.17 us -> 0 us
  starting transfers between devices: 32.3 us -> 34.3 us
    pallas_call x5 -> x4, Pallas kernels: 54.8 us -> 26.1 us  [project(): pl.pallas_call(functools.partial(project_kernel, count), grid=(units // s...]
    ppermute x14 -> x16, waiting for transfers between devices: 41.7 us -> 57.4 us  [swap(): return lax.ppermute(value, 'seq', [(s, s ^ j) for s in range(size)])]
    pallas_call x0 -> x1, Pallas kernels: none -> 6.66 us  [project_score(): pl.pallas_call(project_score_kernel, grid=(units // step,), in_specs=[who...]
    unnamed x22 -> x28, local copies, waits for them, and re-layouts: 7.24 us -> 13.8 us
    ppermute x4 -> x2, waiting for transfers between devices: 6.21 us -> 0.01 us  [move(): return lax.ppermute(value, 'seq', pairs)]
    psum x1 -> x0, blocking collectives: 6.17 us -> none  [body(): return lax.psum(total[0], 'layer')]
    ppermute x0 -> x3, waiting for transfers between devices: none -> 2.69 us  [body(): total += lax.ppermute(mine, 'layer', [(s, s ^ j) for s in range(layers)])]
    ppermute x14 -> x16, starting transfers between devices: 26.4 us -> 29.1 us  [swap(): return lax.ppermute(value, 'seq', [(s, s ^ j) for s in range(size)])]
  transfers between devices with their start and end apart: 18 -> 21, of which waited for: 9 -> 11; matrix products, arithmetic and copies ran while one was open for 0% -> 0% of each run, Pallas kernels for 40% -> 27%
where the time goes in v4:
time: 153 us
  waiting for transfers between devices  60.1 us (39%)
  Pallas kernels  41.6 us (27%)
  starting transfers between devices  34.3 us (22%)
  local copies, waits for them, and re-layouts  14.5 us (9%)
  other arithmetic  2.01 us (1%)
    ppermute x16, waiting for transfers between devices, swap(): return lax.ppermute(value, 'seq', [(s, s ^ j) for s in range(size)])  57.4 us
    ppermute x16, starting transfers between devices, swap(): return lax.ppermute(value, 'seq', [(s, s ^ j) for s in range(size)])  29.1 us
    pallas_call x4, Pallas kernels, project(): pl.pallas_call(functools.partial(project_kernel, count), grid=(units // s...  26.1 us
    unnamed x28, local copies, waits for them, and re-layouts  13.8 us
    pallas_call x1, Pallas kernels, project_score(): pl.pallas_call(project_score_kernel, grid=(units // step,), in_specs=[who...  6.66 us
    pallas_call x5, Pallas kernels, small(): pl.pallas_call(kernel, grid_spec=pltpu.PrefetchScalarGridSpec(num_scalar_...  4.45 us
    pallas_call x5, Pallas kernels, back(): pl.pallas_call(back_kernel, grid=(1,), in_specs=[pl.BlockSpec((None, rows...  3.74 us
    ppermute x2, starting transfers between devices, move(): return lax.ppermute(value, 'seq', pairs)  3.28 us
  transfers between devices with their start and end apart: 21, of which 11 were waited for; matrix products, arithmetic and copies ran while one was open for 0% of the time, Pallas kernels for 27%

profile of v4, /device:TPU:0, one launch (start us, length us, event | category | flops | bytes accessed | tf_op | source)
XLA Modules:
  0.0 152.6 jit_solution(15212876160565930003)
XLA Ops:
  0.0 3.0 %collective-permute-start.1 = (bf16[128,4096]{1,0:T(8,128)(2,1)}, bf16[128,4096]{1,0:T(8,128)(2,1)}, u32[]{:S(2)}, u32[]{:S(2)}) collective-permute-start(bf16[128,4096]{1,0:T(8,128)(2,1)} %bitcast.52), channel_id=1, source_target_pairs={{0,8},{4,12},{8,0},{12,4},{16,24},{20,28},{24,16},{28,20},{1,9},{5... | collective-permute-start | bytes 3145736 | tf_op jit(solution)/shard_map/ppermute | solution.py:216
  3.0 1.6 %collective-permute-start = (bf16[128,4096]{1,0:T(8,128)(2,1)}, bf16[128,4096]{1,0:T(8,128)(2,1)}, u32[]{:S(2)}, u32[]{:S(2)}) collective-permute-start(bf16[128,4096]{1,0:T(8,128)(2,1)} %bitcast.53), channel_id=1, source_target_pairs={{8,16},{12,20},{16,8},{20,12},{9,17},{13,21},{17,9},{21,13},{10,18... | collective-permute-start | bytes 3145736 | tf_op jit(solution)/shard_map/ppermute | solution.py:213
  4.7 1.5 collective-permute-start.5
  6.2 0.6 gather_fusion
  6.8 0.0 copy-start.3
  6.8 2.0 %copy-done.3 = bf16[1,128,14336]{2,1,0:T(8,128)(2,1)S(1)} copy-done((bf16[1,128,14336]{2,1,0:T(8,128)(2,1)S(1)}, bf16[1,128,14336]{2,1,0:T(8,128)(2,1)}, u32[]{:S(2)}) %copy-start.3) | copy-done | bytes 3670040
  8.9 0.6 shard_map.64
  9.5 0.8 copy-done.8
  10.3 0.2 copy-done.7
  10.4 5.2 %copy-done.1 = bf16[1,1792,4096]{2,1,0:T(8,128)(2,1)S(1)} copy-done((bf16[1,1792,4096]{2,1,0:T(8,128)(2,1)S(1)}, bf16[1,1792,4096]{2,1,0:T(8,128)(2,1)}, u32[]{:S(2)}) %copy-start.1) | copy-done | bytes 14680088
  15.6 6.3 %shard_map.65.found = f32[1,128,1792]{2,1,0:T(8,128)S(1)} custom-call(bf16[128,4096]{1,0:T(8,128)(2,1)S(1)} %bitcast.55, bf16[32,128,128]{2,1,0:T(8,128)(2,1)S(1)} %bitcast.47, bf16[1792,4096]{1,0:T(8,128)(2,1)S(1)} %bitcast.24), custom_call_target="tpu_custom_call" | custom-call | tf_op jit(solution)/shard_map/pallas_call | solution.py:43
  21.9 4.6 %collective-permute-done.1.refs_0_ = bf16[128,4096]{1,0:T(8,128)(2,1)} collective-permute-done((bf16[128,4096]{1,0:T(8,128)(2,1)}, bf16[128,4096]{1,0:T(8,128)(2,1)}, u32[]{:S(2)}, u32[]{:S(2)}) %collective-permute-start.1) | collective-permute-done | bytes 1048608 | tf_op jit(solution)/shard_map/ppermute | solution.py:216
  26.5 1.6 %collective-permute-start.2 = (bf16[128,4096]{1,0:T(8,128)(2,1)}, bf16[128,4096]{1,0:T(8,128)(2,1)}, u32[]{:S(2)}, u32[]{:S(2)}) collective-permute-start(bf16[128,4096]{1,0:T(8,128)(2,1)} %collective-permute-done.1.refs_0_), channel_id=1, source_target_pairs={{8,16},{12,20},{16,8},{20,12},{9,17},{13,21},{17,9},{21,13},{10,18... | collective-permute-start | bytes 3145736 | tf_op jit(solution)/shard_map/ppermute | solution.py:213
  28.1 1.7 %collective-permute-start.4 = (bf16[128,4096]{1,0:T(8,128)(2,1)}, bf16[128,4096]{1,0:T(8,128)(2,1)S(1)}, u32[]{:S(2)}, u32[]{:S(2)}) collective-permute-start(bf16[128,4096]{1,0:T(8,128)(2,1)} %collective-permute-done.1.refs_0_), channel_id=1, source_target_pairs={{0,4},{4,0},{8,12},{12,8},{16,20},{20,16},{24,28},{28,24},{1,5},{5... | collective-permute-start | bytes 3145736 | tf_op jit(solution)/shard_map/ppermute | solution.py:216
  29.8 0.0 collective-permute-done
  29.8 3.5 %collective-permute-start.3 = (bf16[128,4096]{1,0:T(8,128)(2,1)}, bf16[128,4096]{1,0:T(8,128)(2,1)}, u32[]{:S(2)}, u32[]{:S(2)}) collective-permute-start(bf16[128,4096]{1,0:T(8,128)(2,1)} %collective-permute-done), channel_id=1, source_target_pairs={{0,8},{4,12},{8,0},{12,4},{16,24},{20,28},{24,16},{28,20},{1,9},{5... | collective-permute-start | bytes 3145736 | tf_op jit(solution)/shard_map/ppermute | solution.py:216
  33.3 0.0 collective-permute-done.5.refs_1_
  33.3 5.2 %copy-done.2 = bf16[1,1792,4096]{2,1,0:T(8,128)(2,1)S(1)} copy-done((bf16[1,1792,4096]{2,1,0:T(8,128)(2,1)S(1)}, bf16[1,1792,4096]{2,1,0:T(8,128)(2,1)}, u32[]{:S(2)}) %copy-start.2) | copy-done | bytes 14680088
  38.5 7.8 %shard_map.67.found = f32[2,128,1792]{2,1,0:T(8,128)S(1)} custom-call(bf16[128,4096]{1,0:T(8,128)(2,1)} %collective-permute-done.1.refs_0_, bf16[128,4096]{1,0:T(8,128)(2,1)} %collective-permute-done.5.refs_1_, bf16[32,128,128]{2,1,0:T(8,128)(2,1)S(1)} %bitcast.48, bf16[1792,4096]{1,0:T(8,128)(2,1)S(1)} %bitcast.25), custom_call_target="tpu_custom_call" | custom-call | tf_op jit(solution)/shard_map/pallas_call | solution.py:43
  46.3 0.0 copy-start.4
  46.3 0.7 shard_map.68
  47.0 0.0 slice-start.3
  47.0 0.7 shard_map.69
  47.8 0.5 copy-done.4
  48.3 0.9 shard_map.66
  49.2 3.5 %collective-permute-done.4.refs_1_ = bf16[128,4096]{1,0:T(8,128)(2,1)S(1)} collective-permute-done((bf16[128,4096]{1,0:T(8,128)(2,1)}, bf16[128,4096]{1,0:T(8,128)(2,1)S(1)}, u32[]{:S(2)}, u32[]{:S(2)}) %collective-permute-start.4) | collective-permute-done | bytes 1048608 | tf_op jit(solution)/shard_map/ppermute | solution.py:216
  52.7 2.6 %collective-permute-done.3 = bf16[128,4096]{1,0:T(8,128)(2,1)} collective-permute-done((bf16[128,4096]{1,0:T(8,128)(2,1)}, bf16[128,4096]{1,0:T(8,128)(2,1)}, u32[]{:S(2)}, u32[]{:S(2)}) %collective-permute-start.3) | collective-permute-done | bytes 1048608 | tf_op jit(solution)/shard_map/ppermute | solution.py:216
  55.3 1.3 broadcast_select_fusion.1.refs_0_
  56.7 0.6 collective-permute-start.7
  57.3 1.7 %collective-permute-start.6 = (bf16[128,4096]{1,0:T(8,128)(2,1)}, bf16[128,4096]{1,0:T(8,128)(2,1)S(1)}, u32[]{:S(2)}, u32[]{:S(2)}) collective-permute-start(bf16[128,4096]{1,0:T(8,128)(2,1)} %collective-permute-done.2), channel_id=1, source_target_pairs={{0,8},{4,12},{8,0},{12,4},{16,24},{20,28},{24,16},{28,20},{1,9},{5... | collective-permute-start | bytes 3145736 | tf_op jit(solution)/shard_map/ppermute | solution.py:216
  59.0 2.3 %collective-permute-start.9 = (bf16[128,1792]{1,0:T(8,128)(2,1)S(1)}, bf16[128,1792]{1,0:T(8,128)(2,1)S(1)}, u32[]{:S(2)}, u32[]{:S(2)}) collective-permute-start(bf16[128,1792]{1,0:T(8,128)(2,1)S(1)} %copy-done.9), channel_id=1, source_target_pairs={{0,28},{4,24},{8,20},{12,16},{16,12},{20,8},{24,4},{28,0},{1,29},{... | collective-permute-start | bytes 1376264 | tf_op jit(solution)/shard_map/ppermute | solution.py:216
  61.3 1.0 collective-permute-start.10
  62.3 2.0 %collective-permute-start.8 = (bf16[128,1792]{1,0:T(8,128)(2,1)S(1)}, bf16[128,1792]{1,0:T(8,128)(2,1)S(1)}, u32[]{:S(2)}, u32[]{:S(2)}) collective-permute-start(bf16[128,1792]{1,0:T(8,128)(2,1)S(1)} %get-tuple-element.44), channel_id=1, source_target_pairs={{0,24},{4,28},{8,16},{12,20},{16,8},{20,12},{24,0},{28,4},{1,25},{... | collective-permute-start | bytes 1376264 | tf_op jit(solution)/shard_map/ppermute | solution.py:216
  64.3 6.0 %shard_map.70.found = f32[2,128,1792]{2,1,0:T(8,128)S(1)} custom-call(bf16[128,4096]{1,0:T(8,128)(2,1)S(1)} %broadcast_select_fusion.1.refs_0_, bf16[128,4096]{1,0:T(8,128)(2,1)S(1)} %collective-permute-done.4.refs_1_, bf16[32,128,128]{2,1,0:T(8,128)(2,1)S(1)} %bitcast.49, bf16[1792,4096]{1,0:T(8,128)(2,1)S(1)} %bitcast.28), custom_call_target="tpu_custom_call" | custom-call | tf_op jit(solution)/shard_map/pallas_call | solution.py:43
  70.4 0.7 shard_map.71
  71.1 0.8 shard_map.72
  71.9 23.5 %collective-permute-done.9.piece = bf16[128,1792]{1,0:T(8,128)(2,1)S(1)} collective-permute-done((bf16[128,1792]{1,0:T(8,128)(2,1)S(1)}, bf16[128,1792]{1,0:T(8,128)(2,1)S(1)}, u32[]{:S(2)}, u32[]{:S(2)}) %collective-permute-start.9) | collective-permute-done | bytes 458784 | tf_op jit(solution)/shard_map/ppermute | solution.py:216
  95.4 3.8 %collective-permute-done.10.refs_0_ = bf16[128,1792]{1,0:T(8,128)(2,1)S(1)} collective-permute-done((bf16[128,1792]{1,0:T(8,128)(2,1)S(1)}, bf16[128,1792]{1,0:T(8,128)(2,1)S(1)}, u32[]{:S(2)}, u32[]{:S(2)}) %collective-permute-start.10) | collective-permute-done | bytes 458784 | tf_op jit(solution)/shard_map/ppermute | solution.py:216
  99.2 2.0 %collective-permute-done.8.piece = bf16[128,1792]{1,0:T(8,128)(2,1)S(1)} collective-permute-done((bf16[128,1792]{1,0:T(8,128)(2,1)S(1)}, bf16[128,1792]{1,0:T(8,128)(2,1)S(1)}, u32[]{:S(2)}, u32[]{:S(2)}) %collective-permute-start.8) | collective-permute-done | bytes 458784 | tf_op jit(solution)/shard_map/ppermute | solution.py:216
  101.2 0.0 collective-permute-done.7.refs_1_
  101.2 0.1 broadcast_select_fusion.refs_0_
  101.3 0.9 collective-permute-start.11
  102.2 1.1 collective-permute-start.14
  103.2 2.0 %collective-permute-start.15 = (bf16[128,1792]{1,0:T(8,128)(2,1)S(1)}, bf16[128,1792]{1,0:T(8,128)(2,1)S(1)}, u32[]{:S(2)}, u32[]{:S(2)}) collective-permute-start(bf16[128,1792]{1,0:T(8,128)(2,1)S(1)} %shard_map.69), channel_id=1, source_target_pairs={{0,8},{4,12},{8,0},{12,4},{16,24},{20,28},{24,16},{28,20},{1,9},{5... | collective-permute-start | bytes 1376264 | tf_op jit(solution)/shard_map/ppermute | solution.py:216
  105.2 6.0 %shard_map.73.found = f32[2,128,1792]{2,1,0:T(8,128)S(1)} custom-call(bf16[128,4096]{1,0:T(8,128)(2,1)S(1)} %broadcast_select_fusion.refs_0_, bf16[128,4096]{1,0:T(8,128)(2,1)S(1)} %collective-permute-done.7.refs_1_, bf16[32,128,128]{2,1,0:T(8,128)(2,1)S(1)} %bitcast.50, bf16[1792,4096]{1,0:T(8,128)(2,1)S(1)} %bitcast.29), custom_call_target="tpu_custom_call" | custom-call | tf_op jit(solution)/shard_map/pallas_call | solution.py:43
  111.2 0.9 shard_map.76
  112.1 1.4 collective-permute-start.12
  113.6 0.7 shard_map.74
  114.3 0.8 shard_map.75
  115.1 8.2 %collective-permute-done.12 = f32[1,128]{1,0:T(1,128)S(1)} collective-permute-done((f32[1,128]{1,0:T(1,128)S(1)}, f32[1,128]{1,0:T(1,128)S(1)}, u32[]{:S(2)}, u32[]{:S(2)}) %collective-permute-start.12) | collective-permute-done | bytes 544 | tf_op jit(solution)/shard_map/ppermute | solution.py:216
  123.3 2.1 %collective-permute-start.16 = (bf16[128,1792]{1,0:T(8,128)(2,1)S(1)}, bf16[128,1792]{1,0:T(8,128)(2,1)S(1)}, u32[]{:S(2)}, u32[]{:S(2)}) collective-permute-start(bf16[128,1792]{1,0:T(8,128)(2,1)S(1)} %shard_map.71), channel_id=1, source_target_pairs={{0,12},{4,8},{8,4},{12,0},{16,28},{20,24},{24,20},{28,16},{1,13},{... | collective-permute-start | bytes 1376264 | tf_op jit(solution)/shard_map/ppermute | solution.py:216
  125.4 0.6 collective-permute-start.17
  126.0 6.7 %shard_map.77 = f32[1,128]{1,0:T(1,128)S(1)} custom-call(bf16[128,4096]{1,0:T(8,128)(2,1)S(1)} %collective-permute-done.11.chunk, bf16[32,128,128]{2,1,0:T(8,128)(2,1)S(1)} %bitcast.51, bf16[1792,4096]{1,0:T(8,128)(2,1)S(1)} %bitcast.30, bf16[128,1792]{1,0:T(8,128)(2,1)S(1)} %collective-permute-done.9.piece, bf16[14,128,128]{2,1,0:T(8,128)(2,1)S(1)} %bitcast.46), custom_call_target="tpu_custom_call" | custom-call | tf_op jit(solution)/shard_map/pallas_call | solution.py:181
  132.7 3.8 %collective-permute-start.13 = (f32[1,128]{1,0:T(1,128)S(1)}, f32[1,128]{1,0:T(1,128)S(1)}, u32[]{:S(2)}, u32[]{:S(2)}) collective-permute-start(f32[1,128]{1,0:T(1,128)S(1)} %shard_map.77), channel_id=1, source_target_pairs={{0,28},{4,24},{8,20},{12,16},{16,12},{20,8},{24,4},{28,0},{1,29},{... | collective-permute-start | bytes 1544 | tf_op jit(solution)/shard_map/ppermute | solution.py:216
  136.5 0.9 shard_map.78
  137.4 8.4 %collective-permute-done.13 = f32[1,128]{1,0:T(1,128)S(1)} collective-permute-done((f32[1,128]{1,0:T(1,128)S(1)}, f32[1,128]{1,0:T(1,128)S(1)}, u32[]{:S(2)}, u32[]{:S(2)}) %collective-permute-start.13) | collective-permute-done | bytes 544 | tf_op jit(solution)/shard_map/ppermute | solution.py:216
  145.8 0.7 collective-permute-done.17.refs_0_
  146.6 0.9 shard_map.79
  147.5 0.1 collective-permute-start.18
  147.6 1.6 %collective-permute-start.19 = (f32[128]{0:T(128)S(1)}, f32[128]{0:T(128)S(1)}, u32[]{:S(2)}, u32[]{:S(2)}) collective-permute-start(f32[128]{0:T(128)S(1)} %bitcast.57), channel_id=1, source_target_pairs={{0,2},{1,3},{2,0},{3,1},{4,6},{5,7},{6,4},{7,5},{8,10},{9,11},{10,... | collective-permute-start | bytes 1544 | tf_op jit(solution)/shard_map/ppermute | solution.py:274
  149.2 0.3 collective-permute-start.20
  149.4 1.7 %collective-permute-done.19 = f32[128]{0:T(128)S(1)} collective-permute-done((f32[128]{0:T(128)S(1)}, f32[128]{0:T(128)S(1)}, u32[]{:S(2)}, u32[]{:S(2)}) %collective-permute-start.19) | collective-permute-done | bytes 544 | tf_op jit(solution)/shard_map/ppermute | solution.py:274
  151.2 0.9 collective-permute-done.20
  152.1 0.5 fusion.1
  (33 shorter events, 0.1 us)
Async XLA Ops:
  0.0 6.2 %copy-start = (s32[1,8]{1,0:T(1,128)S(1)}, s32[1,8]{1,0:T(1,128)}, u32[]{:S(2)}) copy-start(s32[1,8]{1,0:T(1,128)} %param.11) | copy-start | bytes 100
  0.0 26.5 %collective-permute-start.1 = (bf16[128,4096]{1,0:T(8,128)(2,1)}, bf16[128,4096]{1,0:T(8,128)(2,1)}, u32[]{:S(2)}, u32[]{:S(2)}) collective-permute-start(bf16[128,4096]{1,0:T(8,128)(2,1)} %bitcast.52), channel_id=1, source_target_pairs={{0,8},{4,12},{8,0},{12,4},{16,24},{20,28},{24,16},{28,20},{1,9},{5... | collective-permute-start | bytes 3145736 | tf_op jit(solution)/shard_map/ppermute | solution.py:216
  3.0 26.8 %collective-permute-start = (bf16[128,4096]{1,0:T(8,128)(2,1)}, bf16[128,4096]{1,0:T(8,128)(2,1)}, u32[]{:S(2)}, u32[]{:S(2)}) collective-permute-start(bf16[128,4096]{1,0:T(8,128)(2,1)} %bitcast.53), channel_id=1, source_target_pairs={{8,16},{12,20},{16,8},{20,12},{9,17},{13,21},{17,9},{21,13},{10,18... | collective-permute-start | bytes 3145736 | tf_op jit(solution)/shard_map/ppermute | solution.py:213
  4.7 28.6 %collective-permute-start.5 = (bf16[128,4096]{1,0:T(8,128)(2,1)}, bf16[128,4096]{1,0:T(8,128)(2,1)}, u32[]{:S(2)}, u32[]{:S(2)}) collective-permute-start(bf16[128,4096]{1,0:T(8,128)(2,1)} %bitcast.54), channel_id=1, source_target_pairs={{0,4},{4,0},{8,12},{12,8},{16,20},{20,16},{24,28},{28,24},{1,5},{5... | collective-permute-start | bytes 3145736 | tf_op jit(solution)/shard_map/ppermute | solution.py:216
  6.8 2.0 %copy-start.3 = (bf16[1,128,14336]{2,1,0:T(8,128)(2,1)S(1)}, bf16[1,128,14336]{2,1,0:T(8,128)(2,1)}, u32[]{:S(2)}) copy-start(bf16[1,128,14336]{2,1,0:T(8,128)(2,1)} %param.7) | copy-start | bytes 11010052
  8.9 1.4 copy-start.6
  8.9 1.5 %copy-start.7 = (bf16[1,128,4096]{2,1,0:T(8,128)(2,1)S(1)}, bf16[1,128,4096]{2,1,0:T(8,128)(2,1)}, u32[]{:S(2)}) copy-start(bf16[1,128,4096]{2,1,0:T(8,128)(2,1)} %param.6) | copy-start | bytes 3145732
  9.5 0.8 copy-start.8
  10.4 5.2 %copy-start.1 = (bf16[1,1792,4096]{2,1,0:T(8,128)(2,1)S(1)}, bf16[1,1792,4096]{2,1,0:T(8,128)(2,1)}, u32[]{:S(2)}) copy-start(bf16[1,1792,4096]{2,1,0:T(8,128)(2,1)} %param.8) | copy-start | bytes 44040196
  26.5 22.7 %collective-permute-start.2 = (bf16[128,4096]{1,0:T(8,128)(2,1)}, bf16[128,4096]{1,0:T(8,128)(2,1)}, u32[]{:S(2)}, u32[]{:S(2)}) collective-permute-start(bf16[128,4096]{1,0:T(8,128)(2,1)} %collective-permute-done.1.refs_0_), channel_id=1, source_target_pairs={{8,16},{12,20},{16,8},{20,12},{9,17},{13,21},{17,9},{21,13},{10,18... | collective-permute-start | bytes 3145736 | tf_op jit(solution)/shard_map/ppermute | solution.py:213
  28.1 24.6 %collective-permute-start.4 = (bf16[128,4096]{1,0:T(8,128)(2,1)}, bf16[128,4096]{1,0:T(8,128)(2,1)S(1)}, u32[]{:S(2)}, u32[]{:S(2)}) collective-permute-start(bf16[128,4096]{1,0:T(8,128)(2,1)} %collective-permute-done.1.refs_0_), channel_id=1, source_target_pairs={{0,4},{4,0},{8,12},{12,8},{16,20},{20,16},{24,28},{28,24},{1,5},{5... | collective-permute-start | bytes 3145736 | tf_op jit(solution)/shard_map/ppermute | solution.py:216
  29.8 25.5 %collective-permute-start.3 = (bf16[128,4096]{1,0:T(8,128)(2,1)}, bf16[128,4096]{1,0:T(8,128)(2,1)}, u32[]{:S(2)}, u32[]{:S(2)}) collective-permute-start(bf16[128,4096]{1,0:T(8,128)(2,1)} %collective-permute-done), channel_id=1, source_target_pairs={{0,8},{4,12},{8,0},{12,4},{16,24},{20,28},{24,16},{28,20},{1,9},{5... | collective-permute-start | bytes 3145736 | tf_op jit(solution)/shard_map/ppermute | solution.py:216
  33.3 5.2 %copy-start.2 = (bf16[1,1792,4096]{2,1,0:T(8,128)(2,1)S(1)}, bf16[1,1792,4096]{2,1,0:T(8,128)(2,1)}, u32[]{:S(2)}) copy-start(bf16[1,1792,4096]{2,1,0:T(8,128)(2,1)} %param.8) | copy-start | bytes 44040196
  38.5 7.8 %copy-start.5 = (bf16[1,14,128,128]{3,2,1,0:T(8,128)(2,1)S(1)}, bf16[1,14,128,128]{3,2,1,0:T(8,128)(2,1)}, u32[]{:S(2)}) copy-start(bf16[1,14,128,128]{3,2,1,0:T(8,128)(2,1)} %param.10) | copy-start | bytes 1376260
  38.5 25.8 %slice-start = ((s8[14680064]{0:T(1024)(128)(4,1)}), s8[4194304]{0:T(1024)(128)(4,1)S(1)}, s32[]{:S(2)}) async-start(s8[14680064]{0:T(1024)(128)(4,1)} %bitcast.26), calls=%async_computation | async-start | bytes 8388608
  38.5 25.8 %slice-start.1 = ((s8[14680064]{0:T(1024)(128)(4,1)}), s8[4194304]{0:T(1024)(128)(4,1)S(1)}, s32[]{:S(2)}) async-start(s8[14680064]{0:T(1024)(128)(4,1)} %bitcast.26), calls=%async_computation.1 | async-start | bytes 8388608
  38.5 25.8 %slice-start.2 = ((s8[14680064]{0:T(1024)(128)(4,1)}), s8[4194304]{0:T(1024)(128)(4,1)S(1)}, s32[]{:S(2)}) async-start(s8[14680064]{0:T(1024)(128)(4,1)} %bitcast.26), calls=%async_computation.2 | async-start | bytes 8388608
  46.3 2.0 %copy-start.4 = (bf16[1,128,14336]{2,1,0:T(8,128)(2,1)S(1)}, bf16[1,128,14336]{2,1,0:T(8,128)(2,1)}, u32[]{:S(2)}) copy-start(bf16[1,128,14336]{2,1,0:T(8,128)(2,1)} %param.7) | copy-start | bytes 11010052
  47.0 17.3 %slice-start.3 = ((s8[14680064]{0:T(1024)(128)(4,1)}), s8[2097152]{0:T(1024)(128)(4,1)S(1)}, s32[]{:S(2)}) async-start(s8[14680064]{0:T(1024)(128)(4,1)} %bitcast.26), calls=%async_computation.3 | async-start | bytes 4194304
  49.2 9.8 %copy-start.9 = (bf16[128,1792]{1,0:T(8,128)(2,1)S(1)}, bf16[128,1792]{1,0:T(8,128)(2,1)}, u32[]{:S(2)}) copy-start(bf16[128,1792]{1,0:T(8,128)(2,1)} %copy-done.8) | copy-start | bytes 1376260
  56.7 44.5 %collective-permute-start.7 = (bf16[128,4096]{1,0:T(8,128)(2,1)S(1)}, bf16[128,4096]{1,0:T(8,128)(2,1)S(1)}, u32[]{:S(2)}, u32[]{:S(2)}) collective-permute-start(bf16[128,4096]{1,0:T(8,128)(2,1)S(1)} %broadcast_select_fusion.1.refs_0_), channel_id=1, source_target_pairs={{0,4},{4,0},{8,12},{12,8},{16,20},{20,16},{24,28},{28,24},{1,5},{5... | collective-permute-start | bytes 3145736 | tf_op jit(solution)/shard_map/ppermute | solution.py:216
  57.3 43.9 %collective-permute-start.6 = (bf16[128,4096]{1,0:T(8,128)(2,1)}, bf16[128,4096]{1,0:T(8,128)(2,1)S(1)}, u32[]{:S(2)}, u32[]{:S(2)}) collective-permute-start(bf16[128,4096]{1,0:T(8,128)(2,1)} %collective-permute-done.2), channel_id=1, source_target_pairs={{0,8},{4,12},{8,0},{12,4},{16,24},{20,28},{24,16},{28,20},{1,9},{5... | collective-permute-start | bytes 3145736 | tf_op jit(solution)/shard_map/ppermute | solution.py:216
  59.0 36.4 %collective-permute-start.9 = (bf16[128,1792]{1,0:T(8,128)(2,1)S(1)}, bf16[128,1792]{1,0:T(8,128)(2,1)S(1)}, u32[]{:S(2)}, u32[]{:S(2)}) collective-permute-start(bf16[128,1792]{1,0:T(8,128)(2,1)S(1)} %copy-done.9), channel_id=1, source_target_pairs={{0,28},{4,24},{8,20},{12,16},{16,12},{20,8},{24,4},{28,0},{1,29},{... | collective-permute-start | bytes 1376264 | tf_op jit(solution)/shard_map/ppermute | solution.py:216
  61.3 37.9 %collective-permute-start.10 = (bf16[128,1792]{1,0:T(8,128)(2,1)S(1)}, bf16[128,1792]{1,0:T(8,128)(2,1)S(1)}, u32[]{:S(2)}, u32[]{:S(2)}) collective-permute-start(bf16[128,1792]{1,0:T(8,128)(2,1)S(1)} %shard_map.68), channel_id=1, source_target_pairs={{0,4},{4,0},{8,12},{12,8},{16,20},{20,16},{24,28},{28,24},{1,5},{5... | collective-permute-start | bytes 1376264 | tf_op jit(solution)/shard_map/ppermute | solution.py:216
  62.3 38.9 %collective-permute-start.8 = (bf16[128,1792]{1,0:T(8,128)(2,1)S(1)}, bf16[128,1792]{1,0:T(8,128)(2,1)S(1)}, u32[]{:S(2)}, u32[]{:S(2)}) collective-permute-start(bf16[128,1792]{1,0:T(8,128)(2,1)S(1)} %get-tuple-element.44), channel_id=1, source_target_pairs={{0,24},{4,28},{8,16},{12,20},{16,8},{20,12},{24,0},{28,4},{1,25},{... | collective-permute-start | bytes 1376264 | tf_op jit(solution)/shard_map/ppermute | solution.py:216
  101.3 22.0 %collective-permute-start.11 = (bf16[128,4096]{1,0:T(8,128)(2,1)S(1)}, bf16[128,4096]{1,0:T(8,128)(2,1)S(1)}, u32[]{:S(2)}, u32[]{:S(2)}) collective-permute-start(bf16[128,4096]{1,0:T(8,128)(2,1)S(1)} %broadcast_select_fusion.refs_0_), channel_id=1, source_target_pairs={{0,4},{4,0},{8,12},{12,8},{16,20},{20,16},{24,28},{28,24},{1,5},{5... | collective-permute-start | bytes 3145736 | tf_op jit(solution)/shard_map/ppermute | solution.py:216
  102.2 34.3 %collective-permute-start.14 = (bf16[128,1792]{1,0:T(8,128)(2,1)S(1)}, bf16[128,1792]{1,0:T(8,128)(2,1)S(1)}, u32[]{:S(2)}, u32[]{:S(2)}) collective-permute-start(bf16[128,1792]{1,0:T(8,128)(2,1)S(1)} %shard_map.72), channel_id=1, source_target_pairs={{0,16},{4,20},{8,24},{12,28},{16,0},{20,4},{24,8},{28,12},{1,17},{... | collective-permute-start | bytes 1376264 | tf_op jit(solution)/shard_map/ppermute | solution.py:216
  103.2 33.2 %collective-permute-start.15 = (bf16[128,1792]{1,0:T(8,128)(2,1)S(1)}, bf16[128,1792]{1,0:T(8,128)(2,1)S(1)}, u32[]{:S(2)}, u32[]{:S(2)}) collective-permute-start(bf16[128,1792]{1,0:T(8,128)(2,1)S(1)} %shard_map.69), channel_id=1, source_target_pairs={{0,8},{4,12},{8,0},{12,4},{16,24},{20,28},{24,16},{28,20},{1,9},{5... | collective-permute-start | bytes 1376264 | tf_op jit(solution)/shard_map/ppermute | solution.py:216
  112.1 11.2 %collective-permute-start.12 = (f32[1,128]{1,0:T(1,128)S(1)}, f32[1,128]{1,0:T(1,128)S(1)}, u32[]{:S(2)}, u32[]{:S(2)}) collective-permute-start(f32[1,128]{1,0:T(1,128)S(1)} %shard_map.76), channel_id=1, source_target_pairs={{0,24},{4,28},{8,16},{12,20},{16,8},{20,12},{24,0},{28,4},{1,25},{... | collective-permute-start | bytes 1544 | tf_op jit(solution)/shard_map/ppermute | solution.py:216
  123.3 22.5 %collective-permute-start.16 = (bf16[128,1792]{1,0:T(8,128)(2,1)S(1)}, bf16[128,1792]{1,0:T(8,128)(2,1)S(1)}, u32[]{:S(2)}, u32[]{:S(2)}) collective-permute-start(bf16[128,1792]{1,0:T(8,128)(2,1)S(1)} %shard_map.71), channel_id=1, source_target_pairs={{0,12},{4,8},{8,4},{12,0},{16,28},{20,24},{24,20},{28,16},{1,13},{... | collective-permute-start | bytes 1376264 | tf_op jit(solution)/shard_map/ppermute | solution.py:216
  125.4 21.1 %collective-permute-start.17 = (bf16[128,1792]{1,0:T(8,128)(2,1)S(1)}, bf16[128,1792]{1,0:T(8,128)(2,1)S(1)}, u32[]{:S(2)}, u32[]{:S(2)}) collective-permute-start(bf16[128,1792]{1,0:T(8,128)(2,1)S(1)} %shard_map.74), channel_id=1, source_target_pairs={{0,20},{4,16},{8,28},{12,24},{16,4},{20,0},{24,12},{28,8},{1,21},{... | collective-permute-start | bytes 1376264 | tf_op jit(solution)/shard_map/ppermute | solution.py:216
  132.7 13.1 %collective-permute-start.13 = (f32[1,128]{1,0:T(1,128)S(1)}, f32[1,128]{1,0:T(1,128)S(1)}, u32[]{:S(2)}, u32[]{:S(2)}) collective-permute-start(f32[1,128]{1,0:T(1,128)S(1)} %shard_map.77), channel_id=1, source_target_pairs={{0,28},{4,24},{8,20},{12,16},{16,12},{20,8},{24,4},{28,0},{1,29},{... | collective-permute-start | bytes 1544 | tf_op jit(solution)/shard_map/ppermute | solution.py:216
  147.5 1.9 %collective-permute-start.18 = (f32[128]{0:T(128)S(1)}, f32[128]{0:T(128)S(1)}, u32[]{:S(2)}, u32[]{:S(2)}) collective-permute-start(f32[128]{0:T(128)S(1)} %bitcast.56), channel_id=1, source_target_pairs={{0,1},{1,0},{2,3},{3,2},{4,5},{5,4},{6,7},{7,6},{8,9},{9,8},{10,11... | collective-permute-start | bytes 1544 | tf_op jit(solution)/shard_map/ppermute | solution.py:274
  147.6 3.6 %collective-permute-start.19 = (f32[128]{0:T(128)S(1)}, f32[128]{0:T(128)S(1)}, u32[]{:S(2)}, u32[]{:S(2)}) collective-permute-start(f32[128]{0:T(128)S(1)} %bitcast.57), channel_id=1, source_target_pairs={{0,2},{1,3},{2,0},{3,1},{4,6},{5,7},{6,4},{7,5},{8,10},{9,11},{10,... | collective-permute-start | bytes 1544 | tf_op jit(solution)/shard_map/ppermute | solution.py:274
  149.2 3.0 %collective-permute-start.20 = (f32[128]{0:T(128)S(1)}, f32[128]{0:T(128)S(1)}, u32[]{:S(2)}, u32[]{:S(2)}) collective-permute-start(f32[128]{0:T(128)S(1)} %bitcast.58), channel_id=1, source_target_pairs={{0,3},{1,2},{2,1},{3,0},{4,7},{5,6},{6,5},{7,4},{8,11},{9,10},{10,... | collective-permute-start | bytes 1544 | tf_op jit(solution)/shard_map/ppermute | solution.py:274

commit v5 on v4

--- a/solution.py
+++ b/solution.py
@@ -26,7 +26,7 @@
     @pl.when(pl.program_id(0) == 0)
     def _():
         for c, chunk in enumerate(chunks):
-            for n, part in enumerate(blocks_of(chunk.shape[1])):
+            for n, part in enumerate(blocks_of(turned.shape[1])):
                 turned[pl.ds(c * rows, rows), part] = jnp.dot(
                     chunk[:, part], basis[n], preferred_element_type=jnp.float32
                 ).astype(jnp.bfloat16)
@@ -36,8 +36,8 @@
 
 
 def project(chunks, basis, query):
-    count, (rows, wide) = len(chunks), chunks[0].shape
-    units = query.shape[0]
+    count, rows = len(chunks), chunks[0].shape[0]
+    units, wide = query.shape
     step = 2 * TILE if units % (2 * TILE) == 0 else TILE
     whole = lambda *shape: pl.BlockSpec(shape, lambda i: (0,) * len(shape))
     return pl.pallas_call(
@@ -153,6 +153,34 @@
         compiler_params=pltpu.CompilerParams(vmem_limit_bytes=16 * MIB),
         cost_estimate=free,
     )(found, basis)
+
+
+def joined_kernel(wide, found, first, second, basis, out):
+    ends = [(held, n) for held in (first, second) for n in range(wide, held.shape[1], TILE)]
+    total = jnp.zeros((found.shape[0], TILE), jnp.float32)
+    for n, (held, at) in enumerate(ends):
+        piece = held[:, pl.ds(at, TILE)]
+        turned = jnp.dot(piece, basis[n], preferred_element_type=jnp.float32).astype(jnp.bfloat16)
+        total += turned.astype(jnp.float32) * found[:, pl.ds(n * TILE, TILE)]
+    out[...] = lay(total)
+
+
+def score_joined(found, c, first, second, wide, basis):
+    _, rows, units = found.shape
+    return pl.pallas_call(
+        functools.partial(joined_kernel, wide),
+        grid=(1,),
+        in_specs=[
+            pl.BlockSpec((None, rows, units), lambda i: (c, 0, 0)),
+            pl.BlockSpec(first.shape, lambda i: (0, 0)),
+            pl.BlockSpec(second.shape, lambda i: (0, 0)),
+            pl.BlockSpec(basis.shape, lambda i: (0, 0, 0)),
+        ],
+        out_specs=pl.BlockSpec((1, rows), lambda i: (0, 0)),
+        out_shape=jax.ShapeDtypeStruct((1, rows), jnp.float32),
+        compiler_params=pltpu.CompilerParams(vmem_limit_bytes=16 * MIB),
+        cost_estimate=free,
+    )(found, first, second, basis)
 
 
 def project_score_kernel(chunk, basis, query, piece, turn, out, turned, total):
@@ -224,28 +252,29 @@
     aside = lambda d: [d * across + j for j in range(1, across)]
     one, two, three = across, 2 * across, 3 * across
 
+    wide, cut = own.shape[1], units // TILE // 2 * TILE
+    got, come = {}, {}
     a1, a2, a3 = line(own, 1), middle(own), sideways(own)
-    pieces = pack([three] + aside(3), order, grads, units)
+    pieces = pack(aside(0) + [three] + aside(3), order, grads, units)
     p_own = project([own], turn_in, query)
     a1, pieces, p_own = hold((a1, pieces, p_own))
-    got = send(pieces, aside(3))
-    b1, b3, b2 = middle(a1), sideways(a1), line(a2, 1)
-    p_a = project([a1] + a3, turn_in, query)
+    join = lambda value, cols: [swap(jnp.concatenate([value, pieces[j][:, cols]], axis=1), j) for j in range(1, across)]
+    got.update(send(pieces, aside(3)))
+    b1, b2 = middle(a1), line(a2, 1)
+    b3 = join(a1, slice(0, cut))
     total = score(p_own, 0, order, 0, grads, turn_out)
-    ready = {one: back(p_a, 0, turn_out)}
-    for j in range(1, across):
-        ready[j] = back(p_a, j, turn_out)
-    a2, b1, b2, b3, pieces, total, ready = hold((a2, b1, b2, b3, pieces, total, ready))
+    a1, a3, a2, b1, b2, pieces, total = hold((a1, a3, a2, b1, b2, pieces, total))
     c1 = line(b1, 1)
     far2 = jnp.where(inner, b1, b2)
-    side2 = sideways(far2)
+    side2 = join(far2, slice(cut, units))
     got.update(send(pieces, [three]))
-    come = send(ready, aside(0))
+    p_a = project([a1] + a3, turn_in, query)
+    ready = {one: back(p_a, 0, turn_out)}
     p_b = project([far2] + b3, turn_in, query)
     ready[two] = back(p_b, 0, turn_out)
     for j in range(1, across):
         ready[one + j] = back(p_b, j, turn_out)
-    c1, side2, got, come, ready = hold((c1, side2, got, come, ready))
+    c1, got, ready = hold((c1, got, ready))
     far3 = jnp.where(inner, a2, c1)
     side3 = sideways(far3)
     come.update(send(ready, [two, one]))
@@ -253,13 +282,13 @@
     sums = {three: score(p_c, 0, order, None, got[three], turn_out)}
     for j in range(1, across):
         ready[two + j] = back(p_c, j, turn_out)
-    total += meet({j: come[j] for j in aside(0)}, order, grads)
-    sums = send(sums, list(sums))
-    side3, ready, total, sums = hold((side3, ready, total, sums))
-    total += sums[three]
-    sums = {}
+        sums[j] = score_joined(p_a, j, b3[j - 1], side2[j - 1], wide, turn_out)
+    for value in send(sums, list(sums)).values():
+        total += value
+    side3, ready, total, come = hold((side3, ready, total, come))
     late = aside(2) + aside(1)
     come.update(send(ready, late))
+    sums = {}
     for j in range(1, across):
         sums[three + j] = project_score(side3[j - 1], turn_in, query, got[three + j], turn_out)
     for value in send(sums, list(sums)).values():

time: 153 us -> 150 us (0.980)
  waiting for transfers between devices: 60.1 us -> 45.4 us
  starting transfers between devices: 34.3 us -> 42.7 us
  local copies, waits for them, and re-layouts: 14.5 us -> 18.5 us
    ppermute x16, waiting for transfers between devices: 57.4 us -> 42.7 us  [swap(): return lax.ppermute(value, 'seq', [(s, s ^ j) for s in range(size)])]
    ppermute x16, starting transfers between devices: 29.1 us -> 37.5 us  [swap(): return lax.ppermute(value, 'seq', [(s, s ^ j) for s in range(size)])]
    unnamed x28 -> x32, local copies, waits for them, and re-layouts: 13.8 us -> 16.8 us
    pallas_call x5 -> x4, Pallas kernels: 3.74 us -> 2.99 us  [back(): pl.pallas_call(back_kernel, grid=(1,), in_specs=[pl.BlockSpec((None, rows...]
    pallas_call x5 -> x4, Pallas kernels: 4.45 us -> 3.71 us  [small(): pl.pallas_call(kernel, grid_spec=pltpu.PrefetchScalarGridSpec(num_scalar_...]
  transfers between devices with their start and end apart: 21 -> 21, of which waited for: 11 -> 9; matrix products, arithmetic and copies ran while one was open for 0% -> 2% of each run, Pallas kernels for 27% -> 27%
where the time goes in v5:
time: 150 us
  waiting for transfers between devices  45.4 us (30%)
  starting transfers between devices  42.7 us (28%)
  Pallas kernels  41 us (27%)
  local copies, waits for them, and re-layouts  18.5 us (12%)
  other arithmetic  2.28 us (2%)
    ppermute x16, waiting for transfers between devices, swap(): return lax.ppermute(value, 'seq', [(s, s ^ j) for s in range(size)])  42.7 us
    ppermute x16, starting transfers between devices, swap(): return lax.ppermute(value, 'seq', [(s, s ^ j) for s in range(size)])  37.5 us
    pallas_call x4, Pallas kernels, project(): pl.pallas_call(functools.partial(project_kernel, count), grid=(units // s...  26.5 us
    unnamed x32, local copies, waits for them, and re-layouts  16.8 us
    pallas_call x1, Pallas kernels, project_score(): pl.pallas_call(project_score_kernel, grid=(units // step,), in_specs=[who...  6.8 us
    pallas_call x4, Pallas kernels, small(): pl.pallas_call(kernel, grid_spec=pltpu.PrefetchScalarGridSpec(num_scalar_...  3.71 us
    ppermute x2, starting transfers between devices, move(): return lax.ppermute(value, 'seq', pairs)  3.28 us
  transfers between devices with their start and end apart: 21, of which 9 were waited for; matrix products, arithmetic and copies ran while one was open for 2% of the time, Pallas kernels for 27%

profile of v5, /device:TPU:0, one launch (start us, length us, event | category | flops | bytes accessed | tf_op | source)
XLA Modules:
  0.0 150.0 jit_solution(5092974895818276433)
XLA Ops:
  0.0 3.0 %collective-permute-start = (bf16[128,4096]{1,0:T(8,128)(2,1)}, bf16[128,4096]{1,0:T(8,128)(2,1)S(1)}, u32[]{:S(2)}, u32[]{:S(2)}) collective-permute-start(bf16[128,4096]{1,0:T(8,128)(2,1)} %bitcast.50), channel_id=1, source_target_pairs={{0,8},{4,12},{8,0},{12,4},{16,24},{20,28},{24,16},{28,20},{1,9},{5... | collective-permute-start | bytes 3145736 | tf_op jit(solution)/shard_map/ppermute | solution.py:244
  3.0 1.6 %collective-permute-start.2 = (bf16[128,4096]{1,0:T(8,128)(2,1)}, bf16[128,4096]{1,0:T(8,128)(2,1)}, u32[]{:S(2)}, u32[]{:S(2)}) collective-permute-start(bf16[128,4096]{1,0:T(8,128)(2,1)} %bitcast.51), channel_id=1, source_target_pairs={{8,16},{12,20},{16,8},{20,12},{9,17},{13,21},{17,9},{21,13},{10,18... | collective-permute-start | bytes 3145736 | tf_op jit(solution)/shard_map/ppermute | solution.py:241
  4.7 1.5 collective-permute-start.1
  6.2 0.6 gather_fusion
  6.8 0.0 copy-start.4
  6.8 2.0 %copy-done.4 = bf16[1,128,14336]{2,1,0:T(8,128)(2,1)S(1)} copy-done((bf16[1,128,14336]{2,1,0:T(8,128)(2,1)S(1)}, bf16[1,128,14336]{2,1,0:T(8,128)(2,1)}, u32[]{:S(2)}) %copy-start.4) | copy-done | bytes 3670040
  8.9 0.6 shard_map.64
  9.5 0.8 copy-done.10
  10.3 0.8 copy-done.12
  11.1 0.8 copy-done.14
  11.9 5.2 %copy-done.1 = bf16[1,1792,4096]{2,1,0:T(8,128)(2,1)S(1)} copy-done((bf16[1,1792,4096]{2,1,0:T(8,128)(2,1)S(1)}, bf16[1,1792,4096]{2,1,0:T(8,128)(2,1)}, u32[]{:S(2)}) %copy-start.1) | copy-done | bytes 14680088
  17.0 6.4 %shard_map.65.found = f32[1,128,1792]{2,1,0:T(8,128)S(1)} custom-call(bf16[128,4096]{1,0:T(8,128)(2,1)S(1)} %bitcast.53, bf16[32,128,128]{2,1,0:T(8,128)(2,1)S(1)} %bitcast.45, bf16[1792,4096]{1,0:T(8,128)(2,1)S(1)} %bitcast.24), custom_call_target="tpu_custom_call" | custom-call | tf_op jit(solution)/shard_map/pallas_call | solution.py:43
  23.5 0.0 copy-start.7
  23.5 2.9 %collective-permute-done.refs_0_ = bf16[128,4096]{1,0:T(8,128)(2,1)S(1)} collective-permute-done((bf16[128,4096]{1,0:T(8,128)(2,1)}, bf16[128,4096]{1,0:T(8,128)(2,1)S(1)}, u32[]{:S(2)}, u32[]{:S(2)}) %collective-permute-start) | collective-permute-done | bytes 1048608 | tf_op jit(solution)/shard_map/ppermute | solution.py:244
  26.4 1.7 %collective-permute-start.3 = (bf16[128,4096]{1,0:T(8,128)(2,1)S(1)}, bf16[128,4096]{1,0:T(8,128)(2,1)}, u32[]{:S(2)}, u32[]{:S(2)}) collective-permute-start(bf16[128,4096]{1,0:T(8,128)(2,1)S(1)} %collective-permute-done.refs_0_), channel_id=1, source_target_pairs={{8,16},{12,20},{16,8},{20,12},{9,17},{13,21},{17,9},{21,13},{10,18... | collective-permute-start | bytes 3145736 | tf_op jit(solution)/shard_map/ppermute | solution.py:241
  28.1 3.6 %collective-permute-start.4 = (bf16[128,4096]{1,0:T(8,128)(2,1)}, bf16[128,4096]{1,0:T(8,128)(2,1)}, u32[]{:S(2)}, u32[]{:S(2)}) collective-permute-start(bf16[128,4096]{1,0:T(8,128)(2,1)} %collective-permute-done.2), channel_id=1, source_target_pairs={{0,8},{4,12},{8,0},{12,4},{16,24},{20,28},{24,16},{28,20},{1,9},{5... | collective-permute-start | bytes 3145736 | tf_op jit(solution)/shard_map/ppermute | solution.py:244
  31.7 1.0 slice.6
  32.7 0.1 pad_maximum_fusion
  32.8 1.6 %collective-permute-start.8 = (bf16[128,4992]{1,0:T(8,128)(2,1)S(1)}, bf16[128,4992]{1,0:T(8,128)(2,1)S(1)}, u32[]{:S(2)}, u32[]{:S(2)}) collective-permute-start(bf16[128,4992]{1,0:T(8,128)(2,1)S(1)} %pad_maximum_fusion), channel_id=1, source_target_pairs={{0,4},{4,0},{8,12},{12,8},{16,20},{20,16},{24,28},{28,24},{1,5},{5... | collective-permute-start | bytes 3833864 | tf_op jit(solution)/shard_map/ppermute | solution.py:244
  34.4 2.2 %collective-permute-start.7 = (bf16[128,1792]{1,0:T(8,128)(2,1)S(1)}, bf16[128,1792]{1,0:T(8,128)(2,1)S(1)}, u32[]{:S(2)}, u32[]{:S(2)}) collective-permute-start(bf16[128,1792]{1,0:T(8,128)(2,1)S(1)} %copy-done.15), channel_id=1, source_target_pairs={{0,28},{4,24},{8,20},{12,16},{16,12},{20,8},{24,4},{28,0},{1,29},{... | collective-permute-start | bytes 1376264 | tf_op jit(solution)/shard_map/ppermute | solution.py:244
  36.6 2.0 %copy-done.5 = bf16[1,128,14336]{2,1,0:T(8,128)(2,1)S(1)} copy-done((bf16[1,128,14336]{2,1,0:T(8,128)(2,1)S(1)}, bf16[1,128,14336]{2,1,0:T(8,128)(2,1)}, u32[]{:S(2)}) %copy-start.5) | copy-done | bytes 3670040
  38.6 0.9 shard_map.66
  39.5 0.0 collective-permute-done.1.refs_1_
  39.5 0.0 collective-permute-done.3
  39.5 16.1 %collective-permute-done.4 = bf16[128,4096]{1,0:T(8,128)(2,1)} collective-permute-done((bf16[128,4096]{1,0:T(8,128)(2,1)}, bf16[128,4096]{1,0:T(8,128)(2,1)}, u32[]{:S(2)}, u32[]{:S(2)}) %collective-permute-start.4) | collective-permute-done | bytes 1048608 | tf_op jit(solution)/shard_map/ppermute | solution.py:244
  55.6 7.1 %collective-permute-start.5 = (bf16[128,4096]{1,0:T(8,128)(2,1)}, bf16[128,4096]{1,0:T(8,128)(2,1)S(1)}, u32[]{:S(2)}, u32[]{:S(2)}) collective-permute-start(bf16[128,4096]{1,0:T(8,128)(2,1)} %collective-permute-done.3), channel_id=1, source_target_pairs={{0,8},{4,12},{8,0},{12,4},{16,24},{20,28},{24,16},{28,20},{1,9},{5... | collective-permute-start | bytes 3145736 | tf_op jit(solution)/shard_map/ppermute | solution.py:244
  62.7 4.0 %collective-permute-start.6 = (bf16[128,1792]{1,0:T(8,128)(2,1)S(1)}, bf16[128,1792]{1,0:T(8,128)(2,1)S(1)}, u32[]{:S(2)}, u32[]{:S(2)}) collective-permute-start(bf16[128,1792]{1,0:T(8,128)(2,1)S(1)} %copy-done.13), channel_id=1, source_target_pairs={{0,24},{4,28},{8,16},{12,20},{16,8},{20,12},{24,0},{28,4},{1,25},{... | collective-permute-start | bytes 1376264 | tf_op jit(solution)/shard_map/ppermute | solution.py:244
  66.7 1.3 broadcast_select_fusion.1.refs_0_
  68.1 0.1 pad_maximum_fusion.1
  68.2 1.6 %collective-permute-start.10 = (bf16[128,4992]{1,0:T(8,128)(2,1)S(1)}, bf16[128,4992]{1,0:T(8,128)(2,1)S(1)}, u32[]{:S(2)}, u32[]{:S(2)}) collective-permute-start(bf16[128,4992]{1,0:T(8,128)(2,1)S(1)} %pad_maximum_fusion.1), channel_id=1, source_target_pairs={{0,4},{4,0},{8,12},{12,8},{16,20},{20,16},{24,28},{28,24},{1,5},{5... | collective-permute-start | bytes 3833864 | tf_op jit(solution)/shard_map/ppermute | solution.py:244
  69.8 5.2 %copy-done.2 = bf16[1,1792,4096]{2,1,0:T(8,128)(2,1)S(1)} copy-done((bf16[1,1792,4096]{2,1,0:T(8,128)(2,1)S(1)}, bf16[1,1792,4096]{2,1,0:T(8,128)(2,1)}, u32[]{:S(2)}) %copy-start.2) | copy-done | bytes 14680088
  74.9 7.5 %shard_map.67.found = f32[2,128,1792]{2,1,0:T(8,128)S(1)} custom-call(bf16[128,4096]{1,0:T(8,128)(2,1)S(1)} %collective-permute-done.refs_0_, bf16[128,4096]{1,0:T(8,128)(2,1)} %collective-permute-done.1.refs_1_, bf16[32,128,128]{2,1,0:T(8,128)(2,1)S(1)} %bitcast.46, bf16[1792,4096]{1,0:T(8,128)(2,1)S(1)} %bitcast.25), custom_call_target="tpu_custom_call" | custom-call | tf_op jit(solution)/shard_map/pallas_call | solution.py:43
  82.5 0.7 shard_map.68
  83.2 6.3 %shard_map.69.found = f32[2,128,1792]{2,1,0:T(8,128)S(1)} custom-call(bf16[128,4096]{1,0:T(8,128)(2,1)S(1)} %broadcast_select_fusion.1.refs_0_, bf16[128,4992]{1,0:T(8,128)(2,1)S(1)} %collective-permute-done.8.refs_1_.first, bf16[32,128,128]{2,1,0:T(8,128)(2,1)S(1)} %bitcast.47, bf16[1792,4096]{1,0:T(8,128)(2,1)S(1)} %bitcast.26), custom_call_target="tpu_custom_call" | custom-call | tf_op jit(solution)/shard_map/pallas_call | solution.py:43
  89.5 0.7 shard_map.70
  90.3 0.7 shard_map.71
  91.0 7.0 %collective-permute-done.6.piece = bf16[128,1792]{1,0:T(8,128)(2,1)S(1)} collective-permute-done((bf16[128,1792]{1,0:T(8,128)(2,1)S(1)}, bf16[128,1792]{1,0:T(8,128)(2,1)S(1)}, u32[]{:S(2)}, u32[]{:S(2)}) %collective-permute-start.6) | collective-permute-done | bytes 458784 | tf_op jit(solution)/shard_map/ppermute | solution.py:244
  98.0 0.2 broadcast_select_fusion.refs_0_
  98.2 1.6 %collective-permute-start.9 = (bf16[128,4096]{1,0:T(8,128)(2,1)S(1)}, bf16[128,4096]{1,0:T(8,128)(2,1)S(1)}, u32[]{:S(2)}, u32[]{:S(2)}) collective-permute-start(bf16[128,4096]{1,0:T(8,128)(2,1)S(1)} %broadcast_select_fusion.refs_0_), channel_id=1, source_target_pairs={{0,4},{4,0},{8,12},{12,8},{16,20},{20,16},{24,28},{28,24},{1,5},{5... | collective-permute-start | bytes 3145736 | tf_op jit(solution)/shard_map/ppermute | solution.py:244
  99.7 0.0 collective-permute-start.13
  99.7 2.3 %collective-permute-start.14 = (bf16[128,1792]{1,0:T(8,128)(2,1)S(1)}, bf16[128,1792]{1,0:T(8,128)(2,1)S(1)}, u32[]{:S(2)}, u32[]{:S(2)}) collective-permute-start(bf16[128,1792]{1,0:T(8,128)(2,1)S(1)} %shard_map.71), channel_id=1, source_target_pairs={{0,16},{4,20},{8,24},{12,28},{16,0},{20,4},{24,8},{28,12},{1,17},{... | collective-permute-start | bytes 1376264 | tf_op jit(solution)/shard_map/ppermute | solution.py:244
  102.1 0.0 collective-permute-done.10.refs_1_.second
  102.1 6.2 %shard_map.72.found = f32[2,128,1792]{2,1,0:T(8,128)S(1)} custom-call(bf16[128,4096]{1,0:T(8,128)(2,1)S(1)} %broadcast_select_fusion.refs_0_, bf16[128,4992]{1,0:T(8,128)(2,1)S(1)} %collective-permute-done.10.refs_1_.second, bf16[32,128,128]{2,1,0:T(8,128)(2,1)S(1)} %bitcast.48, bf16[1792,4096]{1,0:T(8,128)(2,1)S(1)} %bitcast.27), custom_call_target="tpu_custom_call" | custom-call | tf_op jit(solution)/shard_map/pallas_call | solution.py:43
  108.3 0.9 shard_map.74
  109.2 2.1 %collective-permute-start.11 = (f32[1,128]{1,0:T(1,128)S(1)}, f32[1,128]{1,0:T(1,128)S(1)}, u32[]{:S(2)}, u32[]{:S(2)}) collective-permute-start(f32[1,128]{1,0:T(1,128)S(1)} %shard_map.74), channel_id=1, source_target_pairs={{0,24},{4,28},{8,16},{12,20},{16,8},{20,12},{24,0},{28,4},{1,25},{... | collective-permute-start | bytes 1544 | tf_op jit(solution)/shard_map/ppermute | solution.py:244
  111.3 0.4 shard_map.75
  111.7 0.6 collective-permute-start.12
  112.3 0.7 shard_map.73
  113.1 6.6 %collective-permute-done.11 = f32[1,128]{1,0:T(1,128)S(1)} collective-permute-done((f32[1,128]{1,0:T(1,128)S(1)}, f32[1,128]{1,0:T(1,128)S(1)}, u32[]{:S(2)}, u32[]{:S(2)}) %collective-permute-start.11) | collective-permute-done | bytes 544 | tf_op jit(solution)/shard_map/ppermute | solution.py:244
  119.7 1.4 collective-permute-done.12
  121.1 1.3 collective-permute-start.16
  122.5 2.3 %collective-permute-start.17 = (bf16[128,1792]{1,0:T(8,128)(2,1)S(1)}, bf16[128,1792]{1,0:T(8,128)(2,1)S(1)}, u32[]{:S(2)}, u32[]{:S(2)}) collective-permute-start(bf16[128,1792]{1,0:T(8,128)(2,1)S(1)} %shard_map.73), channel_id=1, source_target_pairs={{0,20},{4,16},{8,28},{12,24},{16,4},{20,0},{24,12},{28,8},{1,21},{... | collective-permute-start | bytes 1376264 | tf_op jit(solution)/shard_map/ppermute | solution.py:244
  124.7 6.8 %shard_map.76 = f32[1,128]{1,0:T(1,128)S(1)} custom-call(bf16[128,4096]{1,0:T(8,128)(2,1)S(1)} %collective-permute-done.9.chunk, bf16[32,128,128]{2,1,0:T(8,128)(2,1)S(1)} %bitcast.49, bf16[1792,4096]{1,0:T(8,128)(2,1)S(1)} %bitcast.28, bf16[128,1792]{1,0:T(8,128)(2,1)S(1)} %collective-permute-done.7.piece, bf16[14,128,128]{2,1,0:T(8,128)(2,1)S(1)} %bitcast.44), custom_call_target="tpu_custom_call" | custom-call | tf_op jit(solution)/shard_map/pallas_call | solution.py:209
  131.5 2.8 %collective-permute-start.15 = (f32[1,128]{1,0:T(1,128)S(1)}, f32[1,128]{1,0:T(1,128)S(1)}, u32[]{:S(2)}, u32[]{:S(2)}) collective-permute-start(f32[1,128]{1,0:T(1,128)S(1)} %shard_map.76), channel_id=1, source_target_pairs={{0,28},{4,24},{8,20},{12,16},{16,12},{20,8},{24,4},{28,0},{1,29},{... | collective-permute-start | bytes 1544 | tf_op jit(solution)/shard_map/ppermute | solution.py:244
  134.3 0.9 shard_map.77
  135.2 6.6 %collective-permute-done.15 = f32[1,128]{1,0:T(1,128)S(1)} collective-permute-done((f32[1,128]{1,0:T(1,128)S(1)}, f32[1,128]{1,0:T(1,128)S(1)}, u32[]{:S(2)}, u32[]{:S(2)}) %collective-permute-start.15) | collective-permute-done | bytes 544 | tf_op jit(solution)/shard_map/ppermute | solution.py:244
  141.9 2.0 %collective-permute-done.17.refs_0_ = bf16[128,1792]{1,0:T(8,128)(2,1)S(1)} collective-permute-done((bf16[128,1792]{1,0:T(8,128)(2,1)S(1)}, bf16[128,1792]{1,0:T(8,128)(2,1)S(1)}, u32[]{:S(2)}, u32[]{:S(2)}) %collective-permute-start.17) | collective-permute-done | bytes 458784 | tf_op jit(solution)/shard_map/ppermute | solution.py:244
  143.9 0.9 shard_map.78
  144.9 0.1 collective-permute-start.18
  144.9 1.6 %collective-permute-start.19 = (f32[128]{0:T(128)S(1)}, f32[128]{0:T(128)S(1)}, u32[]{:S(2)}, u32[]{:S(2)}) collective-permute-start(f32[128]{0:T(128)S(1)} %bitcast.55), channel_id=1, source_target_pairs={{0,2},{1,3},{2,0},{3,1},{4,6},{5,7},{6,4},{7,5},{8,10},{9,11},{10,... | collective-permute-start | bytes 1544 | tf_op jit(solution)/shard_map/ppermute | solution.py:303
  146.5 0.3 collective-permute-start.20
  146.8 1.7 %collective-permute-done.19 = f32[128]{0:T(128)S(1)} collective-permute-done((f32[128]{0:T(128)S(1)}, f32[128]{0:T(128)S(1)}, u32[]{:S(2)}, u32[]{:S(2)}) %collective-permute-start.19) | collective-permute-done | bytes 544 | tf_op jit(solution)/shard_map/ppermute | solution.py:303
  148.6 0.9 collective-permute-done.20
  149.5 0.5 fusion.1
  (39 shorter events, 0.1 us)
Async XLA Ops:
  0.0 6.2 %copy-start = (s32[1,8]{1,0:T(1,128)S(1)}, s32[1,8]{1,0:T(1,128)}, u32[]{:S(2)}) copy-start(s32[1,8]{1,0:T(1,128)} %param.11) | copy-start | bytes 100
  0.0 26.4 %collective-permute-start = (bf16[128,4096]{1,0:T(8,128)(2,1)}, bf16[128,4096]{1,0:T(8,128)(2,1)S(1)}, u32[]{:S(2)}, u32[]{:S(2)}) collective-permute-start(bf16[128,4096]{1,0:T(8,128)(2,1)} %bitcast.50), channel_id=1, source_target_pairs={{0,8},{4,12},{8,0},{12,4},{16,24},{20,28},{24,16},{28,20},{1,9},{5... | collective-permute-start | bytes 3145736 | tf_op jit(solution)/shard_map/ppermute | solution.py:244
  3.0 25.0 %collective-permute-start.2 = (bf16[128,4096]{1,0:T(8,128)(2,1)}, bf16[128,4096]{1,0:T(8,128)(2,1)}, u32[]{:S(2)}, u32[]{:S(2)}) collective-permute-start(bf16[128,4096]{1,0:T(8,128)(2,1)} %bitcast.51), channel_id=1, source_target_pairs={{8,16},{12,20},{16,8},{20,12},{9,17},{13,21},{17,9},{21,13},{10,18... | collective-permute-start | bytes 3145736 | tf_op jit(solution)/shard_map/ppermute | solution.py:241
  4.7 34.9 %collective-permute-start.1 = (bf16[128,4096]{1,0:T(8,128)(2,1)}, bf16[128,4096]{1,0:T(8,128)(2,1)}, u32[]{:S(2)}, u32[]{:S(2)}) collective-permute-start(bf16[128,4096]{1,0:T(8,128)(2,1)} %bitcast.52), channel_id=1, source_target_pairs={{0,4},{4,0},{8,12},{12,8},{16,20},{20,16},{24,28},{28,24},{1,5},{5... | collective-permute-start | bytes 3145736 | tf_op jit(solution)/shard_map/ppermute | solution.py:244
  6.8 2.0 %copy-start.4 = (bf16[1,128,14336]{2,1,0:T(8,128)(2,1)S(1)}, bf16[1,128,14336]{2,1,0:T(8,128)(2,1)}, u32[]{:S(2)}) copy-start(bf16[1,128,14336]{2,1,0:T(8,128)(2,1)} %param.7) | copy-start | bytes 11010052
  8.9 3.0 %copy-start.8 = (bf16[1,32,128,128]{3,2,1,0:T(8,128)(2,1)S(1)}, bf16[1,32,128,128]{3,2,1,0:T(8,128)(2,1)}, u32[]{:S(2)}) copy-start(bf16[1,32,128,128]{3,2,1,0:T(8,128)(2,1)} %param.9) | copy-start | bytes 3145732
  8.9 3.0 %copy-start.9 = (bf16[1,128,4096]{2,1,0:T(8,128)(2,1)S(1)}, bf16[1,128,4096]{2,1,0:T(8,128)(2,1)}, u32[]{:S(2)}) copy-start(bf16[1,128,4096]{2,1,0:T(8,128)(2,1)} %param.6) | copy-start | bytes 3145732
  9.5 0.8 copy-start.10
  10.3 0.8 copy-start.12
  11.1 0.8 copy-start.14
  11.9 5.2 %copy-start.1 = (bf16[1,1792,4096]{2,1,0:T(8,128)(2,1)S(1)}, bf16[1,1792,4096]{2,1,0:T(8,128)(2,1)}, u32[]{:S(2)}) copy-start(bf16[1,1792,4096]{2,1,0:T(8,128)(2,1)} %param.8) | copy-start | bytes 44040196
  23.5 13.1 %copy-start.7 = (bf16[1,14,128,128]{3,2,1,0:T(8,128)(2,1)S(1)}, bf16[1,14,128,128]{3,2,1,0:T(8,128)(2,1)}, u32[]{:S(2)}) copy-start(bf16[1,14,128,128]{3,2,1,0:T(8,128)(2,1)} %param.10) | copy-start | bytes 1376260
  26.4 13.1 %collective-permute-start.3 = (bf16[128,4096]{1,0:T(8,128)(2,1)S(1)}, bf16[128,4096]{1,0:T(8,128)(2,1)}, u32[]{:S(2)}, u32[]{:S(2)}) collective-permute-start(bf16[128,4096]{1,0:T(8,128)(2,1)S(1)} %collective-permute-done.refs_0_), channel_id=1, source_target_pairs={{8,16},{12,20},{16,8},{20,12},{9,17},{13,21},{17,9},{21,13},{10,18... | collective-permute-start | bytes 3145736 | tf_op jit(solution)/shard_map/ppermute | solution.py:241
  28.1 27.6 %collective-permute-start.4 = (bf16[128,4096]{1,0:T(8,128)(2,1)}, bf16[128,4096]{1,0:T(8,128)(2,1)}, u32[]{:S(2)}, u32[]{:S(2)}) collective-permute-start(bf16[128,4096]{1,0:T(8,128)(2,1)} %collective-permute-done.2), channel_id=1, source_target_pairs={{0,8},{4,12},{8,0},{12,4},{16,24},{20,28},{24,16},{28,20},{1,9},{5... | collective-permute-start | bytes 3145736 | tf_op jit(solution)/shard_map/ppermute | solution.py:244
  31.7 2.7 %copy-start.15 = (bf16[128,1792]{1,0:T(8,128)(2,1)S(1)}, bf16[128,1792]{1,0:T(8,128)(2,1)}, u32[]{:S(2)}) copy-start(bf16[128,1792]{1,0:T(8,128)(2,1)} %copy-done.14) | copy-start | bytes 1376260
  32.8 50.4 %collective-permute-start.8 = (bf16[128,4992]{1,0:T(8,128)(2,1)S(1)}, bf16[128,4992]{1,0:T(8,128)(2,1)S(1)}, u32[]{:S(2)}, u32[]{:S(2)}) collective-permute-start(bf16[128,4992]{1,0:T(8,128)(2,1)S(1)} %pad_maximum_fusion), channel_id=1, source_target_pairs={{0,4},{4,0},{8,12},{12,8},{16,20},{20,16},{24,28},{28,24},{1,5},{5... | collective-permute-start | bytes 3833864 | tf_op jit(solution)/shard_map/ppermute | solution.py:244
  34.4 56.6 %collective-permute-start.7 = (bf16[128,1792]{1,0:T(8,128)(2,1)S(1)}, bf16[128,1792]{1,0:T(8,128)(2,1)S(1)}, u32[]{:S(2)}, u32[]{:S(2)}) collective-permute-start(bf16[128,1792]{1,0:T(8,128)(2,1)S(1)} %copy-done.15), channel_id=1, source_target_pairs={{0,28},{4,24},{8,20},{12,16},{16,12},{20,8},{24,4},{28,0},{1,29},{... | collective-permute-start | bytes 1376264 | tf_op jit(solution)/shard_map/ppermute | solution.py:244
  36.5 2.0 %copy-start.5 = (bf16[1,128,14336]{2,1,0:T(8,128)(2,1)S(1)}, bf16[1,128,14336]{2,1,0:T(8,128)(2,1)}, u32[]{:S(2)}) copy-start(bf16[1,128,14336]{2,1,0:T(8,128)(2,1)} %param.7) | copy-start | bytes 11010052
  38.6 24.1 %copy-start.13 = (bf16[128,1792]{1,0:T(8,128)(2,1)S(1)}, bf16[128,1792]{1,0:T(8,128)(2,1)}, u32[]{:S(2)}) copy-start(bf16[128,1792]{1,0:T(8,128)(2,1)} %copy-done.12) | copy-start | bytes 1376260
  39.5 28.5 %copy-start.11 = (bf16[128,1792]{1,0:T(8,128)(2,1)S(1)}, bf16[128,1792]{1,0:T(8,128)(2,1)}, u32[]{:S(2)}) copy-start(bf16[128,1792]{1,0:T(8,128)(2,1)} %copy-done.10) | copy-start | bytes 1376260
  55.6 42.3 %collective-permute-start.5 = (bf16[128,4096]{1,0:T(8,128)(2,1)}, bf16[128,4096]{1,0:T(8,128)(2,1)S(1)}, u32[]{:S(2)}, u32[]{:S(2)}) collective-permute-start(bf16[128,4096]{1,0:T(8,128)(2,1)} %collective-permute-done.3), channel_id=1, source_target_pairs={{0,8},{4,12},{8,0},{12,4},{16,24},{20,28},{24,16},{28,20},{1,9},{5... | collective-permute-start | bytes 3145736 | tf_op jit(solution)/shard_map/ppermute | solution.py:244
  62.7 35.2 %collective-permute-start.6 = (bf16[128,1792]{1,0:T(8,128)(2,1)S(1)}, bf16[128,1792]{1,0:T(8,128)(2,1)S(1)}, u32[]{:S(2)}, u32[]{:S(2)}) collective-permute-start(bf16[128,1792]{1,0:T(8,128)(2,1)S(1)} %copy-done.13), channel_id=1, source_target_pairs={{0,24},{4,28},{8,16},{12,20},{16,8},{20,12},{24,0},{28,4},{1,25},{... | collective-permute-start | bytes 1376264 | tf_op jit(solution)/shard_map/ppermute | solution.py:244
  68.2 33.9 %collective-permute-start.10 = (bf16[128,4992]{1,0:T(8,128)(2,1)S(1)}, bf16[128,4992]{1,0:T(8,128)(2,1)S(1)}, u32[]{:S(2)}, u32[]{:S(2)}) collective-permute-start(bf16[128,4992]{1,0:T(8,128)(2,1)S(1)} %pad_maximum_fusion.1), channel_id=1, source_target_pairs={{0,4},{4,0},{8,12},{12,8},{16,20},{20,16},{24,28},{28,24},{1,5},{5... | collective-permute-start | bytes 3833864 | tf_op jit(solution)/shard_map/ppermute | solution.py:244
  69.7 5.2 %copy-start.2 = (bf16[1,1792,4096]{2,1,0:T(8,128)(2,1)S(1)}, bf16[1,1792,4096]{2,1,0:T(8,128)(2,1)}, u32[]{:S(2)}) copy-start(bf16[1,1792,4096]{2,1,0:T(8,128)(2,1)} %param.8) | copy-start | bytes 44040196
  74.9 8.3 %copy-start.3 = (bf16[1,1792,4096]{2,1,0:T(8,128)(2,1)S(1)}, bf16[1,1792,4096]{2,1,0:T(8,128)(2,1)}, u32[]{:S(2)}) copy-start(bf16[1,1792,4096]{2,1,0:T(8,128)(2,1)} %param.8) | copy-start | bytes 44040196
  98.2 23.0 %collective-permute-start.9 = (bf16[128,4096]{1,0:T(8,128)(2,1)S(1)}, bf16[128,4096]{1,0:T(8,128)(2,1)S(1)}, u32[]{:S(2)}, u32[]{:S(2)}) collective-permute-start(bf16[128,4096]{1,0:T(8,128)(2,1)S(1)} %broadcast_select_fusion.refs_0_), channel_id=1, source_target_pairs={{0,4},{4,0},{8,12},{12,8},{16,20},{20,16},{24,28},{28,24},{1,5},{5... | collective-permute-start | bytes 3145736 | tf_op jit(solution)/shard_map/ppermute | solution.py:244
  99.7 21.4 %collective-permute-start.13 = (bf16[128,1792]{1,0:T(8,128)(2,1)S(1)}, bf16[128,1792]{1,0:T(8,128)(2,1)S(1)}, u32[]{:S(2)}, u32[]{:S(2)}) collective-permute-start(bf16[128,1792]{1,0:T(8,128)(2,1)S(1)} %shard_map.68), channel_id=1, source_target_pairs={{0,8},{4,12},{8,0},{12,4},{16,24},{20,28},{24,16},{28,20},{1,9},{5... | collective-permute-start | bytes 1376264 | tf_op jit(solution)/shard_map/ppermute | solution.py:244
  99.7 21.4 %collective-permute-start.14 = (bf16[128,1792]{1,0:T(8,128)(2,1)S(1)}, bf16[128,1792]{1,0:T(8,128)(2,1)S(1)}, u32[]{:S(2)}, u32[]{:S(2)}) collective-permute-start(bf16[128,1792]{1,0:T(8,128)(2,1)S(1)} %shard_map.71), channel_id=1, source_target_pairs={{0,16},{4,20},{8,24},{12,28},{16,0},{20,4},{24,8},{28,12},{1,17},{... | collective-permute-start | bytes 1376264 | tf_op jit(solution)/shard_map/ppermute | solution.py:244
  109.2 10.5 %collective-permute-start.11 = (f32[1,128]{1,0:T(1,128)S(1)}, f32[1,128]{1,0:T(1,128)S(1)}, u32[]{:S(2)}, u32[]{:S(2)}) collective-permute-start(f32[1,128]{1,0:T(1,128)S(1)} %shard_map.74), channel_id=1, source_target_pairs={{0,24},{4,28},{8,16},{12,20},{16,8},{20,12},{24,0},{28,4},{1,25},{... | collective-permute-start | bytes 1544 | tf_op jit(solution)/shard_map/ppermute | solution.py:244
  111.7 9.4 %collective-permute-start.12 = (f32[1,128]{1,0:T(1,128)S(1)}, f32[1,128]{1,0:T(1,128)S(1)}, u32[]{:S(2)}, u32[]{:S(2)}) collective-permute-start(f32[1,128]{1,0:T(1,128)S(1)} %shard_map.75), channel_id=1, source_target_pairs={{0,4},{4,0},{8,12},{12,8},{16,20},{20,16},{24,28},{28,24},{1,5},{5... | collective-permute-start | bytes 1544 | tf_op jit(solution)/shard_map/ppermute | solution.py:244
  121.1 20.7 %collective-permute-start.16 = (bf16[128,1792]{1,0:T(8,128)(2,1)S(1)}, bf16[128,1792]{1,0:T(8,128)(2,1)S(1)}, u32[]{:S(2)}, u32[]{:S(2)}) collective-permute-start(bf16[128,1792]{1,0:T(8,128)(2,1)S(1)} %shard_map.70), channel_id=1, source_target_pairs={{0,12},{4,8},{8,4},{12,0},{16,28},{20,24},{24,20},{28,16},{1,13},{... | collective-permute-start | bytes 1376264 | tf_op jit(solution)/shard_map/ppermute | solution.py:244
  122.5 21.4 %collective-permute-start.17 = (bf16[128,1792]{1,0:T(8,128)(2,1)S(1)}, bf16[128,1792]{1,0:T(8,128)(2,1)S(1)}, u32[]{:S(2)}, u32[]{:S(2)}) collective-permute-start(bf16[128,1792]{1,0:T(8,128)(2,1)S(1)} %shard_map.73), channel_id=1, source_target_pairs={{0,20},{4,16},{8,28},{12,24},{16,4},{20,0},{24,12},{28,8},{1,21},{... | collective-permute-start | bytes 1376264 | tf_op jit(solution)/shard_map/ppermute | solution.py:244
  124.7 9.6 %copy-start.6 = (bf16[1,128,14336]{2,1,0:T(8,128)(2,1)S(1)}, bf16[1,128,14336]{2,1,0:T(8,128)(2,1)}, u32[]{:S(2)}) copy-start(bf16[1,128,14336]{2,1,0:T(8,128)(2,1)} %param.7) | copy-start | bytes 11010052
  131.5 10.3 %collective-permute-start.15 = (f32[1,128]{1,0:T(1,128)S(1)}, f32[1,128]{1,0:T(1,128)S(1)}, u32[]{:S(2)}, u32[]{:S(2)}) collective-permute-start(f32[1,128]{1,0:T(1,128)S(1)} %shard_map.76), channel_id=1, source_target_pairs={{0,28},{4,24},{8,20},{12,16},{16,12},{20,8},{24,4},{28,0},{1,29},{... | collective-permute-start | bytes 1544 | tf_op jit(solution)/shard_map/ppermute | solution.py:244
  144.9 1.9 %collective-permute-start.18 = (f32[128]{0:T(128)S(1)}, f32[128]{0:T(128)S(1)}, u32[]{:S(2)}, u32[]{:S(2)}) collective-permute-start(f32[128]{0:T(128)S(1)} %bitcast.54), channel_id=1, source_target_pairs={{0,1},{1,0},{2,3},{3,2},{4,5},{5,4},{6,7},{7,6},{8,9},{9,8},{10,11... | collective-permute-start | bytes 1544 | tf_op jit(solution)/shard_map/ppermute | solution.py:303
  144.9 3.6 %collective-permute-start.19 = (f32[128]{0:T(128)S(1)}, f32[128]{0:T(128)S(1)}, u32[]{:S(2)}, u32[]{:S(2)}) collective-permute-start(f32[128]{0:T(128)S(1)} %bitcast.55), channel_id=1, source_target_pairs={{0,2},{1,3},{2,0},{3,1},{4,6},{5,7},{6,4},{7,5},{8,10},{9,11},{10,... | collective-permute-start | bytes 1544 | tf_op jit(solution)/shard_map/ppermute | solution.py:303
  146.5 3.0 %collective-permute-start.20 = (f32[128]{0:T(128)S(1)}, f32[128]{0:T(128)S(1)}, u32[]{:S(2)}, u32[]{:S(2)}) collective-permute-start(f32[128]{0:T(128)S(1)} %bitcast.56), channel_id=1, source_target_pairs={{0,3},{1,2},{2,1},{3,0},{4,7},{5,6},{6,5},{7,4},{8,11},{9,10},{10,... | collective-permute-start | bytes 1544 | tf_op jit(solution)/shard_map/ppermute | solution.py:303

commit v6 on v5

--- a/solution.py
+++ b/solution.py
@@ -86,7 +86,7 @@
     out[...] = lay(total)
 
 
-def meet_kernel(count, order, *refs):
+def meet_kernel(count, *refs):
     total = jnp.zeros((refs[0].shape[0], TILE), jnp.float32)
     for came, piece in zip(refs[:count], refs[count:-1]):
         for part in blocks_of(piece.shape[1]):
@@ -120,13 +120,17 @@
     return small(score_kernel, order, specs, rows, found, values, basis)
 
 
-def meet(come, order, grads):
+def meet(come, pieces):
     offsets = list(come)
-    rows, units = come[offsets[0]].shape
-    specs = [pl.BlockSpec((rows, units), lambda i, order: (0, 0))] * len(offsets)
-    specs += [pl.BlockSpec((rows, units), lambda i, order, j=j: (0, order[j])) for j in offsets]
-    args = [come[j] for j in offsets] + [grads] * len(offsets)
-    return small(functools.partial(meet_kernel, len(offsets)), order, specs, rows, *args)
+    vmem = pl.BlockSpec(memory_space=pltpu.VMEM)
+    return pl.pallas_call(
+        functools.partial(meet_kernel, len(offsets)),
+        in_specs=[vmem] * (2 * len(offsets)),
+        out_specs=vmem,
+        out_shape=jax.ShapeDtypeStruct((1, pieces[offsets[0]].shape[0]), jnp.float32),
+        compiler_params=pltpu.CompilerParams(vmem_limit_bytes=16 * MIB),
+        cost_estimate=free,
+    )(*[come[j] for j in offsets], *[pieces[j] for j in offsets])
 
 
 def back_kernel(found, basis, out):
@@ -255,7 +259,7 @@
     wide, cut = own.shape[1], units // TILE // 2 * TILE
     got, come = {}, {}
     a1, a2, a3 = line(own, 1), middle(own), sideways(own)
-    pieces = pack(aside(0) + [three] + aside(3), order, grads, units)
+    pieces = pack(list(range(1, size)), order, grads, units)
     p_own = project([own], turn_in, query)
     a1, pieces, p_own = hold((a1, pieces, p_own))
     join = lambda value, cols: [swap(jnp.concatenate([value, pieces[j][:, cols]], axis=1), j) for j in range(1, across)]
@@ -293,9 +297,9 @@
         sums[three + j] = project_score(side3[j - 1], turn_in, query, got[three + j], turn_out)
     for value in send(sums, list(sums)).values():
         total += value
-    total += meet({j: come[j] for j in (two, one)}, order, grads)
+    total += meet({j: come[j] for j in (two, one)}, pieces)
     total, come = hold((total, come))
-    total += meet({j: come[j] for j in late}, order, grads)
+    total += meet({j: come[j] for j in late}, pieces)
     mine, layers = total[0], lax.axis_size("layer")
     if layers & (layers - 1) or layers > 4:
         return lax.psum(mine, "layer")

time: 150 us -> 150 us (level)
  waiting for transfers between devices: 45.4 us -> 47.2 us
  local copies, waits for them, and re-layouts: 18.5 us -> 17 us
    pallas_call x4 -> x2, Pallas kernels: 3.71 us -> 1.82 us  [small(): pl.pallas_call(kernel, grid_spec=pltpu.PrefetchScalarGridSpec(num_scalar_...]
    ppermute x16, waiting for transfers between devices: 42.7 us -> 44.5 us  [swap(): return lax.ppermute(value, 'seq', [(s, s ^ j) for s in range(size)])]
    unnamed x32 -> x46, local copies, waits for them, and re-layouts: 16.8 us -> 15.4 us
  transfers between devices with their start and end apart: 21 -> 21, of which waited for: 9 -> 9; matrix products, arithmetic and copies ran while one was open for 2% -> 2% of each run, Pallas kernels for 27% -> 26%
where the time goes in v6:
time: 150 us; the launch traced here: 149 us
  waiting for transfers between devices  47.2 us (31%)
  starting transfers between devices  42.7 us (28%)
  Pallas kernels  39.9 us (27%)
  local copies, waits for them, and re-layouts  17 us (11%)
  other arithmetic  2.28 us (2%)
    ppermute x16, waiting for transfers between devices, swap(): return lax.ppermute(value, 'seq', [(s, s ^ j) for s in range(size)])  44.5 us
    ppermute x16, starting transfers between devices, swap(): return lax.ppermute(value, 'seq', [(s, s ^ j) for s in range(size)])  37.5 us
    pallas_call x4, Pallas kernels, project(): pl.pallas_call(functools.partial(project_kernel, count), grid=(units // s...  26.5 us
    unnamed x46, local copies, waits for them, and re-layouts  15.4 us
    pallas_call x1, Pallas kernels, project_score(): pl.pallas_call(project_score_kernel, grid=(units // step,), in_specs=[who...  6.8 us
    ppermute x2, starting transfers between devices, move(): return lax.ppermute(value, 'seq', pairs)  3.28 us
  transfers between devices with their start and end apart: 21, of which 9 were waited for; matrix products, arithmetic and copies ran while one was open for 2% of the time, Pallas kernels for 26%

profile of v6, /device:TPU:0, one launch (start us, length us, event | category | flops | bytes accessed | tf_op | source)
XLA Modules:
  0.0 149.4 jit_solution(555577889420794581)
XLA Ops:
  0.0 3.0 %collective-permute-start = (bf16[128,4096]{1,0:T(8,128)(2,1)}, bf16[128,4096]{1,0:T(8,128)(2,1)S(1)}, u32[]{:S(2)}, u32[]{:S(2)}) collective-permute-start(bf16[128,4096]{1,0:T(8,128)(2,1)} %bitcast.50), channel_id=1, source_target_pairs={{0,8},{4,12},{8,0},{12,4},{16,24},{20,28},{24,16},{28,20},{1,9},{5... | collective-permute-start | bytes 3145736 | tf_op jit(solution)/shard_map/ppermute | solution.py:248
  3.0 1.6 %collective-permute-start.2 = (bf16[128,4096]{1,0:T(8,128)(2,1)}, bf16[128,4096]{1,0:T(8,128)(2,1)}, u32[]{:S(2)}, u32[]{:S(2)}) collective-permute-start(bf16[128,4096]{1,0:T(8,128)(2,1)} %bitcast.51), channel_id=1, source_target_pairs={{8,16},{12,20},{16,8},{20,12},{9,17},{13,21},{17,9},{21,13},{10,18... | collective-permute-start | bytes 3145736 | tf_op jit(solution)/shard_map/ppermute | solution.py:245
  4.7 1.5 collective-permute-start.1
  6.2 0.6 gather_fusion
  6.8 0.0 copy-start.4
  6.9 2.0 %copy-done.4 = bf16[1,128,14336]{2,1,0:T(8,128)(2,1)S(1)} copy-done((bf16[1,128,14336]{2,1,0:T(8,128)(2,1)S(1)}, bf16[1,128,14336]{2,1,0:T(8,128)(2,1)}, u32[]{:S(2)}) %copy-start.4) | copy-done | bytes 3670040
  8.9 0.8 shard_map.64
  9.7 0.8 copy-done.11
  10.4 0.8 copy-done.15
  11.2 4.0 %copy-done.1 = bf16[1,1792,4096]{2,1,0:T(8,128)(2,1)S(1)} copy-done((bf16[1,1792,4096]{2,1,0:T(8,128)(2,1)S(1)}, bf16[1,1792,4096]{2,1,0:T(8,128)(2,1)}, u32[]{:S(2)}) %copy-start.1) | copy-done | bytes 14680088
  15.2 0.2 copy-done.7
  15.4 0.3 copy-done.8
  15.7 6.4 %shard_map.65.found = f32[1,128,1792]{2,1,0:T(8,128)S(1)} custom-call(bf16[128,4096]{1,0:T(8,128)(2,1)S(1)} %bitcast.53, bf16[32,128,128]{2,1,0:T(8,128)(2,1)S(1)} %bitcast.45, bf16[1792,4096]{1,0:T(8,128)(2,1)S(1)} %bitcast.24), custom_call_target="tpu_custom_call" | custom-call | tf_op jit(solution)/shard_map/pallas_call | solution.py:43
  22.2 0.0 copy-start.6
  22.3 4.1 %collective-permute-done.refs_0_ = bf16[128,4096]{1,0:T(8,128)(2,1)S(1)} collective-permute-done((bf16[128,4096]{1,0:T(8,128)(2,1)}, bf16[128,4096]{1,0:T(8,128)(2,1)S(1)}, u32[]{:S(2)}, u32[]{:S(2)}) %collective-permute-start) | collective-permute-done | bytes 1048608 | tf_op jit(solution)/shard_map/ppermute | solution.py:248
  26.4 1.6 %collective-permute-start.3 = (bf16[128,4096]{1,0:T(8,128)(2,1)S(1)}, bf16[128,4096]{1,0:T(8,128)(2,1)}, u32[]{:S(2)}, u32[]{:S(2)}) collective-permute-start(bf16[128,4096]{1,0:T(8,128)(2,1)S(1)} %collective-permute-done.refs_0_), channel_id=1, source_target_pairs={{8,16},{12,20},{16,8},{20,12},{9,17},{13,21},{17,9},{21,13},{10,18... | collective-permute-start | bytes 3145736 | tf_op jit(solution)/shard_map/ppermute | solution.py:245
  28.0 0.0 collective-permute-done.2
  28.0 3.7 %collective-permute-start.4 = (bf16[128,4096]{1,0:T(8,128)(2,1)}, bf16[128,4096]{1,0:T(8,128)(2,1)}, u32[]{:S(2)}, u32[]{:S(2)}) collective-permute-start(bf16[128,4096]{1,0:T(8,128)(2,1)} %collective-permute-done.2), channel_id=1, source_target_pairs={{0,8},{4,12},{8,0},{12,4},{16,24},{20,28},{24,16},{28,20},{1,9},{5... | collective-permute-start | bytes 3145736 | tf_op jit(solution)/shard_map/ppermute | solution.py:248
  31.7 1.0 slice.6
  32.7 0.1 pad_maximum_fusion
  32.8 1.6 %collective-permute-start.8 = (bf16[128,4992]{1,0:T(8,128)(2,1)S(1)}, bf16[128,4992]{1,0:T(8,128)(2,1)S(1)}, u32[]{:S(2)}, u32[]{:S(2)}) collective-permute-start(bf16[128,4992]{1,0:T(8,128)(2,1)S(1)} %pad_maximum_fusion), channel_id=1, source_target_pairs={{0,4},{4,0},{8,12},{12,8},{16,20},{20,16},{24,28},{28,24},{1,5},{5... | collective-permute-start | bytes 3833864 | tf_op jit(solution)/shard_map/ppermute | solution.py:248
  34.4 2.2 %collective-permute-start.7 = (bf16[128,1792]{1,0:T(8,128)(2,1)S(1)}, bf16[128,1792]{1,0:T(8,128)(2,1)S(1)}, u32[]{:S(2)}, u32[]{:S(2)}) collective-permute-start(bf16[128,1792]{1,0:T(8,128)(2,1)S(1)} %copy-done.22), channel_id=1, source_target_pairs={{0,28},{4,24},{8,20},{12,16},{16,12},{20,8},{24,4},{28,0},{1,29},{... | collective-permute-start | bytes 1376264 | tf_op jit(solution)/shard_map/ppermute | solution.py:248
  36.6 2.0 %copy-done.5 = bf16[1,128,14336]{2,1,0:T(8,128)(2,1)S(1)} copy-done((bf16[1,128,14336]{2,1,0:T(8,128)(2,1)S(1)}, bf16[1,128,14336]{2,1,0:T(8,128)(2,1)}, u32[]{:S(2)}) %copy-start.5) | copy-done | bytes 3670040
  38.6 0.9 shard_map.66
  39.5 16.1 %collective-permute-done.4 = bf16[128,4096]{1,0:T(8,128)(2,1)} collective-permute-done((bf16[128,4096]{1,0:T(8,128)(2,1)}, bf16[128,4096]{1,0:T(8,128)(2,1)}, u32[]{:S(2)}, u32[]{:S(2)}) %collective-permute-start.4) | collective-permute-done | bytes 1048608 | tf_op jit(solution)/shard_map/ppermute | solution.py:248
  55.6 7.1 %collective-permute-start.5 = (bf16[128,4096]{1,0:T(8,128)(2,1)}, bf16[128,4096]{1,0:T(8,128)(2,1)S(1)}, u32[]{:S(2)}, u32[]{:S(2)}) collective-permute-start(bf16[128,4096]{1,0:T(8,128)(2,1)} %collective-permute-done.3), channel_id=1, source_target_pairs={{0,8},{4,12},{8,0},{12,4},{16,24},{20,28},{24,16},{28,20},{1,9},{5... | collective-permute-start | bytes 3145736 | tf_op jit(solution)/shard_map/ppermute | solution.py:248
  62.7 4.0 %collective-permute-start.6 = (bf16[128,1792]{1,0:T(8,128)(2,1)S(1)}, bf16[128,1792]{1,0:T(8,128)(2,1)S(1)}, u32[]{:S(2)}, u32[]{:S(2)}) collective-permute-start(bf16[128,1792]{1,0:T(8,128)(2,1)S(1)} %copy-done.20), channel_id=1, source_target_pairs={{0,24},{4,28},{8,16},{12,20},{16,8},{20,12},{24,0},{28,4},{1,25},{... | collective-permute-start | bytes 1376264 | tf_op jit(solution)/shard_map/ppermute | solution.py:248
  66.7 1.3 broadcast_select_fusion.1.refs_0_
  68.1 0.1 pad_maximum_fusion.1
  68.2 1.6 %collective-permute-start.10 = (bf16[128,4992]{1,0:T(8,128)(2,1)S(1)}, bf16[128,4992]{1,0:T(8,128)(2,1)S(1)}, u32[]{:S(2)}, u32[]{:S(2)}) collective-permute-start(bf16[128,4992]{1,0:T(8,128)(2,1)S(1)} %pad_maximum_fusion.1), channel_id=1, source_target_pairs={{0,4},{4,0},{8,12},{12,8},{16,20},{20,16},{24,28},{28,24},{1,5},{5... | collective-permute-start | bytes 3833864 | tf_op jit(solution)/shard_map/ppermute | solution.py:248
  69.8 5.2 %copy-done.2 = bf16[1,1792,4096]{2,1,0:T(8,128)(2,1)S(1)} copy-done((bf16[1,1792,4096]{2,1,0:T(8,128)(2,1)S(1)}, bf16[1,1792,4096]{2,1,0:T(8,128)(2,1)}, u32[]{:S(2)}) %copy-start.2) | copy-done | bytes 14680088
  74.9 7.5 %shard_map.67.found = f32[2,128,1792]{2,1,0:T(8,128)S(1)} custom-call(bf16[128,4096]{1,0:T(8,128)(2,1)S(1)} %collective-permute-done.refs_0_, bf16[128,4096]{1,0:T(8,128)(2,1)} %collective-permute-done.1.refs_1_, bf16[32,128,128]{2,1,0:T(8,128)(2,1)S(1)} %bitcast.46, bf16[1792,4096]{1,0:T(8,128)(2,1)S(1)} %bitcast.25), custom_call_target="tpu_custom_call" | custom-call | tf_op jit(solution)/shard_map/pallas_call | solution.py:43
  82.5 0.7 shard_map.68
  83.2 6.3 %shard_map.69.found = f32[2,128,1792]{2,1,0:T(8,128)S(1)} custom-call(bf16[128,4096]{1,0:T(8,128)(2,1)S(1)} %broadcast_select_fusion.1.refs_0_, bf16[128,4992]{1,0:T(8,128)(2,1)S(1)} %collective-permute-done.8.refs_1_.first, bf16[32,128,128]{2,1,0:T(8,128)(2,1)S(1)} %bitcast.47, bf16[1792,4096]{1,0:T(8,128)(2,1)S(1)} %bitcast.26), custom_call_target="tpu_custom_call" | custom-call | tf_op jit(solution)/shard_map/pallas_call | solution.py:43
  89.5 0.7 shard_map.70
  90.3 0.7 shard_map.71
  91.0 7.0 %collective-permute-done.6.piece = bf16[128,1792]{1,0:T(8,128)(2,1)S(1)} collective-permute-done((bf16[128,1792]{1,0:T(8,128)(2,1)S(1)}, bf16[128,1792]{1,0:T(8,128)(2,1)S(1)}, u32[]{:S(2)}, u32[]{:S(2)}) %collective-permute-start.6) | collective-permute-done | bytes 458784 | tf_op jit(solution)/shard_map/ppermute | solution.py:248
  98.0 0.2 broadcast_select_fusion.refs_0_
  98.2 1.6 %collective-permute-start.9 = (bf16[128,4096]{1,0:T(8,128)(2,1)S(1)}, bf16[128,4096]{1,0:T(8,128)(2,1)S(1)}, u32[]{:S(2)}, u32[]{:S(2)}) collective-permute-start(bf16[128,4096]{1,0:T(8,128)(2,1)S(1)} %broadcast_select_fusion.refs_0_), channel_id=1, source_target_pairs={{0,4},{4,0},{8,12},{12,8},{16,20},{20,16},{24,28},{28,24},{1,5},{5... | collective-permute-start | bytes 3145736 | tf_op jit(solution)/shard_map/ppermute | solution.py:248
  99.7 0.0 collective-permute-start.13
  99.7 2.3 %collective-permute-start.14 = (bf16[128,1792]{1,0:T(8,128)(2,1)S(1)}, bf16[128,1792]{1,0:T(8,128)(2,1)S(1)}, u32[]{:S(2)}, u32[]{:S(2)}) collective-permute-start(bf16[128,1792]{1,0:T(8,128)(2,1)S(1)} %shard_map.71), channel_id=1, source_target_pairs={{0,16},{4,20},{8,24},{12,28},{16,0},{20,4},{24,8},{28,12},{1,17},{... | collective-permute-start | bytes 1376264 | tf_op jit(solution)/shard_map/ppermute | solution.py:248
  102.1 0.0 collective-permute-done.10.refs_1_.second
  102.1 6.2 %shard_map.72.found = f32[2,128,1792]{2,1,0:T(8,128)S(1)} custom-call(bf16[128,4096]{1,0:T(8,128)(2,1)S(1)} %broadcast_select_fusion.refs_0_, bf16[128,4992]{1,0:T(8,128)(2,1)S(1)} %collective-permute-done.10.refs_1_.second, bf16[32,128,128]{2,1,0:T(8,128)(2,1)S(1)} %bitcast.48, bf16[1792,4096]{1,0:T(8,128)(2,1)S(1)} %bitcast.27), custom_call_target="tpu_custom_call" | custom-call | tf_op jit(solution)/shard_map/pallas_call | solution.py:43
  108.3 0.9 shard_map.74
  109.2 2.1 %collective-permute-start.11 = (f32[1,128]{1,0:T(1,128)S(1)}, f32[1,128]{1,0:T(1,128)S(1)}, u32[]{:S(2)}, u32[]{:S(2)}) collective-permute-start(f32[1,128]{1,0:T(1,128)S(1)} %shard_map.74), channel_id=1, source_target_pairs={{0,24},{4,28},{8,16},{12,20},{16,8},{20,12},{24,0},{28,4},{1,25},{... | collective-permute-start | bytes 1544 | tf_op jit(solution)/shard_map/ppermute | solution.py:248
  111.3 0.4 shard_map.75
  111.7 0.6 collective-permute-start.12
  112.3 0.7 shard_map.73
  113.1 6.6 %collective-permute-done.11 = f32[1,128]{1,0:T(1,128)S(1)} collective-permute-done((f32[1,128]{1,0:T(1,128)S(1)}, f32[1,128]{1,0:T(1,128)S(1)}, u32[]{:S(2)}, u32[]{:S(2)}) %collective-permute-start.11) | collective-permute-done | bytes 544 | tf_op jit(solution)/shard_map/ppermute | solution.py:248
  119.7 1.4 collective-permute-done.12
  121.2 1.3 collective-permute-start.16
  122.5 2.3 %collective-permute-start.17 = (bf16[128,1792]{1,0:T(8,128)(2,1)S(1)}, bf16[128,1792]{1,0:T(8,128)(2,1)S(1)}, u32[]{:S(2)}, u32[]{:S(2)}) collective-permute-start(bf16[128,1792]{1,0:T(8,128)(2,1)S(1)} %shard_map.73), channel_id=1, source_target_pairs={{0,20},{4,16},{8,28},{12,24},{16,4},{20,0},{24,12},{28,8},{1,21},{... | collective-permute-start | bytes 1376264 | tf_op jit(solution)/shard_map/ppermute | solution.py:248
  124.8 6.8 %shard_map.76 = f32[1,128]{1,0:T(1,128)S(1)} custom-call(bf16[128,4096]{1,0:T(8,128)(2,1)S(1)} %collective-permute-done.9.chunk, bf16[32,128,128]{2,1,0:T(8,128)(2,1)S(1)} %bitcast.49, bf16[1792,4096]{1,0:T(8,128)(2,1)S(1)} %bitcast.28, bf16[128,1792]{1,0:T(8,128)(2,1)S(1)} %collective-permute-done.7.piece, bf16[14,128,128]{2,1,0:T(8,128)(2,1)S(1)} %bitcast.44), custom_call_target="tpu_custom_call" | custom-call | tf_op jit(solution)/shard_map/pallas_call | solution.py:213
  131.6 2.8 %collective-permute-start.15 = (f32[1,128]{1,0:T(1,128)S(1)}, f32[1,128]{1,0:T(1,128)S(1)}, u32[]{:S(2)}, u32[]{:S(2)}) collective-permute-start(f32[1,128]{1,0:T(1,128)S(1)} %shard_map.76), channel_id=1, source_target_pairs={{0,28},{4,24},{8,20},{12,16},{16,12},{20,8},{24,4},{28,0},{1,29},{... | collective-permute-start | bytes 1544 | tf_op jit(solution)/shard_map/ppermute | solution.py:248
  134.3 0.3 shard_map.77
  134.7 7.2 %collective-permute-done.15 = f32[1,128]{1,0:T(1,128)S(1)} collective-permute-done((f32[1,128]{1,0:T(1,128)S(1)}, f32[1,128]{1,0:T(1,128)S(1)}, u32[]{:S(2)}, u32[]{:S(2)}) %collective-permute-start.15) | collective-permute-done | bytes 544 | tf_op jit(solution)/shard_map/ppermute | solution.py:248
  141.9 2.0 %collective-permute-done.17.refs_0_ = bf16[128,1792]{1,0:T(8,128)(2,1)S(1)} collective-permute-done((bf16[128,1792]{1,0:T(8,128)(2,1)S(1)}, bf16[128,1792]{1,0:T(8,128)(2,1)S(1)}, u32[]{:S(2)}, u32[]{:S(2)}) %collective-permute-start.17) | collective-permute-done | bytes 458784 | tf_op jit(solution)/shard_map/ppermute | solution.py:248
  143.9 0.3 shard_map.78
  144.3 0.1 collective-permute-start.18
  144.4 1.6 %collective-permute-start.19 = (f32[128]{0:T(128)S(1)}, f32[128]{0:T(128)S(1)}, u32[]{:S(2)}, u32[]{:S(2)}) collective-permute-start(f32[128]{0:T(128)S(1)} %bitcast.55), channel_id=1, source_target_pairs={{0,2},{1,3},{2,0},{3,1},{4,6},{5,7},{6,4},{7,5},{8,10},{9,11},{10,... | collective-permute-start | bytes 1544 | tf_op jit(solution)/shard_map/ppermute | solution.py:307
  146.0 0.3 collective-permute-start.20
  146.2 1.7 %collective-permute-done.19 = f32[128]{0:T(128)S(1)} collective-permute-done((f32[128]{0:T(128)S(1)}, f32[128]{0:T(128)S(1)}, u32[]{:S(2)}, u32[]{:S(2)}) %collective-permute-start.19) | collective-permute-done | bytes 544 | tf_op jit(solution)/shard_map/ppermute | solution.py:307
  148.0 0.9 collective-permute-done.20
  148.9 0.5 fusion.1
  (53 shorter events, 0.2 us)
Async XLA Ops:
  0.0 6.2 %copy-start = (s32[1,8]{1,0:T(1,128)S(1)}, s32[1,8]{1,0:T(1,128)}, u32[]{:S(2)}) copy-start(s32[1,8]{1,0:T(1,128)} %param.11) | copy-start | bytes 100
  0.0 26.4 %collective-permute-start = (bf16[128,4096]{1,0:T(8,128)(2,1)}, bf16[128,4096]{1,0:T(8,128)(2,1)S(1)}, u32[]{:S(2)}, u32[]{:S(2)}) collective-permute-start(bf16[128,4096]{1,0:T(8,128)(2,1)} %bitcast.50), channel_id=1, source_target_pairs={{0,8},{4,12},{8,0},{12,4},{16,24},{20,28},{24,16},{28,20},{1,9},{5... | collective-permute-start | bytes 3145736 | tf_op jit(solution)/shard_map/ppermute | solution.py:248
  3.0 25.0 %collective-permute-start.2 = (bf16[128,4096]{1,0:T(8,128)(2,1)}, bf16[128,4096]{1,0:T(8,128)(2,1)}, u32[]{:S(2)}, u32[]{:S(2)}) collective-permute-start(bf16[128,4096]{1,0:T(8,128)(2,1)} %bitcast.51), channel_id=1, source_target_pairs={{8,16},{12,20},{16,8},{20,12},{9,17},{13,21},{17,9},{21,13},{10,18... | collective-permute-start | bytes 3145736 | tf_op jit(solution)/shard_map/ppermute | solution.py:245
  4.7 34.9 %collective-permute-start.1 = (bf16[128,4096]{1,0:T(8,128)(2,1)}, bf16[128,4096]{1,0:T(8,128)(2,1)}, u32[]{:S(2)}, u32[]{:S(2)}) collective-permute-start(bf16[128,4096]{1,0:T(8,128)(2,1)} %bitcast.52), channel_id=1, source_target_pairs={{0,4},{4,0},{8,12},{12,8},{16,20},{20,16},{24,28},{28,24},{1,5},{5... | collective-permute-start | bytes 3145736 | tf_op jit(solution)/shard_map/ppermute | solution.py:248
  6.8 2.0 %copy-start.4 = (bf16[1,128,14336]{2,1,0:T(8,128)(2,1)S(1)}, bf16[1,128,14336]{2,1,0:T(8,128)(2,1)}, u32[]{:S(2)}) copy-start(bf16[1,128,14336]{2,1,0:T(8,128)(2,1)} %param.7) | copy-start | bytes 11010052
  8.9 6.3 %copy-start.1 = (bf16[1,1792,4096]{2,1,0:T(8,128)(2,1)S(1)}, bf16[1,1792,4096]{2,1,0:T(8,128)(2,1)}, u32[]{:S(2)}) copy-start(bf16[1,1792,4096]{2,1,0:T(8,128)(2,1)} %param.8) | copy-start | bytes 44040196
  8.9 6.6 %copy-start.7 = (bf16[1,32,128,128]{3,2,1,0:T(8,128)(2,1)S(1)}, bf16[1,32,128,128]{3,2,1,0:T(8,128)(2,1)}, u32[]{:S(2)}) copy-start(bf16[1,32,128,128]{3,2,1,0:T(8,128)(2,1)} %param.9) | copy-start | bytes 3145732
  8.9 6.9 %copy-start.8 = (bf16[1,128,4096]{2,1,0:T(8,128)(2,1)S(1)}, bf16[1,128,4096]{2,1,0:T(8,128)(2,1)}, u32[]{:S(2)}) copy-start(bf16[1,128,4096]{2,1,0:T(8,128)(2,1)} %param.6) | copy-start | bytes 3145732
  9.6 0.8 copy-start.11
  10.4 0.8 copy-start.15
  11.2 11.0 %copy-start.9 = (bf16[128,1792]{1,0:T(8,128)(2,1)}, bf16[128,1792]{1,0:T(8,128)(2,1)S(1)}, u32[]{:S(2)}) copy-start(bf16[128,1792]{1,0:T(8,128)(2,1)S(1)} %get-tuple-element.74) | copy-start | bytes 1376260
  11.2 11.0 %copy-start.13 = (bf16[128,1792]{1,0:T(8,128)(2,1)}, bf16[128,1792]{1,0:T(8,128)(2,1)S(1)}, u32[]{:S(2)}) copy-start(bf16[128,1792]{1,0:T(8,128)(2,1)S(1)} %get-tuple-element.89.refs_2_) | copy-start | bytes 1376260
  11.2 11.0 %copy-start.17 = (bf16[128,1792]{1,0:T(8,128)(2,1)}, bf16[128,1792]{1,0:T(8,128)(2,1)S(1)}, u32[]{:S(2)}) copy-start(bf16[128,1792]{1,0:T(8,128)(2,1)S(1)} %get-tuple-element.82.refs_2_) | copy-start | bytes 1376260
  11.2 11.0 %copy-start.19 = (bf16[128,1792]{1,0:T(8,128)(2,1)}, bf16[128,1792]{1,0:T(8,128)(2,1)S(1)}, u32[]{:S(2)}) copy-start(bf16[128,1792]{1,0:T(8,128)(2,1)S(1)} %get-tuple-element.66) | copy-start | bytes 1376260
  11.2 11.0 %copy-start.21 = (bf16[128,1792]{1,0:T(8,128)(2,1)}, bf16[128,1792]{1,0:T(8,128)(2,1)S(1)}, u32[]{:S(2)}) copy-start(bf16[128,1792]{1,0:T(8,128)(2,1)S(1)} %get-tuple-element.62) | copy-start | bytes 1376260
  22.2 14.3 %copy-start.6 = (bf16[1,14,128,128]{3,2,1,0:T(8,128)(2,1)S(1)}, bf16[1,14,128,128]{3,2,1,0:T(8,128)(2,1)}, u32[]{:S(2)}) copy-start(bf16[1,14,128,128]{3,2,1,0:T(8,128)(2,1)} %param.10) | copy-start | bytes 1376260
  26.4 13.1 %collective-permute-start.3 = (bf16[128,4096]{1,0:T(8,128)(2,1)S(1)}, bf16[128,4096]{1,0:T(8,128)(2,1)}, u32[]{:S(2)}, u32[]{:S(2)}) collective-permute-start(bf16[128,4096]{1,0:T(8,128)(2,1)S(1)} %collective-permute-done.refs_0_), channel_id=1, source_target_pairs={{8,16},{12,20},{16,8},{20,12},{9,17},{13,21},{17,9},{21,13},{10,18... | collective-permute-start | bytes 3145736 | tf_op jit(solution)/shard_map/ppermute | solution.py:245
  28.0 27.6 %collective-permute-start.4 = (bf16[128,4096]{1,0:T(8,128)(2,1)}, bf16[128,4096]{1,0:T(8,128)(2,1)}, u32[]{:S(2)}, u32[]{:S(2)}) collective-permute-start(bf16[128,4096]{1,0:T(8,128)(2,1)} %collective-permute-done.2), channel_id=1, source_target_pairs={{0,8},{4,12},{8,0},{12,4},{16,24},{20,28},{24,16},{28,20},{1,9},{5... | collective-permute-start | bytes 3145736 | tf_op jit(solution)/shard_map/ppermute | solution.py:248
  31.7 2.7 %copy-start.22 = (bf16[128,1792]{1,0:T(8,128)(2,1)S(1)}, bf16[128,1792]{1,0:T(8,128)(2,1)}, u32[]{:S(2)}) copy-start(bf16[128,1792]{1,0:T(8,128)(2,1)} %copy-done.21) | copy-start | bytes 1376260
  32.8 50.4 %collective-permute-start.8 = (bf16[128,4992]{1,0:T(8,128)(2,1)S(1)}, bf16[128,4992]{1,0:T(8,128)(2,1)S(1)}, u32[]{:S(2)}, u32[]{:S(2)}) collective-permute-start(bf16[128,4992]{1,0:T(8,128)(2,1)S(1)} %pad_maximum_fusion), channel_id=1, source_target_pairs={{0,4},{4,0},{8,12},{12,8},{16,20},{20,16},{24,28},{28,24},{1,5},{5... | collective-permute-start | bytes 3833864 | tf_op jit(solution)/shard_map/ppermute | solution.py:248
  34.4 56.6 %collective-permute-start.7 = (bf16[128,1792]{1,0:T(8,128)(2,1)S(1)}, bf16[128,1792]{1,0:T(8,128)(2,1)S(1)}, u32[]{:S(2)}, u32[]{:S(2)}) collective-permute-start(bf16[128,1792]{1,0:T(8,128)(2,1)S(1)} %copy-done.22), channel_id=1, source_target_pairs={{0,28},{4,24},{8,20},{12,16},{16,12},{20,8},{24,4},{28,0},{1,29},{... | collective-permute-start | bytes 1376264 | tf_op jit(solution)/shard_map/ppermute | solution.py:248
  36.5 2.0 %copy-start.5 = (bf16[1,128,14336]{2,1,0:T(8,128)(2,1)S(1)}, bf16[1,128,14336]{2,1,0:T(8,128)(2,1)}, u32[]{:S(2)}) copy-start(bf16[1,128,14336]{2,1,0:T(8,128)(2,1)} %param.7) | copy-start | bytes 11010052
  38.6 24.1 %copy-start.20 = (bf16[128,1792]{1,0:T(8,128)(2,1)S(1)}, bf16[128,1792]{1,0:T(8,128)(2,1)}, u32[]{:S(2)}) copy-start(bf16[128,1792]{1,0:T(8,128)(2,1)} %copy-done.19) | copy-start | bytes 1376260
  39.5 28.5 %copy-start.10 = (bf16[128,1792]{1,0:T(8,128)(2,1)S(1)}, bf16[128,1792]{1,0:T(8,128)(2,1)}, u32[]{:S(2)}) copy-start(bf16[128,1792]{1,0:T(8,128)(2,1)} %copy-done.9) | copy-start | bytes 1376260
  55.6 42.3 %collective-permute-start.5 = (bf16[128,4096]{1,0:T(8,128)(2,1)}, bf16[128,4096]{1,0:T(8,128)(2,1)S(1)}, u32[]{:S(2)}, u32[]{:S(2)}) collective-permute-start(bf16[128,4096]{1,0:T(8,128)(2,1)} %collective-permute-done.3), channel_id=1, source_target_pairs={{0,8},{4,12},{8,0},{12,4},{16,24},{20,28},{24,16},{28,20},{1,9},{5... | collective-permute-start | bytes 3145736 | tf_op jit(solution)/shard_map/ppermute | solution.py:248
  62.7 35.2 %collective-permute-start.6 = (bf16[128,1792]{1,0:T(8,128)(2,1)S(1)}, bf16[128,1792]{1,0:T(8,128)(2,1)S(1)}, u32[]{:S(2)}, u32[]{:S(2)}) collective-permute-start(bf16[128,1792]{1,0:T(8,128)(2,1)S(1)} %copy-done.20), channel_id=1, source_target_pairs={{0,24},{4,28},{8,16},{12,20},{16,8},{20,12},{24,0},{28,4},{1,25},{... | collective-permute-start | bytes 1376264 | tf_op jit(solution)/shard_map/ppermute | solution.py:248
  68.2 33.9 %collective-permute-start.10 = (bf16[128,4992]{1,0:T(8,128)(2,1)S(1)}, bf16[128,4992]{1,0:T(8,128)(2,1)S(1)}, u32[]{:S(2)}, u32[]{:S(2)}) collective-permute-start(bf16[128,4992]{1,0:T(8,128)(2,1)S(1)} %pad_maximum_fusion.1), channel_id=1, source_target_pairs={{0,4},{4,0},{8,12},{12,8},{16,20},{20,16},{24,28},{28,24},{1,5},{5... | collective-permute-start | bytes 3833864 | tf_op jit(solution)/shard_map/ppermute | solution.py:248
  69.7 5.2 %copy-start.2 = (bf16[1,1792,4096]{2,1,0:T(8,128)(2,1)S(1)}, bf16[1,1792,4096]{2,1,0:T(8,128)(2,1)}, u32[]{:S(2)}) copy-start(bf16[1,1792,4096]{2,1,0:T(8,128)(2,1)} %param.8) | copy-start | bytes 44040196
  74.9 8.3 %copy-start.3 = (bf16[1,1792,4096]{2,1,0:T(8,128)(2,1)S(1)}, bf16[1,1792,4096]{2,1,0:T(8,128)(2,1)}, u32[]{:S(2)}) copy-start(bf16[1,1792,4096]{2,1,0:T(8,128)(2,1)} %param.8) | copy-start | bytes 44040196
  98.2 23.0 %collective-permute-start.9 = (bf16[128,4096]{1,0:T(8,128)(2,1)S(1)}, bf16[128,4096]{1,0:T(8,128)(2,1)S(1)}, u32[]{:S(2)}, u32[]{:S(2)}) collective-permute-start(bf16[128,4096]{1,0:T(8,128)(2,1)S(1)} %broadcast_select_fusion.refs_0_), channel_id=1, source_target_pairs={{0,4},{4,0},{8,12},{12,8},{16,20},{20,16},{24,28},{28,24},{1,5},{5... | collective-permute-start | bytes 3145736 | tf_op jit(solution)/shard_map/ppermute | solution.py:248
  99.7 21.4 %collective-permute-start.13 = (bf16[128,1792]{1,0:T(8,128)(2,1)S(1)}, bf16[128,1792]{1,0:T(8,128)(2,1)S(1)}, u32[]{:S(2)}, u32[]{:S(2)}) collective-permute-start(bf16[128,1792]{1,0:T(8,128)(2,1)S(1)} %shard_map.68), channel_id=1, source_target_pairs={{0,8},{4,12},{8,0},{12,4},{16,24},{20,28},{24,16},{28,20},{1,9},{5... | collective-permute-start | bytes 1376264 | tf_op jit(solution)/shard_map/ppermute | solution.py:248
  99.7 21.4 %collective-permute-start.14 = (bf16[128,1792]{1,0:T(8,128)(2,1)S(1)}, bf16[128,1792]{1,0:T(8,128)(2,1)S(1)}, u32[]{:S(2)}, u32[]{:S(2)}) collective-permute-start(bf16[128,1792]{1,0:T(8,128)(2,1)S(1)} %shard_map.71), channel_id=1, source_target_pairs={{0,16},{4,20},{8,24},{12,28},{16,0},{20,4},{24,8},{28,12},{1,17},{... | collective-permute-start | bytes 1376264 | tf_op jit(solution)/shard_map/ppermute | solution.py:248
  109.2 10.5 %collective-permute-start.11 = (f32[1,128]{1,0:T(1,128)S(1)}, f32[1,128]{1,0:T(1,128)S(1)}, u32[]{:S(2)}, u32[]{:S(2)}) collective-permute-start(f32[1,128]{1,0:T(1,128)S(1)} %shard_map.74), channel_id=1, source_target_pairs={{0,24},{4,28},{8,16},{12,20},{16,8},{20,12},{24,0},{28,4},{1,25},{... | collective-permute-start | bytes 1544 | tf_op jit(solution)/shard_map/ppermute | solution.py:248
  111.7 9.4 %collective-permute-start.12 = (f32[1,128]{1,0:T(1,128)S(1)}, f32[1,128]{1,0:T(1,128)S(1)}, u32[]{:S(2)}, u32[]{:S(2)}) collective-permute-start(f32[1,128]{1,0:T(1,128)S(1)} %shard_map.75), channel_id=1, source_target_pairs={{0,4},{4,0},{8,12},{12,8},{16,20},{20,16},{24,28},{28,24},{1,5},{5... | collective-permute-start | bytes 1544 | tf_op jit(solution)/shard_map/ppermute | solution.py:248
  121.1 13.2 %copy-start.16 = (bf16[128,1792]{1,0:T(8,128)(2,1)S(1)}, bf16[128,1792]{1,0:T(8,128)(2,1)}, u32[]{:S(2)}) copy-start(bf16[128,1792]{1,0:T(8,128)(2,1)} %copy-done.15) | copy-start | bytes 1376260
  121.1 13.2 %copy-start.18 = (bf16[128,1792]{1,0:T(8,128)(2,1)S(1)}, bf16[128,1792]{1,0:T(8,128)(2,1)}, u32[]{:S(2)}) copy-start(bf16[128,1792]{1,0:T(8,128)(2,1)} %copy-done.17) | copy-start | bytes 1376260
  121.2 20.7 %collective-permute-start.16 = (bf16[128,1792]{1,0:T(8,128)(2,1)S(1)}, bf16[128,1792]{1,0:T(8,128)(2,1)S(1)}, u32[]{:S(2)}, u32[]{:S(2)}) collective-permute-start(bf16[128,1792]{1,0:T(8,128)(2,1)S(1)} %shard_map.70), channel_id=1, source_target_pairs={{0,12},{4,8},{8,4},{12,0},{16,28},{20,24},{24,20},{28,16},{1,13},{... | collective-permute-start | bytes 1376264 | tf_op jit(solution)/shard_map/ppermute | solution.py:248
  122.5 21.4 %collective-permute-start.17 = (bf16[128,1792]{1,0:T(8,128)(2,1)S(1)}, bf16[128,1792]{1,0:T(8,128)(2,1)S(1)}, u32[]{:S(2)}, u32[]{:S(2)}) collective-permute-start(bf16[128,1792]{1,0:T(8,128)(2,1)S(1)} %shard_map.73), channel_id=1, source_target_pairs={{0,20},{4,16},{8,28},{12,24},{16,4},{20,0},{24,12},{28,8},{1,21},{... | collective-permute-start | bytes 1376264 | tf_op jit(solution)/shard_map/ppermute | solution.py:248
  131.6 12.4 %copy-start.12 = (bf16[128,1792]{1,0:T(8,128)(2,1)S(1)}, bf16[128,1792]{1,0:T(8,128)(2,1)}, u32[]{:S(2)}) copy-start(bf16[128,1792]{1,0:T(8,128)(2,1)} %copy-done.11) | copy-start | bytes 1376260
  131.6 12.4 %copy-start.14 = (bf16[128,1792]{1,0:T(8,128)(2,1)S(1)}, bf16[128,1792]{1,0:T(8,128)(2,1)}, u32[]{:S(2)}) copy-start(bf16[128,1792]{1,0:T(8,128)(2,1)} %copy-done.13) | copy-start | bytes 1376260
  131.6 10.3 %collective-permute-start.15 = (f32[1,128]{1,0:T(1,128)S(1)}, f32[1,128]{1,0:T(1,128)S(1)}, u32[]{:S(2)}, u32[]{:S(2)}) collective-permute-start(f32[1,128]{1,0:T(1,128)S(1)} %shard_map.76), channel_id=1, source_target_pairs={{0,28},{4,24},{8,20},{12,16},{16,12},{20,8},{24,4},{28,0},{1,29},{... | collective-permute-start | bytes 1544 | tf_op jit(solution)/shard_map/ppermute | solution.py:248
  144.3 1.9 %collective-permute-start.18 = (f32[128]{0:T(128)S(1)}, f32[128]{0:T(128)S(1)}, u32[]{:S(2)}, u32[]{:S(2)}) collective-permute-start(f32[128]{0:T(128)S(1)} %bitcast.54), channel_id=1, source_target_pairs={{0,1},{1,0},{2,3},{3,2},{4,5},{5,4},{6,7},{7,6},{8,9},{9,8},{10,11... | collective-permute-start | bytes 1544 | tf_op jit(solution)/shard_map/ppermute | solution.py:307
  144.4 3.6 %collective-permute-start.19 = (f32[128]{0:T(128)S(1)}, f32[128]{0:T(128)S(1)}, u32[]{:S(2)}, u32[]{:S(2)}) collective-permute-start(f32[128]{0:T(128)S(1)} %bitcast.55), channel_id=1, source_target_pairs={{0,2},{1,3},{2,0},{3,1},{4,6},{5,7},{6,4},{7,5},{8,10},{9,11},{10,... | collective-permute-start | bytes 1544 | tf_op jit(solution)/shard_map/ppermute | solution.py:307
  146.0 3.0 %collective-permute-start.20 = (f32[128]{0:T(128)S(1)}, f32[128]{0:T(128)S(1)}, u32[]{:S(2)}, u32[]{:S(2)}) collective-permute-start(f32[128]{0:T(128)S(1)} %bitcast.56), channel_id=1, source_target_pairs={{0,3},{1,2},{2,1},{3,0},{4,7},{5,6},{6,5},{7,4},{8,11},{9,10},{10,... | collective-permute-start | bytes 1544 | tf_op jit(solution)/shard_map/ppermute | solution.py:307

commit v7 on v6

--- a/solution.py
+++ b/solution.py
@@ -250,7 +250,7 @@
     def sideways(value):
         return [swap(value, j) for j in range(1, across)]
 
-    middle = lambda value: move(value, lambda z, x: (3 - z, x) if z in (1, 2) else None)
+    middle = lambda value: move(value, lambda z, x: (3 - z, x) if z in (1, 2) else (z, x))
     line = lambda value, d: swap(value, d * across)
     send = lambda values, js: {j: swap(values[j], j) for j in js}
     aside = lambda d: [d * across + j for j in range(1, across)]

time: 150 us -> 154 us (1.027)
  starting transfers between devices: 42.7 us -> 46 us
    ppermute x2, starting transfers between devices: 3.28 us -> 11.3 us  [move(): return lax.ppermute(value, 'seq', pairs)]
    ppermute x16, starting transfers between devices: 37.5 us -> 32.8 us  [swap(): return lax.ppermute(value, 'seq', [(s, s ^ j) for s in range(size)])]
where the time goes in v7:
time: 154 us; the launch traced here: 153 us
  waiting for transfers between devices  47.3 us (31%)
  starting transfers between devices  46 us (30%)
  Pallas kernels  39.9 us (26%)
  local copies, waits for them, and re-layouts  17 us (11%)
  other arithmetic  2.28 us (1%)
    ppermute x16, waiting for transfers between devices, swap(): return lax.ppermute(value, 'seq', [(s, s ^ j) for s in range(size)])  44.6 us
    ppermute x16, starting transfers between devices, swap(): return lax.ppermute(value, 'seq', [(s, s ^ j) for s in range(size)])  32.8 us
    pallas_call x4, Pallas kernels, project(): pl.pallas_call(functools.partial(project_kernel, count), grid=(units // s...  26.5 us
    unnamed x46, local copies, waits for them, and re-layouts  15.4 us
    ppermute x2, starting transfers between devices, move(): return lax.ppermute(value, 'seq', pairs)  11.3 us
    pallas_call x1, Pallas kernels, project_score(): pl.pallas_call(project_score_kernel, grid=(units // step,), in_specs=[who...  6.8 us
  transfers between devices with their start and end apart: 21, of which 9 were waited for; matrix products, arithmetic and copies ran while one was open for 2% of the time, Pallas kernels for 26%

profile of v7, /device:TPU:0, one launch (start us, length us, event | category | flops | bytes accessed | tf_op | source)
XLA Modules:
  0.0 152.9 jit_solution(510329307439218035)
XLA Ops:
  0.0 3.0 %collective-permute-start = (bf16[128,4096]{1,0:T(8,128)(2,1)}, bf16[128,4096]{1,0:T(8,128)(2,1)S(1)}, u32[]{:S(2)}, u32[]{:S(2)}) collective-permute-start(bf16[128,4096]{1,0:T(8,128)(2,1)} %bitcast.50), channel_id=1, source_target_pairs={{0,8},{4,12},{8,0},{12,4},{16,24},{20,28},{24,16},{28,20},{1,9},{5... | collective-permute-start | bytes 3145736 | tf_op jit(solution)/shard_map/ppermute | solution.py:248
  3.0 9.5 %collective-permute-start.2 = (bf16[128,4096]{1,0:T(8,128)(2,1)}, bf16[128,4096]{1,0:T(8,128)(2,1)}, u32[]{:S(2)}, u32[]{:S(2)}) collective-permute-start(bf16[128,4096]{1,0:T(8,128)(2,1)} %bitcast.51), channel_id=1, source_target_pairs={{0,0},{4,4},{8,16},{12,20},{16,8},{20,12},{24,24},{28,28},{1,1},{5... | collective-permute-start | bytes 3145736 | tf_op jit(solution)/shard_map/ppermute | solution.py:245
  12.5 1.5 collective-permute-start.1
  14.0 0.6 gather_fusion
  14.7 0.0 copy-start.4
  14.7 2.0 %copy-done.4 = bf16[1,128,14336]{2,1,0:T(8,128)(2,1)S(1)} copy-done((bf16[1,128,14336]{2,1,0:T(8,128)(2,1)S(1)}, bf16[1,128,14336]{2,1,0:T(8,128)(2,1)}, u32[]{:S(2)}) %copy-start.4) | copy-done | bytes 3670040
  16.7 0.8 shard_map.64
  17.5 0.8 copy-done.11
  18.3 0.8 copy-done.15
  19.1 4.0 %copy-done.1 = bf16[1,1792,4096]{2,1,0:T(8,128)(2,1)S(1)} copy-done((bf16[1,1792,4096]{2,1,0:T(8,128)(2,1)S(1)}, bf16[1,1792,4096]{2,1,0:T(8,128)(2,1)}, u32[]{:S(2)}) %copy-start.1) | copy-done | bytes 14680088
  23.1 0.2 copy-done.7
  23.3 0.3 copy-done.8
  23.6 6.5 %shard_map.65.found = f32[1,128,1792]{2,1,0:T(8,128)S(1)} custom-call(bf16[128,4096]{1,0:T(8,128)(2,1)S(1)} %bitcast.53, bf16[32,128,128]{2,1,0:T(8,128)(2,1)S(1)} %bitcast.45, bf16[1792,4096]{1,0:T(8,128)(2,1)S(1)} %bitcast.24), custom_call_target="tpu_custom_call" | custom-call | tf_op jit(solution)/shard_map/pallas_call | solution.py:43
  30.1 0.0 copy-start.6
  30.1 0.0 collective-permute-done.refs_0_
  30.1 1.8 %collective-permute-start.3 = (bf16[128,4096]{1,0:T(8,128)(2,1)S(1)}, bf16[128,4096]{1,0:T(8,128)(2,1)}, u32[]{:S(2)}, u32[]{:S(2)}) collective-permute-start(bf16[128,4096]{1,0:T(8,128)(2,1)S(1)} %collective-permute-done.refs_0_), channel_id=1, source_target_pairs={{0,0},{4,4},{8,16},{12,20},{16,8},{20,12},{24,24},{28,28},{1,1},{5... | collective-permute-start | bytes 3145736 | tf_op jit(solution)/shard_map/ppermute | solution.py:245
  31.9 0.0 collective-permute-done.2
  31.9 0.0 collective-permute-start.4
  31.9 1.0 slice.6
  32.9 0.1 pad_maximum_fusion
  33.0 1.3 collective-permute-start.8
  34.4 2.7 %collective-permute-start.7 = (bf16[128,1792]{1,0:T(8,128)(2,1)S(1)}, bf16[128,1792]{1,0:T(8,128)(2,1)S(1)}, u32[]{:S(2)}, u32[]{:S(2)}) collective-permute-start(bf16[128,1792]{1,0:T(8,128)(2,1)S(1)} %copy-done.22), channel_id=1, source_target_pairs={{0,28},{4,24},{8,20},{12,16},{16,12},{20,8},{24,4},{28,0},{1,29},{... | collective-permute-start | bytes 1376264 | tf_op jit(solution)/shard_map/ppermute | solution.py:248
  37.0 2.0 %copy-done.5 = bf16[1,128,14336]{2,1,0:T(8,128)(2,1)S(1)} copy-done((bf16[1,128,14336]{2,1,0:T(8,128)(2,1)S(1)}, bf16[1,128,14336]{2,1,0:T(8,128)(2,1)}, u32[]{:S(2)}) %copy-start.5) | copy-done | bytes 3670040
  39.1 0.9 shard_map.66
  40.0 0.0 collective-permute-done.1.refs_1_
  40.0 17.3 %collective-permute-done.4 = bf16[128,4096]{1,0:T(8,128)(2,1)} collective-permute-done((bf16[128,4096]{1,0:T(8,128)(2,1)}, bf16[128,4096]{1,0:T(8,128)(2,1)}, u32[]{:S(2)}, u32[]{:S(2)}) %collective-permute-start.4) | collective-permute-done | bytes 1048608 | tf_op jit(solution)/shard_map/ppermute | solution.py:248
  57.3 1.0 collective-permute-start.5
  58.3 9.8 %collective-permute-start.6 = (bf16[128,1792]{1,0:T(8,128)(2,1)S(1)}, bf16[128,1792]{1,0:T(8,128)(2,1)S(1)}, u32[]{:S(2)}, u32[]{:S(2)}) collective-permute-start(bf16[128,1792]{1,0:T(8,128)(2,1)S(1)} %copy-done.20), channel_id=1, source_target_pairs={{0,24},{4,28},{8,16},{12,20},{16,8},{20,12},{24,0},{28,4},{1,25},{... | collective-permute-start | bytes 1376264 | tf_op jit(solution)/shard_map/ppermute | solution.py:248
  68.1 1.3 broadcast_select_fusion.1.refs_0_
  69.5 0.1 pad_maximum_fusion.1
  69.6 0.2 collective-permute-start.10
  69.8 5.2 %copy-done.2 = bf16[1,1792,4096]{2,1,0:T(8,128)(2,1)S(1)} copy-done((bf16[1,1792,4096]{2,1,0:T(8,128)(2,1)S(1)}, bf16[1,1792,4096]{2,1,0:T(8,128)(2,1)}, u32[]{:S(2)}) %copy-start.2) | copy-done | bytes 14680088
  74.9 7.5 %shard_map.67.found = f32[2,128,1792]{2,1,0:T(8,128)S(1)} custom-call(bf16[128,4096]{1,0:T(8,128)(2,1)S(1)} %collective-permute-done.refs_0_, bf16[128,4096]{1,0:T(8,128)(2,1)} %collective-permute-done.1.refs_1_, bf16[32,128,128]{2,1,0:T(8,128)(2,1)S(1)} %bitcast.46, bf16[1792,4096]{1,0:T(8,128)(2,1)S(1)} %bitcast.25), custom_call_target="tpu_custom_call" | custom-call | tf_op jit(solution)/shard_map/pallas_call | solution.py:43
  82.5 0.7 shard_map.68
  83.2 6.3 %shard_map.69.found = f32[2,128,1792]{2,1,0:T(8,128)S(1)} custom-call(bf16[128,4096]{1,0:T(8,128)(2,1)S(1)} %broadcast_select_fusion.1.refs_0_, bf16[128,4992]{1,0:T(8,128)(2,1)S(1)} %collective-permute-done.8.refs_1_.first, bf16[32,128,128]{2,1,0:T(8,128)(2,1)S(1)} %bitcast.47, bf16[1792,4096]{1,0:T(8,128)(2,1)S(1)} %bitcast.26), custom_call_target="tpu_custom_call" | custom-call | tf_op jit(solution)/shard_map/pallas_call | solution.py:43
  89.5 0.7 shard_map.70
  90.3 0.7 shard_map.71
  91.0 8.3 %collective-permute-done.6.piece = bf16[128,1792]{1,0:T(8,128)(2,1)S(1)} collective-permute-done((bf16[128,1792]{1,0:T(8,128)(2,1)S(1)}, bf16[128,1792]{1,0:T(8,128)(2,1)S(1)}, u32[]{:S(2)}, u32[]{:S(2)}) %collective-permute-start.6) | collective-permute-done | bytes 458784 | tf_op jit(solution)/shard_map/ppermute | solution.py:248
  99.3 0.2 broadcast_select_fusion.refs_0_
  99.6 0.6 collective-permute-start.9
  100.2 2.3 %collective-permute-start.14 = (bf16[128,1792]{1,0:T(8,128)(2,1)S(1)}, bf16[128,1792]{1,0:T(8,128)(2,1)S(1)}, u32[]{:S(2)}, u32[]{:S(2)}) collective-permute-start(bf16[128,1792]{1,0:T(8,128)(2,1)S(1)} %shard_map.71), channel_id=1, source_target_pairs={{0,16},{4,20},{8,24},{12,28},{16,0},{20,4},{24,8},{28,12},{1,17},{... | collective-permute-start | bytes 1376264 | tf_op jit(solution)/shard_map/ppermute | solution.py:248
  102.4 1.0 collective-permute-done.10.refs_1_.second
  103.4 6.2 %shard_map.72.found = f32[2,128,1792]{2,1,0:T(8,128)S(1)} custom-call(bf16[128,4096]{1,0:T(8,128)(2,1)S(1)} %broadcast_select_fusion.refs_0_, bf16[128,4992]{1,0:T(8,128)(2,1)S(1)} %collective-permute-done.10.refs_1_.second, bf16[32,128,128]{2,1,0:T(8,128)(2,1)S(1)} %bitcast.48, bf16[1792,4096]{1,0:T(8,128)(2,1)S(1)} %bitcast.27), custom_call_target="tpu_custom_call" | custom-call | tf_op jit(solution)/shard_map/pallas_call | solution.py:43
  109.6 0.9 shard_map.74
  110.5 2.5 %collective-permute-start.11 = (f32[1,128]{1,0:T(1,128)S(1)}, f32[1,128]{1,0:T(1,128)S(1)}, u32[]{:S(2)}, u32[]{:S(2)}) collective-permute-start(f32[1,128]{1,0:T(1,128)S(1)} %shard_map.74), channel_id=1, source_target_pairs={{0,24},{4,28},{8,16},{12,20},{16,8},{20,12},{24,0},{28,4},{1,25},{... | collective-permute-start | bytes 1544 | tf_op jit(solution)/shard_map/ppermute | solution.py:248
  113.1 0.4 shard_map.75
  113.5 1.6 %collective-permute-start.12 = (f32[1,128]{1,0:T(1,128)S(1)}, f32[1,128]{1,0:T(1,128)S(1)}, u32[]{:S(2)}, u32[]{:S(2)}) collective-permute-start(f32[1,128]{1,0:T(1,128)S(1)} %shard_map.75), channel_id=1, source_target_pairs={{0,4},{4,0},{8,12},{12,8},{16,20},{20,16},{24,28},{28,24},{1,5},{5... | collective-permute-start | bytes 1544 | tf_op jit(solution)/shard_map/ppermute | solution.py:248
  115.0 0.7 shard_map.73
  115.8 4.5 %collective-permute-done.11 = f32[1,128]{1,0:T(1,128)S(1)} collective-permute-done((f32[1,128]{1,0:T(1,128)S(1)}, f32[1,128]{1,0:T(1,128)S(1)}, u32[]{:S(2)}, u32[]{:S(2)}) %collective-permute-start.11) | collective-permute-done | bytes 544 | tf_op jit(solution)/shard_map/ppermute | solution.py:248
  120.2 4.2 %collective-permute-done.12 = f32[1,128]{1,0:T(1,128)S(1)} collective-permute-done((f32[1,128]{1,0:T(1,128)S(1)}, f32[1,128]{1,0:T(1,128)S(1)}, u32[]{:S(2)}, u32[]{:S(2)}) %collective-permute-start.12) | collective-permute-done | bytes 544 | tf_op jit(solution)/shard_map/ppermute | solution.py:248
  124.5 0.1 collective-permute-start.16
  124.6 3.9 %collective-permute-start.17 = (bf16[128,1792]{1,0:T(8,128)(2,1)S(1)}, bf16[128,1792]{1,0:T(8,128)(2,1)S(1)}, u32[]{:S(2)}, u32[]{:S(2)}) collective-permute-start(bf16[128,1792]{1,0:T(8,128)(2,1)S(1)} %shard_map.73), channel_id=1, source_target_pairs={{0,20},{4,16},{8,28},{12,24},{16,4},{20,0},{24,12},{28,8},{1,21},{... | collective-permute-start | bytes 1376264 | tf_op jit(solution)/shard_map/ppermute | solution.py:248
  128.5 6.8 %shard_map.76 = f32[1,128]{1,0:T(1,128)S(1)} custom-call(bf16[128,4096]{1,0:T(8,128)(2,1)S(1)} %collective-permute-done.9.chunk, bf16[32,128,128]{2,1,0:T(8,128)(2,1)S(1)} %bitcast.49, bf16[1792,4096]{1,0:T(8,128)(2,1)S(1)} %bitcast.28, bf16[128,1792]{1,0:T(8,128)(2,1)S(1)} %collective-permute-done.7.piece, bf16[14,128,128]{2,1,0:T(8,128)(2,1)S(1)} %bitcast.44), custom_call_target="tpu_custom_call" | custom-call | tf_op jit(solution)/shard_map/pallas_call | solution.py:213
  135.4 2.3 %collective-permute-start.15 = (f32[1,128]{1,0:T(1,128)S(1)}, f32[1,128]{1,0:T(1,128)S(1)}, u32[]{:S(2)}, u32[]{:S(2)}) collective-permute-start(f32[1,128]{1,0:T(1,128)S(1)} %shard_map.76), channel_id=1, source_target_pairs={{0,28},{4,24},{8,20},{12,16},{16,12},{20,8},{24,4},{28,0},{1,29},{... | collective-permute-start | bytes 1544 | tf_op jit(solution)/shard_map/ppermute | solution.py:248
  137.7 0.3 shard_map.77
  138.1 9.1 %collective-permute-done.15 = f32[1,128]{1,0:T(1,128)S(1)} collective-permute-done((f32[1,128]{1,0:T(1,128)S(1)}, f32[1,128]{1,0:T(1,128)S(1)}, u32[]{:S(2)}, u32[]{:S(2)}) %collective-permute-start.15) | collective-permute-done | bytes 544 | tf_op jit(solution)/shard_map/ppermute | solution.py:248
  147.2 0.2 collective-permute-done.17.refs_0_
  147.4 0.3 shard_map.78
  147.8 0.1 collective-permute-start.18
  147.8 1.6 %collective-permute-start.19 = (f32[128]{0:T(128)S(1)}, f32[128]{0:T(128)S(1)}, u32[]{:S(2)}, u32[]{:S(2)}) collective-permute-start(f32[128]{0:T(128)S(1)} %bitcast.55), channel_id=1, source_target_pairs={{0,2},{1,3},{2,0},{3,1},{4,6},{5,7},{6,4},{7,5},{8,10},{9,11},{10,... | collective-permute-start | bytes 1544 | tf_op jit(solution)/shard_map/ppermute | solution.py:307
  149.4 0.3 collective-permute-start.20
  149.7 1.7 %collective-permute-done.19 = f32[128]{0:T(128)S(1)} collective-permute-done((f32[128]{0:T(128)S(1)}, f32[128]{0:T(128)S(1)}, u32[]{:S(2)}, u32[]{:S(2)}) %collective-permute-start.19) | collective-permute-done | bytes 544 | tf_op jit(solution)/shard_map/ppermute | solution.py:307
  151.5 0.9 collective-permute-done.20
  152.4 0.5 fusion.1
  (53 shorter events, 0.2 us)
Async XLA Ops:
  0.0 14.0 %copy-start = (s32[1,8]{1,0:T(1,128)S(1)}, s32[1,8]{1,0:T(1,128)}, u32[]{:S(2)}) copy-start(s32[1,8]{1,0:T(1,128)} %param.11) | copy-start | bytes 100
  0.0 30.1 %collective-permute-start = (bf16[128,4096]{1,0:T(8,128)(2,1)}, bf16[128,4096]{1,0:T(8,128)(2,1)S(1)}, u32[]{:S(2)}, u32[]{:S(2)}) collective-permute-start(bf16[128,4096]{1,0:T(8,128)(2,1)} %bitcast.50), channel_id=1, source_target_pairs={{0,8},{4,12},{8,0},{12,4},{16,24},{20,28},{24,16},{28,20},{1,9},{5... | collective-permute-start | bytes 3145736 | tf_op jit(solution)/shard_map/ppermute | solution.py:248
  3.0 28.9 %collective-permute-start.2 = (bf16[128,4096]{1,0:T(8,128)(2,1)}, bf16[128,4096]{1,0:T(8,128)(2,1)}, u32[]{:S(2)}, u32[]{:S(2)}) collective-permute-start(bf16[128,4096]{1,0:T(8,128)(2,1)} %bitcast.51), channel_id=1, source_target_pairs={{0,0},{4,4},{8,16},{12,20},{16,8},{20,12},{24,24},{28,28},{1,1},{5... | collective-permute-start | bytes 3145736 | tf_op jit(solution)/shard_map/ppermute | solution.py:245
  12.5 27.5 %collective-permute-start.1 = (bf16[128,4096]{1,0:T(8,128)(2,1)}, bf16[128,4096]{1,0:T(8,128)(2,1)}, u32[]{:S(2)}, u32[]{:S(2)}) collective-permute-start(bf16[128,4096]{1,0:T(8,128)(2,1)} %bitcast.52), channel_id=1, source_target_pairs={{0,4},{4,0},{8,12},{12,8},{16,20},{20,16},{24,28},{28,24},{1,5},{5... | collective-permute-start | bytes 3145736 | tf_op jit(solution)/shard_map/ppermute | solution.py:248
  14.7 2.0 %copy-start.4 = (bf16[1,128,14336]{2,1,0:T(8,128)(2,1)S(1)}, bf16[1,128,14336]{2,1,0:T(8,128)(2,1)}, u32[]{:S(2)}) copy-start(bf16[1,128,14336]{2,1,0:T(8,128)(2,1)} %param.7) | copy-start | bytes 11010052
  16.7 6.3 %copy-start.1 = (bf16[1,1792,4096]{2,1,0:T(8,128)(2,1)S(1)}, bf16[1,1792,4096]{2,1,0:T(8,128)(2,1)}, u32[]{:S(2)}) copy-start(bf16[1,1792,4096]{2,1,0:T(8,128)(2,1)} %param.8) | copy-start | bytes 44040196
  16.7 6.6 %copy-start.7 = (bf16[1,32,128,128]{3,2,1,0:T(8,128)(2,1)S(1)}, bf16[1,32,128,128]{3,2,1,0:T(8,128)(2,1)}, u32[]{:S(2)}) copy-start(bf16[1,32,128,128]{3,2,1,0:T(8,128)(2,1)} %param.9) | copy-start | bytes 3145732
  16.7 6.9 %copy-start.8 = (bf16[1,128,4096]{2,1,0:T(8,128)(2,1)S(1)}, bf16[1,128,4096]{2,1,0:T(8,128)(2,1)}, u32[]{:S(2)}) copy-start(bf16[1,128,4096]{2,1,0:T(8,128)(2,1)} %param.6) | copy-start | bytes 3145732
  17.5 0.8 copy-start.11
  18.3 0.8 copy-start.15
  19.0 11.0 %copy-start.9 = (bf16[128,1792]{1,0:T(8,128)(2,1)}, bf16[128,1792]{1,0:T(8,128)(2,1)S(1)}, u32[]{:S(2)}) copy-start(bf16[128,1792]{1,0:T(8,128)(2,1)S(1)} %get-tuple-element.74) | copy-start | bytes 1376260
  19.0 11.0 %copy-start.13 = (bf16[128,1792]{1,0:T(8,128)(2,1)}, bf16[128,1792]{1,0:T(8,128)(2,1)S(1)}, u32[]{:S(2)}) copy-start(bf16[128,1792]{1,0:T(8,128)(2,1)S(1)} %get-tuple-element.89.refs_2_) | copy-start | bytes 1376260
  19.0 11.1 %copy-start.17 = (bf16[128,1792]{1,0:T(8,128)(2,1)}, bf16[128,1792]{1,0:T(8,128)(2,1)S(1)}, u32[]{:S(2)}) copy-start(bf16[128,1792]{1,0:T(8,128)(2,1)S(1)} %get-tuple-element.82.refs_2_) | copy-start | bytes 1376260
  19.0 11.1 %copy-start.19 = (bf16[128,1792]{1,0:T(8,128)(2,1)}, bf16[128,1792]{1,0:T(8,128)(2,1)S(1)}, u32[]{:S(2)}) copy-start(bf16[128,1792]{1,0:T(8,128)(2,1)S(1)} %get-tuple-element.66) | copy-start | bytes 1376260
  19.0 11.1 %copy-start.21 = (bf16[128,1792]{1,0:T(8,128)(2,1)}, bf16[128,1792]{1,0:T(8,128)(2,1)S(1)}, u32[]{:S(2)}) copy-start(bf16[128,1792]{1,0:T(8,128)(2,1)S(1)} %get-tuple-element.62) | copy-start | bytes 1376260
  30.1 6.9 %copy-start.6 = (bf16[1,14,128,128]{3,2,1,0:T(8,128)(2,1)S(1)}, bf16[1,14,128,128]{3,2,1,0:T(8,128)(2,1)}, u32[]{:S(2)}) copy-start(bf16[1,14,128,128]{3,2,1,0:T(8,128)(2,1)} %param.10) | copy-start | bytes 1376260
  30.1 9.9 %collective-permute-start.3 = (bf16[128,4096]{1,0:T(8,128)(2,1)S(1)}, bf16[128,4096]{1,0:T(8,128)(2,1)}, u32[]{:S(2)}, u32[]{:S(2)}) collective-permute-start(bf16[128,4096]{1,0:T(8,128)(2,1)S(1)} %collective-permute-done.refs_0_), channel_id=1, source_target_pairs={{0,0},{4,4},{8,16},{12,20},{16,8},{20,12},{24,24},{28,28},{1,1},{5... | collective-permute-start | bytes 3145736 | tf_op jit(solution)/shard_map/ppermute | solution.py:245
  31.9 25.4 %collective-permute-start.4 = (bf16[128,4096]{1,0:T(8,128)(2,1)}, bf16[128,4096]{1,0:T(8,128)(2,1)}, u32[]{:S(2)}, u32[]{:S(2)}) collective-permute-start(bf16[128,4096]{1,0:T(8,128)(2,1)} %collective-permute-done.2), channel_id=1, source_target_pairs={{0,8},{4,12},{8,0},{12,4},{16,24},{20,28},{24,16},{28,20},{1,9},{5... | collective-permute-start | bytes 3145736 | tf_op jit(solution)/shard_map/ppermute | solution.py:248
  31.9 2.4 %copy-start.22 = (bf16[128,1792]{1,0:T(8,128)(2,1)S(1)}, bf16[128,1792]{1,0:T(8,128)(2,1)}, u32[]{:S(2)}) copy-start(bf16[128,1792]{1,0:T(8,128)(2,1)} %copy-done.21) | copy-start | bytes 1376260
  33.0 50.2 %collective-permute-start.8 = (bf16[128,4992]{1,0:T(8,128)(2,1)S(1)}, bf16[128,4992]{1,0:T(8,128)(2,1)S(1)}, u32[]{:S(2)}, u32[]{:S(2)}) collective-permute-start(bf16[128,4992]{1,0:T(8,128)(2,1)S(1)} %pad_maximum_fusion), channel_id=1, source_target_pairs={{0,4},{4,0},{8,12},{12,8},{16,20},{20,16},{24,28},{28,24},{1,5},{5... | collective-permute-start | bytes 3833864 | tf_op jit(solution)/shard_map/ppermute | solution.py:248
  34.4 56.6 %collective-permute-start.7 = (bf16[128,1792]{1,0:T(8,128)(2,1)S(1)}, bf16[128,1792]{1,0:T(8,128)(2,1)S(1)}, u32[]{:S(2)}, u32[]{:S(2)}) collective-permute-start(bf16[128,1792]{1,0:T(8,128)(2,1)S(1)} %copy-done.22), channel_id=1, source_target_pairs={{0,28},{4,24},{8,20},{12,16},{16,12},{20,8},{24,4},{28,0},{1,29},{... | collective-permute-start | bytes 1376264 | tf_op jit(solution)/shard_map/ppermute | solution.py:248
  37.0 2.0 %copy-start.5 = (bf16[1,128,14336]{2,1,0:T(8,128)(2,1)S(1)}, bf16[1,128,14336]{2,1,0:T(8,128)(2,1)}, u32[]{:S(2)}) copy-start(bf16[1,128,14336]{2,1,0:T(8,128)(2,1)} %param.7) | copy-start | bytes 11010052
  39.1 19.2 %copy-start.20 = (bf16[128,1792]{1,0:T(8,128)(2,1)S(1)}, bf16[128,1792]{1,0:T(8,128)(2,1)}, u32[]{:S(2)}) copy-start(bf16[128,1792]{1,0:T(8,128)(2,1)} %copy-done.19) | copy-start | bytes 1376260
  40.0 29.4 %copy-start.10 = (bf16[128,1792]{1,0:T(8,128)(2,1)S(1)}, bf16[128,1792]{1,0:T(8,128)(2,1)}, u32[]{:S(2)}) copy-start(bf16[128,1792]{1,0:T(8,128)(2,1)} %copy-done.9) | copy-start | bytes 1376260
  57.3 42.0 %collective-permute-start.5 = (bf16[128,4096]{1,0:T(8,128)(2,1)}, bf16[128,4096]{1,0:T(8,128)(2,1)S(1)}, u32[]{:S(2)}, u32[]{:S(2)}) collective-permute-start(bf16[128,4096]{1,0:T(8,128)(2,1)} %collective-permute-done.3), channel_id=1, source_target_pairs={{0,8},{4,12},{8,0},{12,4},{16,24},{20,28},{24,16},{28,20},{1,9},{5... | collective-permute-start | bytes 3145736 | tf_op jit(solution)/shard_map/ppermute | solution.py:248
  58.3 41.0 %collective-permute-start.6 = (bf16[128,1792]{1,0:T(8,128)(2,1)S(1)}, bf16[128,1792]{1,0:T(8,128)(2,1)S(1)}, u32[]{:S(2)}, u32[]{:S(2)}) collective-permute-start(bf16[128,1792]{1,0:T(8,128)(2,1)S(1)} %copy-done.20), channel_id=1, source_target_pairs={{0,24},{4,28},{8,16},{12,20},{16,8},{20,12},{24,0},{28,4},{1,25},{... | collective-permute-start | bytes 1376264 | tf_op jit(solution)/shard_map/ppermute | solution.py:248
  69.6 33.8 %collective-permute-start.10 = (bf16[128,4992]{1,0:T(8,128)(2,1)S(1)}, bf16[128,4992]{1,0:T(8,128)(2,1)S(1)}, u32[]{:S(2)}, u32[]{:S(2)}) collective-permute-start(bf16[128,4992]{1,0:T(8,128)(2,1)S(1)} %pad_maximum_fusion.1), channel_id=1, source_target_pairs={{0,4},{4,0},{8,12},{12,8},{16,20},{20,16},{24,28},{28,24},{1,5},{5... | collective-permute-start | bytes 3833864 | tf_op jit(solution)/shard_map/ppermute | solution.py:248
  69.7 5.2 %copy-start.2 = (bf16[1,1792,4096]{2,1,0:T(8,128)(2,1)S(1)}, bf16[1,1792,4096]{2,1,0:T(8,128)(2,1)}, u32[]{:S(2)}) copy-start(bf16[1,1792,4096]{2,1,0:T(8,128)(2,1)} %param.8) | copy-start | bytes 44040196
  74.9 8.3 %copy-start.3 = (bf16[1,1792,4096]{2,1,0:T(8,128)(2,1)S(1)}, bf16[1,1792,4096]{2,1,0:T(8,128)(2,1)}, u32[]{:S(2)}) copy-start(bf16[1,1792,4096]{2,1,0:T(8,128)(2,1)} %param.8) | copy-start | bytes 44040196
  99.6 25.0 %collective-permute-start.9 = (bf16[128,4096]{1,0:T(8,128)(2,1)S(1)}, bf16[128,4096]{1,0:T(8,128)(2,1)S(1)}, u32[]{:S(2)}, u32[]{:S(2)}) collective-permute-start(bf16[128,4096]{1,0:T(8,128)(2,1)S(1)} %broadcast_select_fusion.refs_0_), channel_id=1, source_target_pairs={{0,4},{4,0},{8,12},{12,8},{16,20},{20,16},{24,28},{28,24},{1,5},{5... | collective-permute-start | bytes 3145736 | tf_op jit(solution)/shard_map/ppermute | solution.py:248
  100.2 24.3 %collective-permute-start.13 = (bf16[128,1792]{1,0:T(8,128)(2,1)S(1)}, bf16[128,1792]{1,0:T(8,128)(2,1)S(1)}, u32[]{:S(2)}, u32[]{:S(2)}) collective-permute-start(bf16[128,1792]{1,0:T(8,128)(2,1)S(1)} %shard_map.68), channel_id=1, source_target_pairs={{0,8},{4,12},{8,0},{12,4},{16,24},{20,28},{24,16},{28,20},{1,9},{5... | collective-permute-start | bytes 1376264 | tf_op jit(solution)/shard_map/ppermute | solution.py:248
  100.2 24.3 %collective-permute-start.14 = (bf16[128,1792]{1,0:T(8,128)(2,1)S(1)}, bf16[128,1792]{1,0:T(8,128)(2,1)S(1)}, u32[]{:S(2)}, u32[]{:S(2)}) collective-permute-start(bf16[128,1792]{1,0:T(8,128)(2,1)S(1)} %shard_map.71), channel_id=1, source_target_pairs={{0,16},{4,20},{8,24},{12,28},{16,0},{20,4},{24,8},{28,12},{1,17},{... | collective-permute-start | bytes 1376264 | tf_op jit(solution)/shard_map/ppermute | solution.py:248
  110.5 9.7 %collective-permute-start.11 = (f32[1,128]{1,0:T(1,128)S(1)}, f32[1,128]{1,0:T(1,128)S(1)}, u32[]{:S(2)}, u32[]{:S(2)}) collective-permute-start(f32[1,128]{1,0:T(1,128)S(1)} %shard_map.74), channel_id=1, source_target_pairs={{0,24},{4,28},{8,16},{12,20},{16,8},{20,12},{24,0},{28,4},{1,25},{... | collective-permute-start | bytes 1544 | tf_op jit(solution)/shard_map/ppermute | solution.py:248
  113.5 11.0 %collective-permute-start.12 = (f32[1,128]{1,0:T(1,128)S(1)}, f32[1,128]{1,0:T(1,128)S(1)}, u32[]{:S(2)}, u32[]{:S(2)}) collective-permute-start(f32[1,128]{1,0:T(1,128)S(1)} %shard_map.75), channel_id=1, source_target_pairs={{0,4},{4,0},{8,12},{12,8},{16,20},{20,16},{24,28},{28,24},{1,5},{5... | collective-permute-start | bytes 1544 | tf_op jit(solution)/shard_map/ppermute | solution.py:248
  124.5 13.2 %copy-start.16 = (bf16[128,1792]{1,0:T(8,128)(2,1)S(1)}, bf16[128,1792]{1,0:T(8,128)(2,1)}, u32[]{:S(2)}) copy-start(bf16[128,1792]{1,0:T(8,128)(2,1)} %copy-done.15) | copy-start | bytes 1376260
  124.5 13.2 %copy-start.18 = (bf16[128,1792]{1,0:T(8,128)(2,1)S(1)}, bf16[128,1792]{1,0:T(8,128)(2,1)}, u32[]{:S(2)}) copy-start(bf16[128,1792]{1,0:T(8,128)(2,1)} %copy-done.17) | copy-start | bytes 1376260
  124.5 22.7 %collective-permute-start.16 = (bf16[128,1792]{1,0:T(8,128)(2,1)S(1)}, bf16[128,1792]{1,0:T(8,128)(2,1)S(1)}, u32[]{:S(2)}, u32[]{:S(2)}) collective-permute-start(bf16[128,1792]{1,0:T(8,128)(2,1)S(1)} %shard_map.70), channel_id=1, source_target_pairs={{0,12},{4,8},{8,4},{12,0},{16,28},{20,24},{24,20},{28,16},{1,13},{... | collective-permute-start | bytes 1376264 | tf_op jit(solution)/shard_map/ppermute | solution.py:248
  124.6 22.8 %collective-permute-start.17 = (bf16[128,1792]{1,0:T(8,128)(2,1)S(1)}, bf16[128,1792]{1,0:T(8,128)(2,1)S(1)}, u32[]{:S(2)}, u32[]{:S(2)}) collective-permute-start(bf16[128,1792]{1,0:T(8,128)(2,1)S(1)} %shard_map.73), channel_id=1, source_target_pairs={{0,20},{4,16},{8,28},{12,24},{16,4},{20,0},{24,12},{28,8},{1,21},{... | collective-permute-start | bytes 1376264 | tf_op jit(solution)/shard_map/ppermute | solution.py:248
  135.3 12.1 %copy-start.12 = (bf16[128,1792]{1,0:T(8,128)(2,1)S(1)}, bf16[128,1792]{1,0:T(8,128)(2,1)}, u32[]{:S(2)}) copy-start(bf16[128,1792]{1,0:T(8,128)(2,1)} %copy-done.11) | copy-start | bytes 1376260
  135.3 12.1 %copy-start.14 = (bf16[128,1792]{1,0:T(8,128)(2,1)S(1)}, bf16[128,1792]{1,0:T(8,128)(2,1)}, u32[]{:S(2)}) copy-start(bf16[128,1792]{1,0:T(8,128)(2,1)} %copy-done.13) | copy-start | bytes 1376260
  135.4 11.8 %collective-permute-start.15 = (f32[1,128]{1,0:T(1,128)S(1)}, f32[1,128]{1,0:T(1,128)S(1)}, u32[]{:S(2)}, u32[]{:S(2)}) collective-permute-start(f32[1,128]{1,0:T(1,128)S(1)} %shard_map.76), channel_id=1, source_target_pairs={{0,28},{4,24},{8,20},{12,16},{16,12},{20,8},{24,4},{28,0},{1,29},{... | collective-permute-start | bytes 1544 | tf_op jit(solution)/shard_map/ppermute | solution.py:248
  147.8 1.9 %collective-permute-start.18 = (f32[128]{0:T(128)S(1)}, f32[128]{0:T(128)S(1)}, u32[]{:S(2)}, u32[]{:S(2)}) collective-permute-start(f32[128]{0:T(128)S(1)} %bitcast.54), channel_id=1, source_target_pairs={{0,1},{1,0},{2,3},{3,2},{4,5},{5,4},{6,7},{7,6},{8,9},{9,8},{10,11... | collective-permute-start | bytes 1544 | tf_op jit(solution)/shard_map/ppermute | solution.py:307
  147.8 3.6 %collective-permute-start.19 = (f32[128]{0:T(128)S(1)}, f32[128]{0:T(128)S(1)}, u32[]{:S(2)}, u32[]{:S(2)}) collective-permute-start(f32[128]{0:T(128)S(1)} %bitcast.55), channel_id=1, source_target_pairs={{0,2},{1,3},{2,0},{3,1},{4,6},{5,7},{6,4},{7,5},{8,10},{9,11},{10,... | collective-permute-start | bytes 1544 | tf_op jit(solution)/shard_map/ppermute | solution.py:307
  149.4 3.0 %collective-permute-start.20 = (f32[128]{0:T(128)S(1)}, f32[128]{0:T(128)S(1)}, u32[]{:S(2)}, u32[]{:S(2)}) collective-permute-start(f32[128]{0:T(128)S(1)} %bitcast.56), channel_id=1, source_target_pairs={{0,3},{1,2},{2,1},{3,0},{4,7},{5,6},{6,5},{7,4},{8,11},{9,10},{10,... | collective-permute-start | bytes 1544 | tf_op jit(solution)/shard_map/ppermute | solution.py:307
